TPU v7x, 32 devices: a whole 2x2x4 slice. The times are simulated.
32 devices in a mesh: genome: 8 (over z, y), tower: 4 (over x, core).
Axes of the slice: x: 2, y: 2, z: 4, core: 2. Of those that a mesh axis runs over, the one named last changes fastest.
Arguments:
- genome_bases: int32 [1048576], P('genome'), may hold values from 0 to 3
- stitch_weight: int32 [256], replicated, may hold values from 1 to 8
- stem_weight: bfloat16 [96, 8192], replicated, may hold values from -0.125 to 0.125
- trunk_in: bfloat16 [6, 48, 288], replicated, may hold values from -0.375 to 0.375
- trunk_out: bfloat16 [6, 96, 48], replicated, may hold values from -0.875 to 0.875
- pair_weight: bfloat16 [96, 96], replicated, may hold values from -0.625 to 0.625
- distance_rate: float32 [48], replicated, may hold values from 0.05 to 0.3
- tower_conv: bfloat16 [2, 3, 48, 144], replicated, may hold values from -0.3125 to 0.3125
- tower_mix: bfloat16 [2, 48, 48], replicated, may hold values from -0.875 to 0.875
- head_weight: bfloat16 [5, 48], replicated, may hold values from -0.875 to 0.875
Outputs:
- stitched: float32 [5, 512, 256], P(None, ('genome', 'tower'))
- scores: float32 [2, 5, 512], P(None, None, ('genome', 'tower'))
All inputs are finite; a program needn't handle non-finite values.
Results may differ from a plain program's by a relative error of at most 0.019.
Values may be sent and summed in bfloat16 or wider, within the bound.
No kernel may reach another device: no remote copies, remote signals or barrier semaphores. Data moves between devices by JAX's collectives and lax.ppermute only.
A program may use at most 64 MiB of HBM per device.

v0:
```python
import jax
import jax.numpy as jnp
from jax import lax
from jax.sharding import PartitionSpec as P

BP = 2048
STRIDE = 64
BINS = 256


def from_behind(block, axis, distance):
    devices = range(lax.axis_size(axis))
    route = [(i - distance, i) for i in devices if i - distance in devices]
    return lax.ppermute(block, axis, route)


def as_sent(value):
    return jax.tree.map(lambda a: a.astype(jnp.bfloat16) if a.dtype == jnp.float32 else a, value)


def shift_cols(values, offset):
    extent = values.shape[-1]
    margins = [(0, 0)] * (values.ndim - 1)
    if offset >= 0:
        padded = jnp.pad(values, margins + [(0, offset)])
        return padded[..., offset : offset + extent]
    padded = jnp.pad(values, margins + [(-offset, 0)])
    return padded[..., :extent]


def stem_features(genome_bases, stem_weight):
    letters = genome_bases.reshape(-1, BP)
    onehot = (letters[:, :, None] == jnp.arange(4, dtype=jnp.int32)[None, None, :]).astype(
        jnp.bfloat16
    )
    onehot = onehot.reshape(letters.shape[0], 4 * BP)
    summed = lax.dot_general(
        stem_weight, onehot, (((1,), (1,)), ((), ())), preferred_element_type=jnp.float32
    )
    return summed.astype(jnp.bfloat16)


def trunk_stream(window, trunk_in, trunk_out):
    stream = window.astype(jnp.float32)
    layers = trunk_in.shape[0]
    extent = window.shape[-1]
    for layer_index in range(layers):
        dilation = max(1, extent // 2 ** (layers - layer_index))
        active = jax.nn.relu(stream).astype(jnp.bfloat16)
        stacked = jnp.concatenate(
            [shift_cols(active, -dilation), active, shift_cols(active, dilation)], axis=0
        )
        inner = jnp.dot(trunk_in[layer_index], stacked, preferred_element_type=jnp.float32)
        squeezed = jax.nn.relu(inner).astype(jnp.bfloat16)
        stream = stream + jnp.dot(
            trunk_out[layer_index], squeezed, preferred_element_type=jnp.float32
        )
    return stream


def conv_rows(active, kernel):
    height = active.shape[2] - 2
    extent = active.shape[3]
    padded = jnp.pad(active, ((0, 0), (0, 0), (0, 0), (1, 1)))
    summed = None
    for row_tap in range(3):
        stacked = jnp.concatenate(
            [
                padded[:, :, row_tap : row_tap + height, col_tap : col_tap + extent]
                for col_tap in range(3)
            ],
            axis=0,
        )
        partial_value = jnp.einsum(
            "oc,ckrj->okrj", kernel[row_tap], stacked, preferred_element_type=jnp.float32
        )
        summed = partial_value if summed is None else summed + partial_value
    return summed


def block_rows(tower_index, height, margin):
    starts = []
    for block_index in range(BINS // STRIDE):
        starts.append(
            STRIDE * block_index + height * tower_index - margin + jnp.arange(height + 2 * margin)
        )
    return jnp.stack(starts, axis=0)


def build_pair(projected, distance_rate, tower_index, height, margin):
    channels = distance_rate.shape[0]
    left_padded = jnp.pad(projected[:channels], ((0, 0), (margin, margin)))
    right_cols = projected[channels:]
    col_pos = jnp.arange(BINS)
    pair_blocks = []
    for block_index in range(BINS // STRIDE):
        start_row = STRIDE * block_index + height * tower_index - margin
        left_rows = lax.dynamic_slice_in_dim(
            left_padded, start_row + margin, height + 2 * margin, axis=1
        )
        row_pos = start_row + jnp.arange(height + 2 * margin)
        separation = jnp.abs(row_pos[:, None] - col_pos[None, :]).astype(jnp.float32)
        inside = ((row_pos >= 0) & (row_pos < BINS)).astype(jnp.float32)
        mixed = (
            left_rows[:, :, None]
            + right_cols[:, None, :]
            - distance_rate[:, None, None] * jnp.log1p(separation)[None]
        )
        pair_blocks.append((jax.nn.relu(mixed) * inside[None, :, None]).astype(jnp.bfloat16))
    return jnp.stack(pair_blocks, axis=1)


def skew_rows(rows_map, first_row):
    targets = rows_map.shape[0]
    height = rows_map.shape[1]
    extent = rows_map.shape[2]
    padded = jnp.pad(rows_map, ((0, 0), (0, 0), (0, extent)))
    flattened = padded.reshape(targets, height * 2 * extent)
    flattened = jnp.pad(flattened, ((0, 0), (0, extent + height)))
    sliced = lax.dynamic_slice_in_dim(flattened, first_row, height * (2 * extent + 1), axis=1)
    return sliced.reshape(targets, height, 2 * extent + 1)[:, :, :extent]


def per_device(
    genome_bases,
    stitch_weight,
    stem_weight,
    trunk_in,
    trunk_out,
    pair_weight,
    distance_rate,
    tower_conv,
    tower_mix,
    head_weight,
):
    blocks = BINS // STRIDE
    towers = lax.axis_size("tower")
    height = STRIDE // towers
    tower_index = lax.axis_index("tower")
    genome_index = lax.axis_index("genome")
    own_features = stem_features(genome_bases, stem_weight)
    gathered = [own_features]
    for distance in range(1, blocks):
        gathered.append(from_behind(own_features, "genome", -distance))
    window = jnp.concatenate(gathered, axis=1)
    stream = trunk_stream(window, trunk_in, trunk_out)
    projected = jnp.dot(
        pair_weight, jax.nn.relu(stream).astype(jnp.bfloat16), preferred_element_type=jnp.float32
    )
    layers = tower_conv.shape[0]
    pair_map = build_pair(projected, distance_rate, tower_index, height, layers)
    tower_stream = pair_map.astype(jnp.float32)
    for layer_index in range(layers):
        margin = layers - layer_index
        row_pos = block_rows(tower_index, height, margin)
        inside = (row_pos >= 0) & (row_pos < BINS)
        active = jnp.where(inside[None, :, :, None], jax.nn.relu(tower_stream), 0.0).astype(
            jnp.bfloat16
        )
        convolved = conv_rows(active, tower_conv[layer_index])
        squeezed = jax.nn.relu(convolved).astype(jnp.bfloat16)
        tower_stream = tower_stream[:, :, 1:-1] + jnp.einsum(
            "oc,ckrj->okrj", tower_mix[layer_index], squeezed, preferred_element_type=jnp.float32
        )
    final_act = jax.nn.relu(tower_stream).astype(jnp.bfloat16)
    contact_maps = jnp.einsum(
        "tc,ckrj->tkrj", head_weight, final_act, preferred_element_type=jnp.float32
    )
    weights_float = stitch_weight.astype(jnp.float32)
    offsets = jnp.arange(BINS)
    local_rows = jnp.arange(height)
    pieces = []
    weight_sum = jnp.zeros((height, BINS), jnp.float32)
    for block_index in range(blocks):
        first_row = STRIDE * block_index + height * tower_index
        skewed = skew_rows(contact_maps[:, block_index], first_row)
        row_weight = lax.dynamic_slice_in_dim(weights_float, first_row, height)
        pieces.append(skewed * row_weight[None, :, None])
        covered = (genome_index >= block_index) & (
            first_row + local_rows[:, None] + offsets[None, :] < BINS
        )
        weight_sum = weight_sum + jnp.where(covered, row_weight[:, None], 0.0)
    weighted = pieces[0]
    for block_index in range(1, blocks):
        weighted = weighted + from_behind(
            pieces[block_index].astype(jnp.bfloat16), "genome", block_index
        ).astype(jnp.float32)
    stitched = weighted / jnp.maximum(weight_sum, 1.0)[None]
    head_cols = stitched[:, :, : 2 * STRIDE]
    received = []
    for distance in range(towers, 0, -1):
        received.append(
            from_behind(as_sent(head_cols), ("genome", "tower"), distance).astype(head_cols.dtype)
        )
    previous = jnp.concatenate(received, axis=1)
    extended = jnp.concatenate([previous, head_cols], axis=1)
    targets = extended.shape[0]
    prefix = jnp.concatenate(
        [jnp.zeros((targets, STRIDE + height, 1), jnp.float32), jnp.cumsum(extended, axis=2)],
        axis=2,
    )
    square = prefix[:, :, STRIDE + 1 : 2 * STRIDE + 1] - prefix[:, :, 1 : STRIDE + 1]
    contact = jnp.exp(extended[:, :, 1 : STRIDE + 1])
    row_pos = jnp.arange(STRIDE + height)
    col_pos = jnp.arange(STRIDE)
    out_row = jnp.arange(height)
    pick_square = (
        row_pos[None, :, None] == STRIDE + out_row[:, None, None] - col_pos[None, None, :]
    ).astype(jnp.float32)
    pick_up = (
        row_pos[None, :, None] == STRIDE + out_row[:, None, None] - col_pos[None, None, :] - 1
    ).astype(jnp.float32)
    insulation = jnp.einsum("txa,rxa->tr", square, pick_square, precision=lax.Precision.HIGHEST) / (
        STRIDE * STRIDE
    )
    upstream = jnp.einsum("txa,rxa->tr", contact, pick_up, precision=lax.Precision.HIGHEST)
    downstream = jnp.sum(contact[:, STRIDE:], axis=2)
    direction = (downstream - upstream) / (downstream + upstream)
    return (stitched, jnp.stack([insulation, direction]))


def solution(mesh):
    placed = (P("genome"), P(), P(), P(), P(), P(), P(), P(), P(), P())
    return jax.shard_map(
        per_device,
        mesh=mesh,
        in_specs=placed,
        out_specs=(P(None, ("genome", "tower"), None), P(None, None, ("genome", "tower"))),
        check_vma=False,
    )
```

profile of v0, /device:TPU:0, one launch (start us, length us, event | category | flops | bytes accessed | tf_op | source)
XLA Modules:
  0.0 87.9 jit_solution(6720304950513291291)
XLA Ops:
  0.6 1.2 %eq.48 = s32[64,2048]{1,0:T(8,128)S(1)} reshape(s32[131072]{0:T(1024)} %param.10) | data formatting | bytes 1048576 | tf_op jit(solution)/shard_map/eq | solution.py:33
  1.9 0.3 copy.61
  2.2 1.1 %eq.51 = s32[2048,4]{1,0:T(8,128)} iota(), iota_dimension=1 | iota | bytes 32768 | tf_op jit(solution)/shard_map/eq | solution.py:33
  3.3 1.8 %eq.52 = s32[8192]{0:T(1024)S(1)} reshape(s32[2048,4]{1,0:T(8,128)} %eq.51) | data formatting | bytes 65536 | tf_op jit(solution)/shard_map/eq | solution.py:33
  5.1 0.8 eq.49
  6.0 2.1 %fusion.71 = bf16[96,64]{0,1:T(8,128)(2,1)S(1)} fusion(bf16[96,8192]{1,0:T(8,128)(2,1)S(1)} %copy-done, s32[64,8192]{0,1:T(8,128)S(1)} %bitcast.216, s32[8192]{0:T(1024)S(1)} %eq.52), kind=kOutput, calls=%fused_computation.92 | convolution fusion | flops 101718016 | bytes 3715072 | tf_op jit(solution)/shard_map/dot_general | solution.py:37
  8.1 1.3 %collective-permute-start.2 = (bf16[96,64]{0,1:T(8,128)(2,1)S(1)}, bf16[96,64]{0,1:T(8,128)(2,1)S(1)}, u32[]{:S(2)}, u32[]{:S(2)}) collective-permute-start(bf16[96,64]{0,1:T(8,128)(2,1)S(1)} %fusion.71), channel_id=1, source_target_pairs={{12,0},{16,4},{20,8},{24,12},{28,16},{13,1},{17,5},{21,9},{25,13},... | collective-permute-start | bytes 36872 | tf_op jit(solution)/shard_map/ppermute | solution.py:14
  9.4 1.3 %collective-permute-start.1 = (bf16[96,64]{0,1:T(8,128)(2,1)S(1)}, bf16[96,64]{0,1:T(8,128)(2,1)S(1)}, u32[]{:S(2)}, u32[]{:S(2)}) collective-permute-start(bf16[96,64]{0,1:T(8,128)(2,1)S(1)} %fusion.71), channel_id=1, source_target_pairs={{8,0},{12,4},{16,8},{20,12},{24,16},{28,20},{9,1},{13,5},{17,9},{2... | collective-permute-start | bytes 36872 | tf_op jit(solution)/shard_map/ppermute | solution.py:14
  10.7 1.5 %collective-permute-start = (bf16[96,64]{0,1:T(8,128)(2,1)S(1)}, bf16[96,64]{0,1:T(8,128)(2,1)S(1)}, u32[]{:S(2)}, u32[]{:S(2)}) collective-permute-start(bf16[96,64]{0,1:T(8,128)(2,1)S(1)} %fusion.71), channel_id=1, source_target_pairs={{4,0},{8,4},{12,8},{16,12},{20,16},{24,20},{28,24},{5,1},{9,5},{13... | collective-permute-start | bytes 36872 | tf_op jit(solution)/shard_map/ppermute | solution.py:14
  12.4 0.1 convert_log-plus-one_fusion.2
  12.5 0.1 convert_log-plus-one_fusion
  12.6 0.1 fusion.234
  12.7 0.1 add_maximum_fusion
  12.8 2.9 %collective-permute-done.2 = bf16[96,64]{0,1:T(8,128)(2,1)S(1)} collective-permute-done((bf16[96,64]{0,1:T(8,128)(2,1)S(1)}, bf16[96,64]{0,1:T(8,128)(2,1)S(1)}, u32[]{:S(2)}, u32[]{:S(2)}) %collective-permute-start.2) | collective-permute-done | bytes 12320 | tf_op jit(solution)/shard_map/ppermute | solution.py:14
  15.7 0.4 collective-permute-done.1
  16.0 1.2 %collective-permute-done = bf16[96,64]{0,1:T(8,128)(2,1)S(1)} collective-permute-done((bf16[96,64]{0,1:T(8,128)(2,1)S(1)}, bf16[96,64]{0,1:T(8,128)(2,1)S(1)}, u32[]{:S(2)}, u32[]{:S(2)}) %collective-permute-start) | collective-permute-done | bytes 12320 | tf_op jit(solution)/shard_map/ppermute | solution.py:14
  17.3 0.5 maximum_convert_fusion.7
  17.9 0.5 maximum_convert_fusion.6
  18.4 0.5 maximum_convert_fusion.5
  18.9 0.5 maximum_convert_fusion.4
  19.4 0.5 maximum_convert_fusion.3
  19.9 0.3 fusion.69
  20.2 0.3 convolution_bitcast_fusion.6
  20.6 0.1 pad_dynamic-slice_fusion.7
  20.9 0.1 copy.71
  21.0 1.2 %multiply_convert_fusion.3 = (bf16[48,1,20,256]{3,0,2,1:T(8,128)(2,1)S(1)}, bf16[48,1,20,256]{3,0,2,1:T(8,128)(2,1)S(1)}, bf16[48,1,20,256]{3,0,2,1:T(8,128)(2,1)S(1)}, bf16[48,1,20,256]{3,0,2,1:T(8,128)(2,1)S(1)}) fusion(f32[20]{0:T(128)S(1)} %get-tuple-element.75, f32[20,256]{1,0:T(8,128)S(1)} %get-tuple-element.87, f32[48]{0:T(128)S(1)} %copy-done.9, ...), kind=kLoop, calls=%fused_computation.100 | loop fusion | flops 5898240 | bytes 2113024 | tf_op jit(solution)/shard_map/convert_element_type | solution.py:109
  22.2 2.2 %maximum_convert_fusion.2 = f32[48,4,20,256]{3,0,2,1:T(8,128)} fusion(bf16[48,1,20,256]{3,0,2,1:T(8,128)(2,1)S(1)} %get-tuple-element.49, bf16[48,1,20,256]{3,0,2,1:T(8,128)(2,1)S(1)} %get-tuple-element.48, bf16[48,1,20,256]{3,0,2,1:T(8,128)(2,1)S(1)} %get-tuple-element.47, bf16[48,1,20,256]{3,0,2,1:T(8,128)(2,1)S(1)} %get-tuple-element.46), kind=kLoop, calls=%fused_computation.59 | loop fusion | flops 3932160 | bytes 5898240 | tf_op jit(solution)/shard_map/convert_element_type | solution.py:152
  24.4 0.5 select_convert_fusion
  25.0 5.5 %pad_slice_fusion.1 = (bf16[48,4,18,256]{3,0,2,1:T(8,128)(2,1)}, bf16[48,4,18,256]{3,0,2,1:T(8,128)(2,1)S(1)}, bf16[48,4,18,256]{3,0,2,1:T(8,128)(2,1)S(1)}, bf1...) fusion(bf16[48,4,20,256]{3,0,2,1:T(8,128)(2,1)S(1)} %select_con, ...), kind=kLoop, calls=%fused_computation.39 | loop fusion | bytes 23199744 | tf_op jit(solution)/shard_map/slice | solution.py:69
  30.4 2.3 %fusion = f32[4,18,256,48]{2,3,1,0:T(8,128)} fusion(bf16[48,4,18,256]{3,0,2,1:T(8,128)(2,1)S(1)} %get-tuple-element.11, bf16[48,4,18,256]{3,0,2,1:T(8,128)(2,1)S(1)} %get-tuple-element.17, bf16[48,4,18,256]{3,0,2,1:T(8,128)(2,1)S(1)} %get-tuple-element.18, bf16[2,3,48,144]{3,2,1,0:T(8,128)(2,1)S(1)} %copy-done.5), kind=kOutput, calls=%fused_computation | convolution fusion | flops 270729216 | bytes 8871936 | tf_op jit(solution)/shard_map/oc,ckrj->okrj/dot_general | solution.py:74
  32.7 2.4 %fusion.6 = f32[4,18,256,48]{2,3,1,0:T(8,128)} fusion(bf16[48,4,18,256]{3,0,2,1:T(8,128)(2,1)S(1)} %get-tuple-element.13, bf16[48,4,18,256]{3,0,2,1:T(8,128)(2,1)S(1)} %get-tuple-element.16, bf16[48,4,18,256]{3,0,2,1:T(8,128)(2,1)S(1)} %get-tuple-element.12, bf16[2,3,48,144]{3,2,1,0:T(8,128)(2,1)S(1)} %copy-done.5), kind=kOutput, calls=%fused_computation.6 | convolution fusion | flops 270729216 | bytes 8871936 | tf_op jit(solution)/shard_map/oc,ckrj->okrj/dot_general | solution.py:74
  35.1 8.4 %select_convert_fusion.1 = (bf16[48,4,18,256]{3,0,2,1:T(8,128)(2,1)S(1)}, f32[48,4,18,256]{3,0,2,1:T(8,128)}) fusion(pred[4,18]{1,0:T(4,128)(4,1)S(1)} %compare_and_fusion, bf16[48,4,18,256]{3,0,2,1:T(8,128)(2,1)} %get-tuple-element.14, bf16[48,4,18,256]{3,0,2,1:T(8,128)(2,1)} %get-tuple-element.15, bf16[48,4,18,256]{3,0,2,1:T(8,128)(2,1)} %get-tuple-element.10, ...), kind=kOutput, calls=%fused_computation.45 | convolution fusion | flops 362741760 | bytes 21271040 | tf_op jit(solution)/shard_map/oc,ckrj->okrj/dot_general | solution.py:162
  43.5 3.9 %pad_slice_fusion.7 = (bf16[48,4,16,256]{3,0,2,1:T(8,128)(2,1)S(1)}, bf16[48,4,16,256]{3,0,2,1:T(8,128)(2,1)S(1)}, bf16[48,4,16,256]{3,0,2,1:T(8,128)(2,1)S(1)},...) fusion(bf16[48,4,18,256]{3,0,2,1:T(8,128)(2,1)S(1)} %get-tuple-, ...), kind=kLoop, calls=%fused_computation.48 | loop fusion | bytes 20643840 | tf_op jit(solution)/shard_map/slice | solution.py:69
  47.4 0.8 fusion.18
  48.2 0.8 fusion.24
  49.0 1.3 %maximum_convert_fusion.1 = bf16[4,16,256,48]{2,3,1,0:T(8,128)(2,1)S(1)} fusion(f32[4,16,256,48]{2,3,1,0:T(8,128)S(1)} %fusion.18, f32[4,16,256,48]{2,3,1,0:T(8,128)S(1)} %fusion.24, bf16[48,4,16,256]{3,0,2,1:T(8,128)(2,1)S(1)} %get-tuple-element.23, bf16[48,4,16,256]{3,0,2,1:T(8,128)(2,1)S(1)} %get-tuple-element.24, ...), kind=kOutput, calls=%fused_computation.56 | convolution fusion | flops 243793920 | bytes 12607488 | tf_op jit(solution)/shard_map/oc,ckrj->okrj/dot_general | solution.py:74
  50.3 2.7 %fusion.53 = f32[5,4,16,256]{3,0,2,1:T(8,128)S(1)} fusion(f32[48,4,18,256]{3,0,2,1:T(8,128)} %get-tuple-element.71, bf16[4,16,256,48]{2,3,1,0:T(8,128)(2,1)S(1)} %maximum_convert_fusion.1, bf16[2,48,48]{2,1,0:T(8,128)(2,1)S(1)} %copy-done.4, bf16[5,48]{1,0:T(8,128)(2,1)S(1)} %copy-done.6), kind=kOutput, calls=%fused_computation.63 | convolution fusion | flops 85721088 | bytes 5060608 | tf_op jit(solution)/shard_map/tc,ckrj->tkrj/dot_general | solution.py:166
  53.1 0.1 pad_dynamic-slice_fusion
  53.2 0.2 reshape.612
  53.4 7.1 %collective-permute-start.5 = (bf16[5,16,256]{2,1,0:T(8,128)(2,1)S(1)}, bf16[5,16,256]{2,1,0:T(8,128)(2,1)S(1)}, u32[]{:S(2)}, u32[]{:S(2)}) collective-permute-start(bf16[5,16,256]{2,1,0:T(8,128)(2,1)S(1)} %fusion.132), channel_id=1, source_target_pairs={{0,12},{4,16},{8,20},{12,24},{16,28},{1,13},{5,17},{9,21},{13,25},... | collective-permute-start | bytes 122888 | tf_op jit(solution)/shard_map/ppermute | solution.py:14
  60.6 0.1 pad_dynamic-slice_fusion.1
  60.7 0.2 reshape.610
  60.9 3.9 %collective-permute-start.4 = (bf16[5,16,256]{2,1,0:T(8,128)(2,1)S(1)}, bf16[5,16,256]{2,1,0:T(8,128)(2,1)S(1)}, u32[]{:S(2)}, u32[]{:S(2)}) collective-permute-start(bf16[5,16,256]{2,1,0:T(8,128)(2,1)S(1)} %fusion.133), channel_id=1, source_target_pairs={{0,8},{4,12},{8,16},{12,20},{16,24},{20,28},{1,9},{5,13},{9,17},{1... | collective-permute-start | bytes 122888 | tf_op jit(solution)/shard_map/ppermute | solution.py:14
  64.9 0.1 pad_dynamic-slice_fusion.2
  65.0 0.2 reshape.608
  65.3 3.8 %collective-permute-start.3 = (bf16[5,16,256]{2,1,0:T(8,128)(2,1)S(1)}, bf16[5,16,256]{2,1,0:T(8,128)(2,1)S(1)}, u32[]{:S(2)}, u32[]{:S(2)}) collective-permute-start(bf16[5,16,256]{2,1,0:T(8,128)(2,1)S(1)} %fusion.134), channel_id=1, source_target_pairs={{0,4},{4,8},{8,12},{12,16},{16,20},{20,24},{24,28},{1,5},{5,9},{9,... | collective-permute-start | bytes 122888 | tf_op jit(solution)/shard_map/ppermute | solution.py:14
  69.1 0.1 pad_dynamic-slice_fusion.3
  69.2 0.2 reshape.606
  69.4 1.3 %collective-permute-done.3 = bf16[5,16,256]{2,1,0:T(8,128)(2,1)S(1)} collective-permute-done((bf16[5,16,256]{2,1,0:T(8,128)(2,1)S(1)}, bf16[5,16,256]{2,1,0:T(8,128)(2,1)S(1)}, u32[]{:S(2)}, u32[]{:S(2)}) %collective-permute-start.3) | collective-permute-done | bytes 40992 | tf_op jit(solution)/shard_map/ppermute | solution.py:14
  70.7 0.1 fusion.138
  70.9 4.2 %collective-permute-start.6 = (bf16[5,16,128]{2,1,0:T(8,128)(2,1)S(1)}, bf16[5,16,128]{2,1,0:T(8,128)(2,1)S(1)}, u32[]{:S(2)}, u32[]{:S(2)}) collective-permute-start(bf16[5,16,128]{2,1,0:T(8,128)(2,1)S(1)} %slice.460), channel_id=1, source_target_pairs={{0,4},{1,5},{2,6},{3,7},{4,8},{5,9},{6,10},{7,11},{8,12},{9,13},{1... | collective-permute-start | bytes 61448 | tf_op jit(solution)/shard_map/ppermute | solution.py:14
  75.1 1.3 %collective-permute-start.7 = (bf16[5,16,128]{2,1,0:T(8,128)(2,1)S(1)}, bf16[5,16,128]{2,1,0:T(8,128)(2,1)S(1)}, u32[]{:S(2)}, u32[]{:S(2)}) collective-permute-start(bf16[5,16,128]{2,1,0:T(8,128)(2,1)S(1)} %slice.460), channel_id=1, source_target_pairs={{0,3},{1,4},{2,5},{3,6},{4,7},{5,8},{6,9},{7,10},{8,11},{9,12},{10... | collective-permute-start | bytes 61448 | tf_op jit(solution)/shard_map/ppermute | solution.py:14
  76.4 3.4 %collective-permute-start.8 = (bf16[5,16,128]{2,1,0:T(8,128)(2,1)S(1)}, bf16[5,16,128]{2,1,0:T(8,128)(2,1)S(1)}, u32[]{:S(2)}, u32[]{:S(2)}) collective-permute-start(bf16[5,16,128]{2,1,0:T(8,128)(2,1)S(1)} %slice.460), channel_id=1, source_target_pairs={{0,2},{1,3},{2,4},{3,5},{4,6},{5,7},{6,8},{7,9},{8,10},{9,11},{10,... | collective-permute-start | bytes 61448 | tf_op jit(solution)/shard_map/ppermute | solution.py:14
  79.8 3.3 %collective-permute-start.9 = (bf16[5,16,128]{2,1,0:T(8,128)(2,1)S(1)}, bf16[5,16,128]{2,1,0:T(8,128)(2,1)S(1)}, u32[]{:S(2)}, u32[]{:S(2)}) collective-permute-start(bf16[5,16,128]{2,1,0:T(8,128)(2,1)S(1)} %slice.460), channel_id=1, source_target_pairs={{0,1},{1,2},{2,3},{3,4},{4,5},{5,6},{6,7},{7,8},{8,9},{9,10},{10,1... | collective-permute-start | bytes 61448 | tf_op jit(solution)/shard_map/ppermute | solution.py:14
  83.2 0.8 collective-permute-done.9
  83.9 0.1 slice.309
  84.0 1.5 %reduce_window_sum.11 = f32[5,80,128]{2,1,0:T(8,128)S(1)} reduce-window(f32[5,80,128]{2,1,0:T(8,128)S(1)} %slice_dynamic-update-slice_fusion, f32[]{:T(128)} %constant.96.clone.1), window={size=1x1x128 pad=0_0x0_0x127_0}, to_apply=%region_0.1 | reduce-window | flops 6502400 | bytes 409604 | tf_op jit(solution)/shard_map/jit(cumsum)/reduce_window_sum | solution.py:199
  85.6 0.2 copy.90
  85.8 0.1 slice_reduce_fusion
  86.0 0.1 slice_subtract_fusion
  86.1 0.2 copy.72
  86.3 0.5 divide_bitcast_fusion
  86.8 0.5 fusion.73
  87.3 0.6 copy.74
  (71 shorter events, 1.0 us)
Async XLA Ops:
  0.6 5.3 %copy-start = (bf16[96,8192]{1,0:T(8,128)(2,1)S(1)}, bf16[96,8192]{1,0:T(8,128)(2,1)}, u32[]{:S(2)}) copy-start(bf16[96,8192]{1,0:T(8,128)(2,1)} %param.12) | copy-start | bytes 4718596
  5.9 6.4 %copy-start.8 = (s32[256]{0:T(256)S(1)}, s32[256]{0:T(256)}, u32[]{:S(2)}) copy-start(s32[256]{0:T(256)} %param.11) | copy-start | bytes 3076
  5.9 11.4 %copy-start.7 = (bf16[6,96,48]{1,2,0:T(8,128)(2,1)S(1)}, bf16[6,96,48]{1,2,0:T(8,128)(2,1)}, u32[]{:S(2)}) copy-start(bf16[6,96,48]{1,2,0:T(8,128)(2,1)} %param.14) | copy-start | bytes 165892
  5.9 11.4 %copy-start.10 = (bf16[6,48,288]{2,1,0:T(8,128)(2,1)S(1)}, bf16[6,48,288]{2,1,0:T(8,128)(2,1)}, u32[]{:S(2)}) copy-start(bf16[6,48,288]{2,1,0:T(8,128)(2,1)} %param.13) | copy-start | bytes 497668
  8.1 7.6 %collective-permute-start.2 = (bf16[96,64]{0,1:T(8,128)(2,1)S(1)}, bf16[96,64]{0,1:T(8,128)(2,1)S(1)}, u32[]{:S(2)}, u32[]{:S(2)}) collective-permute-start(bf16[96,64]{0,1:T(8,128)(2,1)S(1)} %fusion.71), channel_id=1, source_target_pairs={{12,0},{16,4},{20,8},{24,12},{28,16},{13,1},{17,5},{21,9},{25,13},... | collective-permute-start | bytes 36872 | tf_op jit(solution)/shard_map/ppermute | solution.py:14
  9.4 6.7 %collective-permute-start.1 = (bf16[96,64]{0,1:T(8,128)(2,1)S(1)}, bf16[96,64]{0,1:T(8,128)(2,1)S(1)}, u32[]{:S(2)}, u32[]{:S(2)}) collective-permute-start(bf16[96,64]{0,1:T(8,128)(2,1)S(1)} %fusion.71), channel_id=1, source_target_pairs={{8,0},{12,4},{16,8},{20,12},{24,16},{28,20},{9,1},{13,5},{17,9},{2... | collective-permute-start | bytes 36872 | tf_op jit(solution)/shard_map/ppermute | solution.py:14
  10.7 6.6 %collective-permute-start = (bf16[96,64]{0,1:T(8,128)(2,1)S(1)}, bf16[96,64]{0,1:T(8,128)(2,1)S(1)}, u32[]{:S(2)}, u32[]{:S(2)}) collective-permute-start(bf16[96,64]{0,1:T(8,128)(2,1)S(1)} %fusion.71), channel_id=1, source_target_pairs={{4,0},{8,4},{12,8},{16,12},{20,16},{24,20},{28,24},{5,1},{9,5},{13... | collective-permute-start | bytes 36872 | tf_op jit(solution)/shard_map/ppermute | solution.py:14
  17.3 2.9 %copy-start.3 = (bf16[96,96]{1,0:T(8,128)(2,1)S(1)}, bf16[96,96]{1,0:T(8,128)(2,1)}, u32[]{:S(2)}) copy-start(bf16[96,96]{1,0:T(8,128)(2,1)} %param.15) | copy-start | bytes 55300
  17.8 3.2 %copy-start.9 = (f32[48]{0:T(128)S(1)}, f32[48]{0:T(128)}, u32[]{:S(2)}) copy-start(f32[48]{0:T(128)} %param.16) | copy-start | bytes 580
  24.9 5.5 %copy-start.5 = (bf16[2,3,48,144]{3,2,1,0:T(8,128)(2,1)S(1)}, bf16[2,3,48,144]{3,2,1,0:T(8,128)(2,1)}, u32[]{:S(2)}) copy-start(bf16[2,3,48,144]{3,2,1,0:T(8,128)(2,1)} %param.17) | copy-start | bytes 248836
  32.7 2.4 %copy-start.4 = (bf16[2,48,48]{2,1,0:T(8,128)(2,1)S(1)}, bf16[2,48,48]{2,1,0:T(8,128)(2,1)}, u32[]{:S(2)}) copy-start(bf16[2,48,48]{2,1,0:T(8,128)(2,1)} %param.18) | copy-start | bytes 27652
  49.0 1.3 %copy-start.6 = (bf16[5,48]{1,0:T(8,128)(2,1)S(1)}, bf16[5,48]{1,0:T(8,128)(2,1)}, u32[]{:S(2)}) copy-start(bf16[5,48]{1,0:T(8,128)(2,1)} %param.19) | copy-start | bytes 1444
  53.4 16.0 %collective-permute-start.5 = (bf16[5,16,256]{2,1,0:T(8,128)(2,1)S(1)}, bf16[5,16,256]{2,1,0:T(8,128)(2,1)S(1)}, u32[]{:S(2)}, u32[]{:S(2)}) collective-permute-start(bf16[5,16,256]{2,1,0:T(8,128)(2,1)S(1)} %fusion.132), channel_id=1, source_target_pairs={{0,12},{4,16},{8,20},{12,24},{16,28},{1,13},{5,17},{9,21},{13,25},... | collective-permute-start | bytes 122888 | tf_op jit(solution)/shard_map/ppermute | solution.py:14
  60.9 8.5 %collective-permute-start.4 = (bf16[5,16,256]{2,1,0:T(8,128)(2,1)S(1)}, bf16[5,16,256]{2,1,0:T(8,128)(2,1)S(1)}, u32[]{:S(2)}, u32[]{:S(2)}) collective-permute-start(bf16[5,16,256]{2,1,0:T(8,128)(2,1)S(1)} %fusion.133), channel_id=1, source_target_pairs={{0,8},{4,12},{8,16},{12,20},{16,24},{20,28},{1,9},{5,13},{9,17},{1... | collective-permute-start | bytes 122888 | tf_op jit(solution)/shard_map/ppermute | solution.py:14
  65.3 5.5 %collective-permute-start.3 = (bf16[5,16,256]{2,1,0:T(8,128)(2,1)S(1)}, bf16[5,16,256]{2,1,0:T(8,128)(2,1)S(1)}, u32[]{:S(2)}, u32[]{:S(2)}) collective-permute-start(bf16[5,16,256]{2,1,0:T(8,128)(2,1)S(1)} %fusion.134), channel_id=1, source_target_pairs={{0,4},{4,8},{8,12},{12,16},{16,20},{20,24},{24,28},{1,5},{5,9},{9,... | collective-permute-start | bytes 122888 | tf_op jit(solution)/shard_map/ppermute | solution.py:14
  69.1 18.9 %copy-start.1 = (bf16[96,8192]{1,0:T(8,128)(2,1)S(1)}, bf16[96,8192]{1,0:T(8,128)(2,1)}, u32[]{:S(2)}) copy-start(bf16[96,8192]{1,0:T(8,128)(2,1)} %param.12) | copy-start | bytes 4718596
  70.8 17.1 %copy-start.2 = (f32[5,16,256]{2,1,0:T(8,128)}, f32[5,16,256]{2,1,0:T(8,128)S(1)}, u32[]{:S(2)}) copy-start(f32[5,16,256]{2,1,0:T(8,128)S(1)} %fusion.138) | copy-start | bytes 245764
  70.9 12.2 %collective-permute-start.6 = (bf16[5,16,128]{2,1,0:T(8,128)(2,1)S(1)}, bf16[5,16,128]{2,1,0:T(8,128)(2,1)S(1)}, u32[]{:S(2)}, u32[]{:S(2)}) collective-permute-start(bf16[5,16,128]{2,1,0:T(8,128)(2,1)S(1)} %slice.460), channel_id=1, source_target_pairs={{0,4},{1,5},{2,6},{3,7},{4,8},{5,9},{6,10},{7,11},{8,12},{9,13},{1... | collective-permute-start | bytes 61448 | tf_op jit(solution)/shard_map/ppermute | solution.py:14
  75.1 8.0 %collective-permute-start.7 = (bf16[5,16,128]{2,1,0:T(8,128)(2,1)S(1)}, bf16[5,16,128]{2,1,0:T(8,128)(2,1)S(1)}, u32[]{:S(2)}, u32[]{:S(2)}) collective-permute-start(bf16[5,16,128]{2,1,0:T(8,128)(2,1)S(1)} %slice.460), channel_id=1, source_target_pairs={{0,3},{1,4},{2,5},{3,6},{4,7},{5,8},{6,9},{7,10},{8,11},{9,12},{10... | collective-permute-start | bytes 61448 | tf_op jit(solution)/shard_map/ppermute | solution.py:14
  76.4 6.7 %collective-permute-start.8 = (bf16[5,16,128]{2,1,0:T(8,128)(2,1)S(1)}, bf16[5,16,128]{2,1,0:T(8,128)(2,1)S(1)}, u32[]{:S(2)}, u32[]{:S(2)}) collective-permute-start(bf16[5,16,128]{2,1,0:T(8,128)(2,1)S(1)} %slice.460), channel_id=1, source_target_pairs={{0,2},{1,3},{2,4},{3,5},{4,6},{5,7},{6,8},{7,9},{8,10},{9,11},{10,... | collective-permute-start | bytes 61448 | tf_op jit(solution)/shard_map/ppermute | solution.py:14
  79.8 4.1 %collective-permute-start.9 = (bf16[5,16,128]{2,1,0:T(8,128)(2,1)S(1)}, bf16[5,16,128]{2,1,0:T(8,128)(2,1)S(1)}, u32[]{:S(2)}, u32[]{:S(2)}) collective-permute-start(bf16[5,16,128]{2,1,0:T(8,128)(2,1)S(1)} %slice.460), channel_id=1, source_target_pairs={{0,1},{1,2},{2,3},{3,4},{4,5},{5,6},{6,7},{7,8},{8,9},{9,10},{10,1... | collective-permute-start | bytes 61448 | tf_op jit(solution)/shard_map/ppermute | solution.py:14
where the time goes:
time: 88.9 us; the launch traced here: 87.9 us
  starting transfers between devices  31 us (35%)
  matrix products  24.6 us (28%)
  local copies, waits for them, and re-layouts  17.8 us (20%)
  waiting for transfers between devices  6.54 us (7%)
  other arithmetic  6.48 us (7%)
  between operations  1.43 us (2%)
    ppermute x10, starting transfers between devices, from_behind(): return lax.ppermute(block, axis, route)  31 us
    slice x2, local copies, waits for them, and re-layouts, conv_rows(): padded[:, :, row_tap:row_tap + height, col_tap:col_tap + extent]  9.42 us
    dot_general x1, matrix products, per_device(): jnp.einsum('oc,ckrj->okrj', tower_mix[layer_index], squeezed, preferred_e...  8.36 us
    dot_general x5, matrix products, conv_rows(): jnp.einsum('oc,ckrj->okrj', kernel[row_tap], stacked, preferred_element_t...  7.51 us
    ppermute x10, waiting for transfers between devices, from_behind(): return lax.ppermute(block, axis, route)  6.54 us
    eq x5, local copies, waits for them, and re-layouts, stem_features(): letters[:, :, None] == jnp.arange(4, dtype=jnp.int32)[None, None, :]  5.25 us
    dot_general x1, matrix products, per_device(): jnp.einsum('tc,ckrj->tkrj', head_weight, final_act, preferred_element_typ...  2.65 us
    dot_general x5, matrix products, trunk_stream(): jnp.dot(trunk_out[layer_index], squeezed, preferred_element_type=jnp.floa...  2.36 us
  transfers between devices with their start and end apart: 10, of which 5 were waited for; matrix products, arithmetic and copies ran while one was open for 2% of the time, Pallas kernels for 0%

commit v1 on v0

v1 whole, which is shorter than its diff:
```python
import functools

import jax
import jax.numpy as jnp
from jax import lax
from jax.experimental import pallas as pl
from jax.experimental.pallas import tpu as pltpu
from jax.sharding import PartitionSpec as P

BP = 2048
STRIDE = 64
BINS = 256
BLOCKS = BINS // STRIDE
LANES = 128
F32 = jnp.float32
BF16 = jnp.bfloat16
VMEM_BYTES = 48 * 1024 * 1024


def from_behind(block, axis, distance):
    devices = range(lax.axis_size(axis))
    route = [(i - distance, i) for i in devices if i - distance in devices]
    return lax.ppermute(block, axis, route)


def dot(a, b):
    return jnp.dot(a, b, preferred_element_type=F32)


def stem_kernel(bins, bases_hbm, weight_hbm, out_ref, bases, weight, base_sem, weight_sem):
    groups = BP // LANES
    chunks = weight.shape[0]
    span = weight.shape[2]
    base_copy = pltpu.make_async_copy(bases_hbm, bases, base_sem)
    base_copy.start()
    copies = []
    for k in range(chunks):
        copy = pltpu.make_async_copy(
            weight_hbm.at[:, pl.ds(k * span, span)], weight.at[k], weight_sem.at[k]
        )
        copy.start()
        copies.append(copy)
    row = lax.broadcasted_iota(jnp.int32, (LANES, 4 * LANES), 0)
    col = lax.broadcasted_iota(jnp.int32, (LANES, 4 * LANES), 1)
    repeat = (row == col // 4).astype(F32).astype(BF16)
    letter = (lax.broadcasted_iota(jnp.int32, (bins, 4 * LANES), 1) % 4).astype(F32)
    base_copy.wait()
    total = None
    per_chunk = groups // chunks
    for k in range(chunks):
        hot = []
        for q in range(per_chunk):
            rows = bases[pl.ds(k * per_chunk + q, bins, stride=groups), :]
            spread = dot(rows.astype(F32).astype(BF16), repeat)
            hot.append(jnp.where(spread == letter, 1.0, 0.0).astype(BF16))
        hot = jnp.concatenate(hot, axis=1)
        copies[k].wait()
        part = lax.dot_general(
            weight[k], hot, (((1,), (1,)), ((), ())), preferred_element_type=F32
        )
        total = part if total is None else total + part
    out_ref[...] = total.astype(BF16)


def stem(genome_bases, stem_weight):
    bins = genome_bases.shape[0] // BP
    channels, depth = stem_weight.shape
    chunks = 4
    return pl.pallas_call(
        functools.partial(stem_kernel, bins),
        out_shape=jax.ShapeDtypeStruct((channels, bins), BF16),
        in_specs=[pl.BlockSpec(memory_space=pl.ANY)] * 2,
        out_specs=pl.BlockSpec(memory_space=pltpu.VMEM),
        scratch_shapes=[
            pltpu.VMEM((genome_bases.shape[0] // LANES, LANES), jnp.int32),
            pltpu.VMEM((chunks, channels, depth // chunks), BF16),
            pltpu.SemaphoreType.DMA,
            pltpu.SemaphoreType.DMA((chunks,)),
        ],
        compiler_params=pltpu.CompilerParams(vmem_limit_bytes=VMEM_BYTES),
        name="stem",
    )(genome_bases.reshape(-1, LANES), stem_weight)


def banded(kernel, rows):
    taps, out_channels, depth = kernel.shape
    flat = jnp.concatenate([kernel[u] for u in range(taps)], axis=1)
    bands = []
    for r in range(rows):
        parts = [flat]
        if r:
            parts.insert(0, jnp.zeros((out_channels, r * depth), BF16))
        if rows - 1 - r:
            parts.append(jnp.zeros((out_channels, (rows - 1 - r) * depth), BF16))
        bands.append(jnp.concatenate(parts, axis=1) if len(parts) > 1 else flat)
    return jnp.concatenate(bands, axis=0)


def block_diagonal(matrix, count):
    height, width = matrix.shape
    tiled = jnp.concatenate([jnp.concatenate([matrix] * count, axis=1)] * count, axis=0)
    row = lax.broadcasted_iota(jnp.int32, tiled.shape, 0) // height
    col = lax.broadcasted_iota(jnp.int32, tiled.shape, 1) // width
    return jnp.where(row == col, tiled, jnp.zeros((), BF16))


def head_by_row(head, count):
    targets, width = head.shape
    wide = jnp.concatenate([head] * count, axis=1)
    tall = jnp.broadcast_to(wide[:, None, :], (targets, count, count * width))
    row = lax.broadcasted_iota(jnp.int32, tall.shape, 1)
    col = lax.broadcasted_iota(jnp.int32, tall.shape, 2) // width
    return jnp.where(row == col, tall, jnp.zeros((), BF16)).reshape(targets * count, count * width)


def segments(margin):
    sizes = [BINS - STRIDE * b + margin + 1 for b in range(BLOCKS)]
    offsets = [sum(sizes[:b]) for b in range(BLOCKS)]
    lanes = -(-sum(sizes) // LANES) * LANES
    return sizes, offsets, lanes


def shifted(values, offset):
    if offset == 0:
        return values
    channels, extent = values.shape
    edge = jnp.zeros((channels, abs(offset)), values.dtype)
    if offset >= 0:
        return jnp.concatenate([values[:, offset:], edge], axis=1)
    return jnp.concatenate([edge, values[:, : extent + offset]], axis=1)


def main_kernel(
    height,
    groups,
    place_ref,
    *refs,
):
    feature_refs = refs[: 2 * BLOCKS - 1]
    (
        trunk_in,
        trunk_out,
        pair_weight,
        rate_ref,
        conv_a,
        conv_b,
        mix_a,
        mix_b,
        head,
        row_weight,
        stitched_ref,
        keep_ref,
        *rest,
    ) = refs[2 * BLOCKS - 1 :]
    send_refs = rest[: STRIDE // height]
    taps_a, taps_b, grid_ref, final_ref = rest[STRIDE // height :]
    margin = 2
    sizes, offsets, lanes = segments(margin)
    tower_row = place_ref[0] * height
    channels = rate_ref.shape[0]
    depth = 3 * channels

    blocks = jnp.concatenate([r[...] for r in feature_refs], axis=1)
    extent = BINS
    windows = []
    for b in range(BLOCKS):
        first = (BLOCKS - 1 - b) * STRIDE
        windows.append(blocks[:, first : first + BINS].astype(F32))
    stream = jnp.concatenate(windows, axis=1)
    layers = trunk_in.shape[0]
    for layer in range(layers):
        dilation = max(1, extent // 2 ** (layers - layer))
        active = jax.nn.relu(stream)
        parts = [active[:, b * BINS : (b + 1) * BINS] for b in range(BLOCKS)]
        stacked = jnp.concatenate(
            [
                jnp.concatenate([shifted(p, o) for p in parts], axis=1).astype(BF16)
                for o in (-dilation, 0, dilation)
            ],
            axis=0,
        )
        inner = dot(trunk_in[layer], stacked)
        squeezed = jax.nn.relu(inner).astype(BF16)
        stream = stream + dot(trunk_out[layer], squeezed)
    projected = dot(pair_weight[...], jax.nn.relu(stream).astype(BF16))

    lane = lax.broadcasted_iota(jnp.int32, (1, lanes), 1)
    block_of = jnp.zeros((1, lanes), jnp.int32)
    start_of = jnp.zeros((1, lanes), jnp.int32)
    for b in range(1, BLOCKS):
        block_of = jnp.where(lane >= offsets[b], b, block_of)
        start_of = jnp.where(lane >= offsets[b], offsets[b], start_of)
    step = lane - start_of
    first_row = STRIDE * block_of + tower_row - margin
    column = first_row + step
    in_column = (column < BINS) & (column >= 0)

    right = []
    left = []
    for b in range(BLOCKS):
        begin = STRIDE * b + tower_row - margin
        turn = jnp.where(begin > 0, BINS - begin, -begin)
        terms = projected[:, b * BINS : (b + 1) * BINS]
        turned = pltpu.roll(terms, turn, 1)
        left.append(turned[:channels, :LANES])
        own = turned[channels:]
        if sizes[b] > BINS:
            own = jnp.concatenate([own, own[:, : sizes[b] - BINS]], axis=1)
        right.append(own[:, : sizes[b]])
    used = sum(sizes)
    if lanes > used:
        right.append(jnp.zeros((channels, lanes - used), F32))
    right = jnp.concatenate(right, axis=1)
    rate = jnp.broadcast_to(rate_ref[...], (channels, LANES))
    rate = jnp.concatenate([rate] * (lanes // LANES), axis=1)

    def place_taps(ref, slot, act):
        before = pltpu.roll(act, 1, 1)
        after = pltpu.roll(act, lanes - 1, 1)
        ref[pl.ds(slot * depth, channels), :] = before.astype(BF16)
        ref[pl.ds(slot * depth + channels, channels), :] = act.astype(BF16)
        ref[pl.ds(slot * depth + 2 * channels, channels), :] = after.astype(BF16)

    def inside(row):
        at = first_row + row
        return in_column & (at >= 0) & (at < BINS)

    for row in range(height + 2 * margin):
        apart = jnp.abs(step - row).astype(F32)
        decay = jnp.log1p(apart)
        tiles = []
        for tile in range(lanes // LANES):
            piece = None
            here = lane[:, tile * LANES : (tile + 1) * LANES]
            for b in range(BLOCKS):
                low, high = offsets[b], offsets[b] + sizes[b]
                if high <= tile * LANES or low >= (tile + 1) * LANES:
                    continue
                spread = jnp.broadcast_to(left[b][:, row : row + 1], (channels, LANES))
                piece = spread if piece is None else jnp.where(here >= low, spread, piece)
            tiles.append(piece)
        mixed = jnp.concatenate(tiles, axis=1) + right - rate * decay
        place_taps(taps_a, row, jnp.where(inside(row), jnp.maximum(mixed, 0.0), 0.0))

    span = groups[0]
    for group in range((height + 2) // span):
        first = group * span
        conv = dot(conv_a[...], taps_a[pl.ds(first * depth, (span + 2) * depth), :])
        update = dot(mix_a[...], jnp.maximum(conv, 0.0).astype(BF16))
        for r in range(span):
            row = first + r
            kept = taps_a[pl.ds((row + 1) * depth + channels, channels), :].astype(F32)
            grid = kept + update[r * channels : (r + 1) * channels]
            if 1 <= row <= height:
                grid_ref[pl.ds((row - 1) * channels, channels), :] = grid
            place_taps(taps_b, row, jnp.where(inside(row + 1), jnp.maximum(grid, 0.0), 0.0))
    span = groups[1]
    for group in range(height // span):
        first = group * span
        conv = dot(conv_b[...], taps_b[pl.ds(first * depth, (span + 2) * depth), :])
        update = dot(mix_b[...], jnp.maximum(conv, 0.0).astype(BF16))
        rows = pl.ds(first * channels, span * channels)
        final_ref[rows, :] = jnp.maximum(grid_ref[rows, :] + update, 0.0).astype(BF16)
    targets = head.shape[0] // height
    contact = dot(head[...], final_ref[...]).reshape(targets, height, lanes)

    local = lax.broadcasted_iota(jnp.int32, (height, BINS), 0)
    ahead = lax.broadcasted_iota(jnp.int32, (height, BINS), 1)
    weight_sum = jnp.zeros((height, BINS), F32)
    weights = []
    for b in range(BLOCKS):
        weight = jnp.concatenate([row_weight[b]] * (BINS // LANES), axis=1)
        reach = STRIDE * b + tower_row + local + ahead < BINS
        weight = jnp.where(reach, weight, 0.0)
        weights.append(weight)
        weight_sum = weight_sum + weight
    scale = 1.0 / jnp.maximum(weight_sum, 1.0)
    weights = [w * scale for w in weights]
    stitched = []
    map_row = lax.broadcasted_iota(jnp.int32, (height, lanes), 0)
    for t in range(targets):
        band = None
        skewed = contact[t]
        for bit in range((height - 1).bit_length()):
            turned = pltpu.roll(skewed, lanes - (1 << bit), 1)
            skewed = jnp.where((map_row >> bit) & 1 == 1, turned, skewed)
        for b in range(BLOCKS):
            first, reach = offsets[b] + margin, BINS - STRIDE * b
            piece = skewed[:, first : first + reach]
            if reach < BINS:
                piece = jnp.concatenate([piece, jnp.zeros((height, BINS - reach), F32)], axis=1)
            piece = piece * weights[b]
            band = piece if band is None else band + piece
        stitched_ref[t] = band
        stitched.append(band[:, : 2 * STRIDE])

    near = jnp.concatenate(stitched, axis=0)
    wide = 2 * STRIDE
    col = lax.broadcasted_iota(jnp.int32, (wide, wide), 0)
    corner = lax.broadcasted_iota(jnp.int32, (wide, wide), 1)
    box = ((col > corner) & (col <= corner + STRIDE) & (corner < STRIDE)).astype(F32)
    square = jnp.dot(near, box, preferred_element_type=F32, precision=lax.Precision.HIGHEST)
    at = lax.broadcasted_iota(jnp.int32, near.shape, 1)
    contact = jnp.where((at >= 1) & (at <= STRIDE), jnp.exp(near), 0.0)
    down = jnp.sum(contact, axis=1, keepdims=True)
    here = lax.broadcasted_iota(jnp.int32, (height, wide), 0)
    there = lax.broadcasted_iota(jnp.int32, (height, wide), 1)

    def by_row(values):
        rows = []
        for t in range(targets):
            own = pltpu.roll(
                values[t * height : (t + 1) * height], 0, 1, stride=1, stride_axis=0
            )
            rows.append(jnp.sum(own, axis=0, keepdims=True))
        return rows

    down_rows = []
    for t in range(targets):
        own = jnp.where(here == there, down[t * height : (t + 1) * height], 0.0)
        down_rows.append(jnp.sum(own, axis=0, keepdims=True))
    parts = jnp.concatenate(by_row(square) + by_row(contact) + down_rows, axis=0)
    keep_ref[...] = parts[:, :height]
    for k, ref in enumerate(send_refs):
        ref[...] = parts[: 2 * targets, (k + 1) * height : (k + 2) * height]


def per_device(
    genome_bases,
    stitch_weight,
    stem_weight,
    trunk_in,
    trunk_out,
    pair_weight,
    distance_rate,
    tower_conv,
    tower_mix,
    head_weight,
):
    towers = lax.axis_size("tower")
    height = STRIDE // towers
    tower_index = lax.axis_index("tower")
    genome_index = lax.axis_index("genome")
    own = stem(genome_bases, stem_weight)
    features = [
        own if d == 0 else from_behind(own, "genome", -d) for d in range(1 - BLOCKS, BLOCKS)
    ]
    groups = (3, 4)
    channels = distance_rate.shape[0]
    targets = head_weight.shape[0]
    conv_a = banded(tower_conv[0], groups[0])
    conv_b = banded(tower_conv[1], groups[1])
    mix_a = block_diagonal(tower_mix[0], groups[0])
    mix_b = block_diagonal(tower_mix[1], groups[1])
    head = head_by_row(head_weight, height)
    row_weight = lax.dynamic_slice_in_dim(
        stitch_weight.reshape(BLOCKS, STRIDE), tower_index * height, height, axis=1
    )
    row_weight = jnp.where(jnp.arange(BLOCKS)[:, None] <= genome_index, row_weight, 0)
    row_weight = jnp.broadcast_to(row_weight.astype(F32)[:, :, None], (BLOCKS, height, LANES))
    place = tower_index.astype(jnp.int32).reshape(1)
    lanes = segments(2)[2]
    steps = STRIDE // height
    vmem = pl.BlockSpec(memory_space=pltpu.VMEM)
    small = jax.ShapeDtypeStruct((2 * targets, height), F32)
    stitched, keep, *sends = pl.pallas_call(
        functools.partial(main_kernel, height, groups),
        out_shape=[
            jax.ShapeDtypeStruct((targets, height, BINS), F32),
            jax.ShapeDtypeStruct((3 * targets, height), F32),
        ]
        + [small] * steps,
        in_specs=[pl.BlockSpec(memory_space=pltpu.SMEM)] + [vmem] * (2 * BLOCKS - 1 + 10),
        out_specs=[vmem] * (2 + steps),
        scratch_shapes=[
            pltpu.VMEM(((height + 4) * 3 * channels, lanes), BF16),
            pltpu.VMEM(((height + 2) * 3 * channels, lanes), BF16),
            pltpu.VMEM((height * channels, lanes), F32),
            pltpu.VMEM((height * channels, lanes), BF16),
        ],
        compiler_params=pltpu.CompilerParams(vmem_limit_bytes=VMEM_BYTES),
        name="windows",
    )(
        place,
        *features,
        trunk_in,
        trunk_out,
        pair_weight,
        distance_rate.reshape(channels, 1),
        conv_a,
        conv_b,
        mix_a,
        mix_b,
        head,
        row_weight,
    )
    sums = keep[: 2 * targets]
    for k in range(steps):
        sums = sums + from_behind(sends[k], ("genome", "tower"), k + 1)
    row = (genome_index * towers + tower_index) * height + jnp.arange(height)
    missing = jnp.maximum(STRIDE - row, 0).astype(F32)
    upstream = sums[targets:] + missing[None]
    downstream = keep[2 * targets :]
    insulation = sums[:targets] / (STRIDE * STRIDE)
    direction = (downstream - upstream) / (downstream + upstream)
    return (stitched, jnp.stack([insulation, direction]))


def solution(mesh):
    placed = (P("genome"), P(), P(), P(), P(), P(), P(), P(), P(), P())
    return jax.shard_map(
        per_device,
        mesh=mesh,
        in_specs=placed,
        out_specs=(P(None, ("genome", "tower"), None), P(None, None, ("genome", "tower"))),
        check_vma=False,
    )
```

time: 88.9 us -> 57.1 us (0.64)
  matrix products: 24.6 us -> 0 us
  local copies, waits for them, and re-layouts: 17.8 us -> 4.05 us
  Pallas kernels: 0 us -> 11.5 us
  other arithmetic: 6.48 us -> 0.89 us
  waiting for transfers between devices: 6.54 us -> 7.85 us
    dot_general x17 -> x0, matrix products: 24.6 us -> none  [the longest x1 8.36 us: per_device(): jnp.einsum('oc,ckrj->okrj', tower_mix[layer_index], squeezed, preferred_e...]
    pallas_call x0 -> x2, Pallas kernels: none -> 11.5 us  [the longest x1 9.74 us: per_device(): pl.pallas_call(functools.partial(main_kernel, height, groups), out_shape=...]
    slice x11 -> x0, local copies, waits for them, and re-layouts: 9.67 us -> none  [the longest x2 9.42 us: conv_rows(): padded[:, :, row_tap:row_tap + height, col_tap:col_tap + extent]]
    eq x5 -> x0, local copies, waits for them, and re-layouts: 5.25 us -> none  [stem_features(): letters[:, :, None] == jnp.arange(4, dtype=jnp.int32)[None, None, :]]
    convert_element_type x10 -> x2, other arithmetic: 4.19 us -> 0.09 us  [the longest x1 0.08 us: per_device(): row_weight.astype(F32)[:, :, None]]
    unnamed x24 -> x22, local copies, waits for them, and re-layouts: 0.85 us -> 3.24 us
    another operation x1 -> x0, other arithmetic: 1.55 us -> none  [per_device(): jnp.cumsum(extended, axis=2)]
    ppermute x10, waiting for transfers between devices: 6.54 us -> 7.85 us  [from_behind(): return lax.ppermute(block, axis, route)]
  transfers between devices with their start and end apart: 10 -> 10, of which waited for: 5 -> 3; matrix products, arithmetic and copies ran while one was open for 2% -> 3% of each run, Pallas kernels for 0% -> 0%
where the time goes in v1:
time: 57.1 us; the launch traced here: 56 us
  starting transfers between devices  30.7 us (54%)
  Pallas kernels  11.5 us (20%)
  waiting for transfers between devices  7.85 us (14%)
  local copies, waits for them, and re-layouts  4.05 us (7%)
  between operations  0.99 us (2%)
  other arithmetic  0.89 us (2%)
    ppermute x10, starting transfers between devices, from_behind(): return lax.ppermute(block, axis, route)  30.7 us
    pallas_call x1, Pallas kernels, per_device(): pl.pallas_call(functools.partial(main_kernel, height, groups), out_shape=...  9.74 us
    ppermute x10, waiting for transfers between devices, from_behind(): return lax.ppermute(block, axis, route)  7.85 us
    unnamed x22, local copies, waits for them, and re-layouts  3.24 us
    pallas_call x1, Pallas kernels, stem(): pl.pallas_call(functools.partial(stem_kernel, bins), out_shape=jax.ShapeD...  1.8 us
  transfers between devices with their start and end apart: 10, of which 3 were waited for; matrix products, arithmetic and copies ran while one was open for 3% of the time, Pallas kernels for 0%

profile of v1, /device:TPU:0, one launch (start us, length us, event | category | flops | bytes accessed | tf_op | source)
XLA Modules:
  0.0 56.0 jit_solution(12577563788997832998)
XLA Ops:
  0.6 0.0 copy-start
  0.6 1.4 %copy-done = bf16[96,8192]{1,0:T(8,128)(2,1)S(1)} copy-done((bf16[96,8192]{1,0:T(8,128)(2,1)S(1)}, bf16[96,8192]{1,0:T(8,128)(2,1)}, u32[]{:S(2)}) %copy-start) | copy-done | bytes 1572888
  2.0 0.0 copy-start.1
  2.0 1.0 %copy-done.1 = s32[131072]{0:T(1024)S(1)} copy-done((s32[131072]{0:T(1024)S(1)}, s32[131072]{0:T(1024)}, u32[]{:S(2)}) %copy-start.1) | copy-done | bytes 524312
  3.1 0.0 copy-start.5
  3.1 0.0 copy-start.8
  3.1 0.0 copy-start.7
  3.1 1.8 %stem.1.refs_3_ = bf16[96,64]{1,0:T(8,128)(2,1)S(1)} custom-call(s32[1024,128]{1,0:T(8,128)S(1)} %bitcast.25, bf16[96,8192]{1,0:T(8,128)(2,1)S(1)} %copy-done), custom_call_target="tpu_custom_call" | custom-call | tf_op jit(solution)/shard_map/stem/pallas_call | solution.py:69
  4.9 0.0 copy-start.4
  4.9 0.0 copy-start.6
  4.9 0.0 copy-start.9
  4.9 0.0 copy-start.2
  4.9 0.0 copy-start.3
  5.0 6.0 %collective-permute-start = (bf16[96,64]{1,0:T(8,128)(2,1)S(1)}, bf16[96,64]{1,0:T(8,128)(2,1)S(1)}, u32[]{:S(2)}, u32[]{:S(2)}) collective-permute-start(bf16[96,64]{1,0:T(8,128)(2,1)S(1)} %stem.1.refs_3_), channel_id=1, source_target_pairs={{0,12},{4,16},{8,20},{12,24},{16,28},{1,13},{5,17},{9,21},{13,25},... | collective-permute-start | bytes 36872 | tf_op jit(solution)/shard_map/ppermute | solution.py:23
  11.0 3.5 %collective-permute-start.1 = (bf16[96,64]{1,0:T(8,128)(2,1)S(1)}, bf16[96,64]{1,0:T(8,128)(2,1)S(1)}, u32[]{:S(2)}, u32[]{:S(2)}) collective-permute-start(bf16[96,64]{1,0:T(8,128)(2,1)S(1)} %stem.1.refs_3_), channel_id=1, source_target_pairs={{0,8},{4,12},{8,16},{12,20},{16,24},{20,28},{1,9},{5,13},{9,17},{1... | collective-permute-start | bytes 36872 | tf_op jit(solution)/shard_map/ppermute | solution.py:23
  14.5 3.4 %collective-permute-start.2 = (bf16[96,64]{1,0:T(8,128)(2,1)S(1)}, bf16[96,64]{1,0:T(8,128)(2,1)S(1)}, u32[]{:S(2)}, u32[]{:S(2)}) collective-permute-start(bf16[96,64]{1,0:T(8,128)(2,1)S(1)} %stem.1.refs_3_), channel_id=1, source_target_pairs={{0,4},{4,8},{8,12},{12,16},{16,20},{20,24},{24,28},{1,5},{5,9},{9,... | collective-permute-start | bytes 36872 | tf_op jit(solution)/shard_map/ppermute | solution.py:23
  17.9 1.3 %collective-permute-start.3 = (bf16[96,64]{1,0:T(8,128)(2,1)S(1)}, bf16[96,64]{1,0:T(8,128)(2,1)S(1)}, u32[]{:S(2)}, u32[]{:S(2)}) collective-permute-start(bf16[96,64]{1,0:T(8,128)(2,1)S(1)} %stem.1.refs_3_), channel_id=1, source_target_pairs={{4,0},{8,4},{12,8},{16,12},{20,16},{24,20},{28,24},{5,1},{9,5},{13... | collective-permute-start | bytes 36872 | tf_op jit(solution)/shard_map/ppermute | solution.py:23
  19.2 1.3 %collective-permute-start.4 = (bf16[96,64]{1,0:T(8,128)(2,1)S(1)}, bf16[96,64]{1,0:T(8,128)(2,1)S(1)}, u32[]{:S(2)}, u32[]{:S(2)}) collective-permute-start(bf16[96,64]{1,0:T(8,128)(2,1)S(1)} %stem.1.refs_3_), channel_id=1, source_target_pairs={{8,0},{12,4},{16,8},{20,12},{24,16},{28,20},{9,1},{13,5},{17,9},{2... | collective-permute-start | bytes 36872 | tf_op jit(solution)/shard_map/ppermute | solution.py:23
  20.5 0.0 copy-done.5
  20.6 0.1 concatenate.56
  20.7 0.1 concatenate.57
  20.9 0.1 concatenate.52
  21.0 0.1 maximum_maximum_fusion.1.refs_11_
  21.1 0.0 copy-done.8
  21.1 0.1 reshape.48
  21.2 0.0 copy-done.7
  21.2 0.1 maximum_maximum_fusion.refs_12_
  21.4 0.1 select_convert_fusion
  21.5 0.2 fusion.1.refs_14_
  21.7 0.2 fusion.2.refs_13_
  21.9 0.0 collective-permute-done.refs_0_
  21.9 1.3 %collective-permute-start.5 = (bf16[96,64]{1,0:T(8,128)(2,1)S(1)}, bf16[96,64]{1,0:T(8,128)(2,1)S(1)}, u32[]{:S(2)}, u32[]{:S(2)}) collective-permute-start(bf16[96,64]{1,0:T(8,128)(2,1)S(1)} %stem.1.refs_3_), channel_id=1, source_target_pairs={{12,0},{16,4},{20,8},{24,12},{28,16},{13,1},{17,5},{21,9},{25,13},... | collective-permute-start | bytes 36872 | tf_op jit(solution)/shard_map/ppermute | solution.py:23
  23.2 0.0 copy-done.4
  23.2 0.1 concatenate.64
  23.3 0.1 iota.82
  23.4 0.0 copy-done.6
  23.4 0.1 copy.12.refs_8_
  23.5 0.0 copy-done.9
  23.5 0.1 copy.13.refs_10_
  23.6 0.1 fusion.refs_15_
  23.7 0.0 collective-permute-done.1.refs_1_
  23.7 0.0 collective-permute-done.2.refs_2_
  23.7 0.0 collective-permute-done.3.refs_4_
  23.8 2.8 %collective-permute-done.4.refs_5_ = bf16[96,64]{1,0:T(8,128)(2,1)S(1)} collective-permute-done((bf16[96,64]{1,0:T(8,128)(2,1)S(1)}, bf16[96,64]{1,0:T(8,128)(2,1)S(1)}, u32[]{:S(2)}, u32[]{:S(2)}) %collective-permute-start.4) | collective-permute-done | bytes 12320 | tf_op jit(solution)/shard_map/ppermute | solution.py:23
  26.5 3.8 %collective-permute-done.5.refs_6_ = bf16[96,64]{1,0:T(8,128)(2,1)S(1)} collective-permute-done((bf16[96,64]{1,0:T(8,128)(2,1)S(1)}, bf16[96,64]{1,0:T(8,128)(2,1)S(1)}, u32[]{:S(2)}, u32[]{:S(2)}) %collective-permute-start.5) | collective-permute-done | bytes 12320 | tf_op jit(solution)/shard_map/ppermute | solution.py:23
  30.3 0.1 broadcast_in_dim.47.refs_16_
  30.4 0.0 copy-done.2
  30.4 0.0 copy-done.3
  30.4 9.7 %windows.1 = (f32[5,16,256]{2,1,0:T(8,128)}, f32[15,16]{1,0:T(8,128)S(1)}, f32[10,16]{1,0:T(8,128)S(1)}, f32[10,16]{1,0:T(8,128)S(1)}, f32[10,16]{1,0:T(8,128)S(1)}, /*index=5*/f32[10,16]{1,0:T(8,128)S(1)}) custom-call(s32[1]{0:T(128)} %bitcast.place_ref, bf16[96,64]{1,0:T(8,128)(2,1)S(1)} %collective-permute-done.refs_0_, ...), custom_call_target="tpu_custom_call" | custom-call | tf_op jit(solution)/shard_map/windows/pallas_call | solution.py:366
  40.1 1.3 %collective-permute-start.6 = (f32[10,16]{1,0:T(8,128)S(1)}, f32[10,16]{1,0:T(8,128)S(1)}, u32[]{:S(2)}, u32[]{:S(2)}) collective-permute-start(f32[10,16]{1,0:T(8,128)S(1)} %get-tuple-element.10), channel_id=1, source_target_pairs={{0,1},{1,2},{2,3},{3,4},{4,5},{5,6},{6,7},{7,8},{8,9},{9,10},{10,1... | collective-permute-start | bytes 1928 | tf_op jit(solution)/shard_map/ppermute | solution.py:23
  41.4 4.0 %collective-permute-start.7 = (f32[10,16]{1,0:T(8,128)S(1)}, f32[10,16]{1,0:T(8,128)S(1)}, u32[]{:S(2)}, u32[]{:S(2)}) collective-permute-start(f32[10,16]{1,0:T(8,128)S(1)} %get-tuple-element.11), channel_id=1, source_target_pairs={{0,2},{1,3},{2,4},{3,5},{4,6},{5,7},{6,8},{7,9},{8,10},{9,11},{10,... | collective-permute-start | bytes 1928 | tf_op jit(solution)/shard_map/ppermute | solution.py:23
  45.4 5.2 %collective-permute-start.8 = (f32[10,16]{1,0:T(8,128)S(1)}, f32[10,16]{1,0:T(8,128)S(1)}, u32[]{:S(2)}, u32[]{:S(2)}) collective-permute-start(f32[10,16]{1,0:T(8,128)S(1)} %get-tuple-element.12), channel_id=1, source_target_pairs={{0,3},{1,4},{2,5},{3,6},{4,7},{5,8},{6,9},{7,10},{8,11},{9,12},{10... | collective-permute-start | bytes 1928 | tf_op jit(solution)/shard_map/ppermute | solution.py:23
  50.7 3.4 %collective-permute-start.9 = (f32[10,16]{1,0:T(8,128)S(1)}, f32[10,16]{1,0:T(8,128)S(1)}, u32[]{:S(2)}, u32[]{:S(2)}) collective-permute-start(f32[10,16]{1,0:T(8,128)S(1)} %get-tuple-element.13), channel_id=1, source_target_pairs={{0,4},{1,5},{2,6},{3,7},{4,8},{5,9},{6,10},{7,11},{8,12},{9,13},{1... | collective-permute-start | bytes 1928 | tf_op jit(solution)/shard_map/ppermute | solution.py:23
  54.1 0.0 collective-permute-done.6
  54.1 0.0 collective-permute-done.7
  54.1 0.0 collective-permute-done.8
  54.1 1.3 %collective-permute-done.9 = f32[10,16]{1,0:T(8,128)S(1)} collective-permute-done((f32[10,16]{1,0:T(8,128)S(1)}, f32[10,16]{1,0:T(8,128)S(1)}, u32[]{:S(2)}, u32[]{:S(2)}) %collective-permute-start.9) | collective-permute-done | bytes 672 | tf_op jit(solution)/shard_map/ppermute | solution.py:23
  55.4 0.6 %copy.14 = f32[2,5,16]{2,0,1:T(2,128)} copy(f32[2,5,16]{2,1,0:T(8,128)S(1)} %pad_maximum_fusion) | data formatting | bytes 1280
  (17 shorter events, 0.1 us)
Async XLA Ops:
  0.6 1.4 %copy-start = (bf16[96,8192]{1,0:T(8,128)(2,1)S(1)}, bf16[96,8192]{1,0:T(8,128)(2,1)}, u32[]{:S(2)}) copy-start(bf16[96,8192]{1,0:T(8,128)(2,1)} %weight_hbm.1) | copy-start | bytes 4718596
  2.0 1.0 %copy-start.1 = (s32[131072]{0:T(1024)S(1)}, s32[131072]{0:T(1024)}, u32[]{:S(2)}) copy-start(s32[131072]{0:T(1024)} %param.10) | copy-start | bytes 1572868
  3.1 17.4 %copy-start.5 = (bf16[2,3,48,144]{3,2,1,0:T(8,128)(2,1)S(1)}, bf16[2,3,48,144]{3,2,1,0:T(8,128)(2,1)}, u32[]{:S(2)}) copy-start(bf16[2,3,48,144]{3,2,1,0:T(8,128)(2,1)} %param.17) | copy-start | bytes 248836
  3.1 18.0 %copy-start.8 = (s32[256]{0:T(256)S(1)}, s32[256]{0:T(256)}, u32[]{:S(2)}) copy-start(s32[256]{0:T(256)} %param.11) | copy-start | bytes 3076
  3.1 18.1 %copy-start.7 = (bf16[2,48,48]{2,1,0:T(8,128)(2,1)S(1)}, bf16[2,48,48]{2,1,0:T(8,128)(2,1)}, u32[]{:S(2)}) copy-start(bf16[2,48,48]{2,1,0:T(8,128)(2,1)} %param.18) | copy-start | bytes 27652
  4.9 18.3 %copy-start.4 = (bf16[5,48]{1,0:T(8,128)(2,1)S(1)}, bf16[5,48]{1,0:T(8,128)(2,1)}, u32[]{:S(2)}) copy-start(bf16[5,48]{1,0:T(8,128)(2,1)} %param.19) | copy-start | bytes 1444
  4.9 18.5 %copy-start.6 = (bf16[6,96,48]{1,2,0:T(8,128)(2,1)S(1)}, bf16[6,96,48]{1,2,0:T(8,128)(2,1)}, u32[]{:S(2)}) copy-start(bf16[6,96,48]{1,2,0:T(8,128)(2,1)} %param.14) | copy-start | bytes 165892
  4.9 18.6 %copy-start.9 = (f32[48]{0:T(128)S(1)}, f32[48]{0:T(128)}, u32[]{:S(2)}) copy-start(f32[48]{0:T(128)} %param.16) | copy-start | bytes 580
  4.9 25.4 %copy-start.2 = (bf16[6,48,288]{2,1,0:T(8,128)(2,1)S(1)}, bf16[6,48,288]{2,1,0:T(8,128)(2,1)}, u32[]{:S(2)}) copy-start(bf16[6,48,288]{2,1,0:T(8,128)(2,1)} %refs_7_.1) | copy-start | bytes 497668
  4.9 25.4 %copy-start.3 = (bf16[96,96]{1,0:T(8,128)(2,1)S(1)}, bf16[96,96]{1,0:T(8,128)(2,1)}, u32[]{:S(2)}) copy-start(bf16[96,96]{1,0:T(8,128)(2,1)} %refs_9_.1) | copy-start | bytes 55300
  5.0 16.9 %collective-permute-start = (bf16[96,64]{1,0:T(8,128)(2,1)S(1)}, bf16[96,64]{1,0:T(8,128)(2,1)S(1)}, u32[]{:S(2)}, u32[]{:S(2)}) collective-permute-start(bf16[96,64]{1,0:T(8,128)(2,1)S(1)} %stem.1.refs_3_), channel_id=1, source_target_pairs={{0,12},{4,16},{8,20},{12,24},{16,28},{1,13},{5,17},{9,21},{13,25},... | collective-permute-start | bytes 36872 | tf_op jit(solution)/shard_map/ppermute | solution.py:23
  11.0 12.7 %collective-permute-start.1 = (bf16[96,64]{1,0:T(8,128)(2,1)S(1)}, bf16[96,64]{1,0:T(8,128)(2,1)S(1)}, u32[]{:S(2)}, u32[]{:S(2)}) collective-permute-start(bf16[96,64]{1,0:T(8,128)(2,1)S(1)} %stem.1.refs_3_), channel_id=1, source_target_pairs={{0,8},{4,12},{8,16},{12,20},{16,24},{20,28},{1,9},{5,13},{9,17},{1... | collective-permute-start | bytes 36872 | tf_op jit(solution)/shard_map/ppermute | solution.py:23
  14.5 9.3 %collective-permute-start.2 = (bf16[96,64]{1,0:T(8,128)(2,1)S(1)}, bf16[96,64]{1,0:T(8,128)(2,1)S(1)}, u32[]{:S(2)}, u32[]{:S(2)}) collective-permute-start(bf16[96,64]{1,0:T(8,128)(2,1)S(1)} %stem.1.refs_3_), channel_id=1, source_target_pairs={{0,4},{4,8},{8,12},{12,16},{16,20},{20,24},{24,28},{1,5},{5,9},{9,... | collective-permute-start | bytes 36872 | tf_op jit(solution)/shard_map/ppermute | solution.py:23
  17.9 5.9 %collective-permute-start.3 = (bf16[96,64]{1,0:T(8,128)(2,1)S(1)}, bf16[96,64]{1,0:T(8,128)(2,1)S(1)}, u32[]{:S(2)}, u32[]{:S(2)}) collective-permute-start(bf16[96,64]{1,0:T(8,128)(2,1)S(1)} %stem.1.refs_3_), channel_id=1, source_target_pairs={{4,0},{8,4},{12,8},{16,12},{20,16},{24,20},{28,24},{5,1},{9,5},{13... | collective-permute-start | bytes 36872 | tf_op jit(solution)/shard_map/ppermute | solution.py:23
  19.2 7.3 %collective-permute-start.4 = (bf16[96,64]{1,0:T(8,128)(2,1)S(1)}, bf16[96,64]{1,0:T(8,128)(2,1)S(1)}, u32[]{:S(2)}, u32[]{:S(2)}) collective-permute-start(bf16[96,64]{1,0:T(8,128)(2,1)S(1)} %stem.1.refs_3_), channel_id=1, source_target_pairs={{8,0},{12,4},{16,8},{20,12},{24,16},{28,20},{9,1},{13,5},{17,9},{2... | collective-permute-start | bytes 36872 | tf_op jit(solution)/shard_map/ppermute | solution.py:23
  21.9 8.4 %collective-permute-start.5 = (bf16[96,64]{1,0:T(8,128)(2,1)S(1)}, bf16[96,64]{1,0:T(8,128)(2,1)S(1)}, u32[]{:S(2)}, u32[]{:S(2)}) collective-permute-start(bf16[96,64]{1,0:T(8,128)(2,1)S(1)} %stem.1.refs_3_), channel_id=1, source_target_pairs={{12,0},{16,4},{20,8},{24,12},{28,16},{13,1},{17,5},{21,9},{25,13},... | collective-permute-start | bytes 36872 | tf_op jit(solution)/shard_map/ppermute | solution.py:23
  40.1 14.0 %collective-permute-start.6 = (f32[10,16]{1,0:T(8,128)S(1)}, f32[10,16]{1,0:T(8,128)S(1)}, u32[]{:S(2)}, u32[]{:S(2)}) collective-permute-start(f32[10,16]{1,0:T(8,128)S(1)} %get-tuple-element.10), channel_id=1, source_target_pairs={{0,1},{1,2},{2,3},{3,4},{4,5},{5,6},{6,7},{7,8},{8,9},{9,10},{10,1... | collective-permute-start | bytes 1928 | tf_op jit(solution)/shard_map/ppermute | solution.py:23
  41.4 12.7 %collective-permute-start.7 = (f32[10,16]{1,0:T(8,128)S(1)}, f32[10,16]{1,0:T(8,128)S(1)}, u32[]{:S(2)}, u32[]{:S(2)}) collective-permute-start(f32[10,16]{1,0:T(8,128)S(1)} %get-tuple-element.11), channel_id=1, source_target_pairs={{0,2},{1,3},{2,4},{3,5},{4,6},{5,7},{6,8},{7,9},{8,10},{9,11},{10,... | collective-permute-start | bytes 1928 | tf_op jit(solution)/shard_map/ppermute | solution.py:23
  45.4 8.7 %collective-permute-start.8 = (f32[10,16]{1,0:T(8,128)S(1)}, f32[10,16]{1,0:T(8,128)S(1)}, u32[]{:S(2)}, u32[]{:S(2)}) collective-permute-start(f32[10,16]{1,0:T(8,128)S(1)} %get-tuple-element.12), channel_id=1, source_target_pairs={{0,3},{1,4},{2,5},{3,6},{4,7},{5,8},{6,9},{7,10},{8,11},{9,12},{10... | collective-permute-start | bytes 1928 | tf_op jit(solution)/shard_map/ppermute | solution.py:23
  50.7 4.7 %collective-permute-start.9 = (f32[10,16]{1,0:T(8,128)S(1)}, f32[10,16]{1,0:T(8,128)S(1)}, u32[]{:S(2)}, u32[]{:S(2)}) collective-permute-start(f32[10,16]{1,0:T(8,128)S(1)} %get-tuple-element.13), channel_id=1, source_target_pairs={{0,4},{1,5},{2,6},{3,7},{4,8},{5,9},{6,10},{7,11},{8,12},{9,13},{1... | collective-permute-start | bytes 1928 | tf_op jit(solution)/shard_map/ppermute | solution.py:23

commit v2 on v1

--- a/solution.py
+++ b/solution.py
@@ -15,12 +15,6 @@
 F32 = jnp.float32
 BF16 = jnp.bfloat16
 VMEM_BYTES = 48 * 1024 * 1024
-
-
-def from_behind(block, axis, distance):
-    devices = range(lax.axis_size(axis))
-    route = [(i - distance, i) for i in devices if i - distance in devices]
-    return lax.ppermute(block, axis, route)
 
 
 def dot(a, b):
@@ -59,7 +53,9 @@
             weight[k], hot, (((1,), (1,)), ((), ())), preferred_element_type=F32
         )
         total = part if total is None else total + part
-    out_ref[...] = total.astype(BF16)
+    total = total.astype(BF16)
+    half = out_ref.shape[0]
+    out_ref[...] = jnp.concatenate([total[:half], total[half:]], axis=1)
 
 
 def stem(genome_bases, stem_weight):
@@ -68,8 +64,8 @@
     chunks = 4
     return pl.pallas_call(
         functools.partial(stem_kernel, bins),
-        out_shape=jax.ShapeDtypeStruct((channels, bins), BF16),
-        in_specs=[pl.BlockSpec(memory_space=pl.ANY)] * 2,
+        out_shape=jax.ShapeDtypeStruct((channels // 2, 2 * bins), BF16),
+        in_specs=[pl.BlockSpec(memory_space=pltpu.HBM)] * 2,
         out_specs=pl.BlockSpec(memory_space=pltpu.VMEM),
         scratch_shapes=[
             pltpu.VMEM((genome_bases.shape[0] // LANES, LANES), jnp.int32),
@@ -77,7 +73,7 @@
             pltpu.SemaphoreType.DMA,
             pltpu.SemaphoreType.DMA((chunks,)),
         ],
-        compiler_params=pltpu.CompilerParams(vmem_limit_bytes=VMEM_BYTES),
+        compiler_params=pltpu.CompilerParams(vmem_limit_bytes=63 * 1024 * 1024),
         name="stem",
     )(genome_bases.reshape(-1, LANES), stem_weight)
 
@@ -136,8 +132,8 @@
     place_ref,
     *refs,
 ):
-    feature_refs = refs[: 2 * BLOCKS - 1]
     (
+        features,
         trunk_in,
         trunk_out,
         pair_weight,
@@ -150,17 +146,31 @@
         row_weight,
         stitched_ref,
         keep_ref,
-        *rest,
-    ) = refs[2 * BLOCKS - 1 :]
-    send_refs = rest[: STRIDE // height]
-    taps_a, taps_b, grid_ref, final_ref = rest[STRIDE // height :]
+        send_ref,
+        taps_a,
+        taps_b,
+        grid_ref,
+        final_ref,
+    ) = refs
     margin = 2
     sizes, offsets, lanes = segments(margin)
     tower_row = place_ref[0] * height
     channels = rate_ref.shape[0]
     depth = 3 * channels
 
-    blocks = jnp.concatenate([r[...] for r in feature_refs], axis=1)
+    starts = features.shape[0]
+    blocks = []
+    for d in range(1 - BLOCKS, BLOCKS):
+        at = place_ref[1] + d
+        block = features[jnp.clip(at, 0, starts - 1)]
+        blocks.append(jnp.where((at >= 0) & (at < starts), block, jnp.zeros_like(block)))
+    blocks = jnp.concatenate(
+        [
+            jnp.concatenate([half[:, :STRIDE] for half in blocks], axis=1),
+            jnp.concatenate([half[:, STRIDE:] for half in blocks], axis=1),
+        ],
+        axis=0,
+    )
     extent = BINS
     windows = []
     for b in range(BLOCKS):
@@ -319,10 +329,51 @@
     for t in range(targets):
         own = jnp.where(here == there, down[t * height : (t + 1) * height], 0.0)
         down_rows.append(jnp.sum(own, axis=0, keepdims=True))
-    parts = jnp.concatenate(by_row(square) + by_row(contact) + down_rows, axis=0)
-    keep_ref[...] = parts[:, :height]
-    for k, ref in enumerate(send_refs):
-        ref[...] = parts[: 2 * targets, (k + 1) * height : (k + 2) * height]
+    rows = by_row(square) + by_row(contact)
+    keep_ref[...] = jnp.concatenate(rows + down_rows, axis=0)
+    send_ref[...] = jnp.zeros_like(send_ref)
+    per_row = LANES // height
+    slots = send_ref.shape[0]
+    own = place_ref[1] * (STRIDE // height) + place_ref[0]
+    first = lax.broadcasted_iota(jnp.int32, (per_row, LANES), 1) < height
+    packs = [
+        jnp.concatenate(
+            rows[p : p + per_row]
+            + [jnp.zeros((1, LANES), F32)] * (per_row - len(rows[p : p + per_row])),
+            axis=0,
+        )
+        for p in range(0, len(rows), per_row)
+    ]
+    for k in range(1, STRIDE // height + 1):
+        packed = []
+        for pack in packs:
+            turned = jnp.where(first, pltpu.roll(pack, LANES - k * height, 1), 0.0)
+            turned = pltpu.roll(turned, 0, 1, stride=height, stride_axis=0)
+            packed.append(jnp.sum(turned, axis=0, keepdims=True))
+
+        @pl.when(own + k < slots)
+        def _():
+            send_ref[own + k] = jnp.concatenate(packed, axis=0)
+
+
+def finish_kernel(height, place_ref, keep_ref, got_ref, out_ref):
+    targets = out_ref.shape[0]
+    per_row = LANES // height
+    keep = keep_ref[...][:, :height]
+    got = jnp.sum(got_ref[...], axis=0)
+    rows = []
+    for q in range(2 * targets):
+        at = (q % per_row) * height
+        rows.append(got[q // per_row : q // per_row + 1, at : at + height])
+    sums = keep[: 2 * targets] + jnp.concatenate(rows, axis=0)
+    own = place_ref[1] * (STRIDE // height) + place_ref[0]
+    row = own * height + lax.broadcasted_iota(jnp.int32, (targets, height), 1)
+    upstream = sums[targets:] + jnp.maximum(STRIDE - row, 0).astype(F32)
+    downstream = keep[2 * targets :]
+    insulation = sums[:targets] / (STRIDE * STRIDE)
+    direction = (downstream - upstream) / (downstream + upstream)
+    for t in range(targets):
+        out_ref[t] = jnp.concatenate([insulation[t : t + 1], direction[t : t + 1]], axis=0)
 
 
 def per_device(
@@ -342,9 +393,7 @@
     tower_index = lax.axis_index("tower")
     genome_index = lax.axis_index("genome")
     own = stem(genome_bases, stem_weight)
-    features = [
-        own if d == 0 else from_behind(own, "genome", -d) for d in range(1 - BLOCKS, BLOCKS)
-    ]
+    features = lax.all_gather(own, "genome")
     groups = (3, 4)
     channels = distance_rate.shape[0]
     targets = head_weight.shape[0]
@@ -358,20 +407,21 @@
     )
     row_weight = jnp.where(jnp.arange(BLOCKS)[:, None] <= genome_index, row_weight, 0)
     row_weight = jnp.broadcast_to(row_weight.astype(F32)[:, :, None], (BLOCKS, height, LANES))
-    place = tower_index.astype(jnp.int32).reshape(1)
+    place = jnp.stack([tower_index, genome_index]).astype(jnp.int32)
     lanes = segments(2)[2]
-    steps = STRIDE // height
+    slots = lax.axis_size("genome") * towers
+    packs = -(-2 * targets * height // LANES)
     vmem = pl.BlockSpec(memory_space=pltpu.VMEM)
-    small = jax.ShapeDtypeStruct((2 * targets, height), F32)
-    stitched, keep, *sends = pl.pallas_call(
+    smem = pl.BlockSpec(memory_space=pltpu.SMEM)
+    stitched, keep, send = pl.pallas_call(
         functools.partial(main_kernel, height, groups),
         out_shape=[
             jax.ShapeDtypeStruct((targets, height, BINS), F32),
-            jax.ShapeDtypeStruct((3 * targets, height), F32),
-        ]
-        + [small] * steps,
-        in_specs=[pl.BlockSpec(memory_space=pltpu.SMEM)] + [vmem] * (2 * BLOCKS - 1 + 10),
-        out_specs=[vmem] * (2 + steps),
+            jax.ShapeDtypeStruct((3 * targets, LANES), F32),
+            jax.ShapeDtypeStruct((slots, packs, LANES), F32),
+        ],
+        in_specs=[smem] + [vmem] * 11,
+        out_specs=[vmem] * 3,
         scratch_shapes=[
             pltpu.VMEM(((height + 4) * 3 * channels, lanes), BF16),
             pltpu.VMEM(((height + 2) * 3 * channels, lanes), BF16),
@@ -382,7 +432,7 @@
         name="windows",
     )(
         place,
-        *features,
+        features,
         trunk_in,
         trunk_out,
         pair_weight,
@@ -394,16 +444,15 @@
         head,
         row_weight,
     )
-    sums = keep[: 2 * targets]
-    for k in range(steps):
-        sums = sums + from_behind(sends[k], ("genome", "tower"), k + 1)
-    row = (genome_index * towers + tower_index) * height + jnp.arange(height)
-    missing = jnp.maximum(STRIDE - row, 0).astype(F32)
-    upstream = sums[targets:] + missing[None]
-    downstream = keep[2 * targets :]
-    insulation = sums[:targets] / (STRIDE * STRIDE)
-    direction = (downstream - upstream) / (downstream + upstream)
-    return (stitched, jnp.stack([insulation, direction]))
+    got = lax.all_to_all(send, ("genome", "tower"), 0, 0, tiled=True)
+    scores = pl.pallas_call(
+        functools.partial(finish_kernel, height),
+        out_shape=jax.ShapeDtypeStruct((targets, 2, height), F32),
+        in_specs=[smem, vmem, vmem],
+        out_specs=vmem,
+        name="finish",
+    )(place, keep, got)
+    return (stitched, jnp.transpose(scores, (1, 0, 2)))
 
 
 def solution(mesh):

time: 57.1 us -> 68.2 us (1.19)
  blocking collectives: 0 us -> 45.2 us
  starting transfers between devices: 30.7 us -> 0 us
  waiting for transfers between devices: 7.85 us -> 0 us
  Pallas kernels: 11.5 us -> 16.4 us
    all_gather x0 -> x1, blocking collectives: none -> 32.5 us  [per_device(): features = lax.all_gather(own, 'genome')]
    ppermute x10 -> x0, starting transfers between devices: 30.7 us -> none  [from_behind(): return lax.ppermute(block, axis, route)]
    all_to_all x0 -> x1, blocking collectives: none -> 12.7 us  [per_device(): got = lax.all_to_all(send, ('genome', 'tower'), 0, 0, tiled=True)]
    ppermute x10 -> x0, waiting for transfers between devices: 7.85 us -> none  [from_behind(): return lax.ppermute(block, axis, route)]
    unnamed x22 -> x13, local copies, waits for them, and re-layouts: 3.24 us -> 0.18 us
    pallas_call x1, Pallas kernels: 1.8 us -> 3.75 us  [stem(): pl.pallas_call(functools.partial(stem_kernel, bins), out_shape=jax.ShapeD...]
    pallas_call x0 -> x1, Pallas kernels: none -> 1.5 us  [per_device(): pl.pallas_call(functools.partial(finish_kernel, height), out_shape=jax.Sh...]
    pallas_call x1, Pallas kernels: 9.74 us -> 11.1 us  [per_device(): pl.pallas_call(functools.partial(main_kernel, height, groups), out_shape=...]
  transfers between devices with their start and end apart: 10 -> 0, of which waited for: 3 -> 0; matrix products, arithmetic and copies ran while one was open for 3% -> 0% of each run, Pallas kernels for 0% -> 0%
where the time goes in v2:
time: 68.2 us; the launch traced here: 67.8 us
  blocking collectives  45.2 us (66%)
  Pallas kernels  16.4 us (24%)
  local copies, waits for them, and re-layouts  4.49 us (7%)
  other arithmetic  0.93 us (1%)
  between operations  0.8 us (1%)
    all_gather x1, blocking collectives, per_device(): features = lax.all_gather(own, 'genome')  32.5 us
    all_to_all x1, blocking collectives, per_device(): got = lax.all_to_all(send, ('genome', 'tower'), 0, 0, tiled=True)  12.7 us
    pallas_call x1, Pallas kernels, per_device(): pl.pallas_call(functools.partial(main_kernel, height, groups), out_shape=...  11.1 us
    pallas_call x1, Pallas kernels, stem(): pl.pallas_call(functools.partial(stem_kernel, bins), out_shape=jax.ShapeD...  3.75 us
    pallas_call x1, Pallas kernels, per_device(): pl.pallas_call(functools.partial(finish_kernel, height), out_shape=jax.Sh...  1.5 us

profile of v2, /device:TPU:0, one launch (start us, length us, event | category | flops | bytes accessed | tf_op | source)
XLA Modules:
  0.0 67.8 jit_solution(373959310850046607)
XLA Ops:
  0.6 0.0 copy-start.4
  0.6 0.9 %slice_bitcast_fusion.2 = (bf16[48,144]{1,0:T(8,128)(2,1)S(1)}, bf16[48,144]{1,0:T(8,128)(2,1)S(1)}, bf16[48,144]{1,0:T(8,128)(2,1)S(1)}, bf16[48,144]{1,0:T(8,1...) fusion(bf16[2,3,48,144]{3,2,1,0:T(8,128)(2,1)} %param.17), kind=kLoop, calls=%fused_computation.10 | loop fusion | bytes 165888 | tf_op jit(solution)/shard_map/squeeze | solution.py:83
  1.5 0.1 concatenate.56
  1.7 0.1 concatenate.57
  1.9 0.0 copy-start.5
  1.9 0.1 concatenate.52
  2.0 0.1 maximum_maximum_fusion.1.refs_5_
  2.2 0.8 %reshape.37 = s32[4,64]{1,0:T(4,128)S(1)} reshape(s32[256]{0:T(256)} %param.11) | data formatting | bytes 2048 | tf_op jit(solution)/shard_map/reshape | solution.py:406
  2.9 0.7 %slice_bitcast_fusion.6 = (bf16[48,48]{1,0:T(8,128)(2,1)S(1)}, bf16[48,48]{1,0:T(8,128)(2,1)S(1)}) fusion(bf16[2,48,48]{2,1,0:T(8,128)(2,1)} %param.18), kind=kLoop, calls=%fused_computation.14 | loop fusion | bytes 18432 | tf_op jit(solution)/shard_map/squeeze | solution.py:403
  3.6 1.3 %concatenate.64 = bf16[5,768]{1,0:T(8,128)(2,1)S(1)} concatenate(bf16[5,48]{1,0:T(8,128)(2,1)} %param.19, bf16[5,48]{1,0:T(8,128)(2,1)} %param.19, bf16[5,48]{1,0:T(8,128)(2,1)} %param.19, bf16[5,48]{1,0:T(8,128)(2,1)} %param.19, bf16[5,48]{1,0:T(8,128)(2,1)} %param.19, bf16[5,48]{1,0:T(8,128)(2,1)} %param.19, bf16[5,48]{1,0:T(8,128)(2,1)} %param.19, bf16[5,48]{1,0:T(8,128)(2,1)} %param.19, ...), dimensions={1} | concatenate | bytes 15360 | tf_op jit(solution)/shard_map/concatenate | solution.py:105
  5.0 0.1 iota.77
  5.1 0.0 copy-done.4
  5.1 0.1 copy.12.refs_2_
  5.2 0.0 copy-start
  5.2 0.0 copy-start.1
  5.3 3.8 %stem.1 = bf16[48,128]{1,0:T(8,128)(2,1)} custom-call(s32[1024,128]{1,0:T(8,128)} %bitcast.25, bf16[96,8192]{1,0:T(8,128)(2,1)} %weight_hbm.1), custom_call_target="tpu_custom_call" | custom-call | tf_op jit(solution)/shard_map/stem/pallas_call | solution.py:65
  9.0 32.5 %all-gather = bf16[384,128]{1,0:T(8,128)(2,1)S(1)} all-gather(bf16[48,128]{1,0:T(8,128)(2,1)} %stem.1), channel_id=2, replica_groups=mesh['genome'=8,'tower'=4] {'genome'}, dimensions={0}, use_global_device_ids=true | all-gather | bytes 110592 | tf_op jit(solution)/shard_map/all_gather | solution.py:396
  41.6 0.0 copy-done.5
  41.6 0.1 copy.13.refs_4_
  41.7 0.1 pad_add_fusion.place_ref
  41.7 0.0 copy-start.3
  41.7 0.1 maximum_maximum_fusion.refs_6_
  41.9 0.1 select_convert_fusion
  42.0 0.2 fusion.1.refs_8_
  42.2 0.2 fusion.2.refs_7_
  42.3 0.1 fusion.refs_9_
  42.4 0.1 broadcast_in_dim.46.refs_10_
  42.5 0.0 copy-done
  42.5 0.0 copy-done.1
  42.5 11.1 %windows.1 = (f32[5,16,256]{2,1,0:T(8,128)}, f32[15,128]{1,0:T(8,128)S(1)}, f32[32,2,128]{2,1,0:T(2,128)S(1)}) custom-call(s32[2]{0:T(128)S(1)} %pad_add_fusion.place_ref, bf16[8,48,128]{2,1,0:T(8,128)(2,1)S(1)} %bitcast.24, bf16[6,48,288]{2,1,0:T(8,128)(2,1)S(1)} %copy-done, bf16[6,96,48]{2,1,0:T(8,128)(2,1)S(1)} %copy.12.refs_2_, ...), custom_call_target="tpu_custom_call" | custom-call | tf_op jit(solution)/shard_map/windows/pallas_call | solution.py:416
  53.6 0.0 copy-start.2
  53.6 12.7 %all_to_all.5.got_ref = f32[32,2,128]{2,1,0:T(2,128)} all-to-all(f32[32,2,128]{2,1,0:T(2,128)S(1)} %get-tuple-element.7), channel_id=1, replica_groups=mesh['genome'=8,'tower'=4] {'genome','tower'}, dimensions={0} | all-to-all | bytes 65536 | tf_op jit(solution)/shard_map/all_to_all | solution.py:447
  66.3 0.0 copy-done.2
  66.3 0.0 copy-done.3
  66.3 1.5 %finish.1 = f32[5,2,16]{2,1,0:T(2,128)} custom-call(s32[2]{0:T(128)} %copy-done.3, f32[15,128]{1,0:T(8,128)} %copy-done.2, f32[32,2,128]{2,1,0:T(2,128)} %all_to_all.5.got_ref), custom_call_target="tpu_custom_call" | custom-call | tf_op jit(solution)/shard_map/finish/pallas_call | solution.py:448
  (11 shorter events, 0.1 us)
Async XLA Ops:
  0.6 4.4 %copy-start.4 = (bf16[6,96,48]{1,2,0:T(8,128)(2,1)S(1)}, bf16[6,96,48]{1,2,0:T(8,128)(2,1)}, u32[]{:S(2)}) copy-start(bf16[6,96,48]{1,2,0:T(8,128)(2,1)} %param.14) | copy-start | bytes 165892
  1.9 39.7 %copy-start.5 = (f32[48]{0:T(128)S(1)}, f32[48]{0:T(128)}, u32[]{:S(2)}) copy-start(f32[48]{0:T(128)} %param.16) | copy-start | bytes 580
  5.2 37.3 %copy-start = (bf16[6,48,288]{2,1,0:T(8,128)(2,1)S(1)}, bf16[6,48,288]{2,1,0:T(8,128)(2,1)}, u32[]{:S(2)}) copy-start(bf16[6,48,288]{2,1,0:T(8,128)(2,1)} %refs_1_.1) | copy-start | bytes 497668
  5.2 37.3 %copy-start.1 = (bf16[96,96]{1,0:T(8,128)(2,1)S(1)}, bf16[96,96]{1,0:T(8,128)(2,1)}, u32[]{:S(2)}) copy-start(bf16[96,96]{1,0:T(8,128)(2,1)} %refs_3_.1) | copy-start | bytes 55300
  41.7 24.5 %copy-start.3 = (s32[2]{0:T(128)}, s32[2]{0:T(128)S(1)}, u32[]{:S(2)}) copy-start(s32[2]{0:T(128)S(1)} %pad_add_fusion.place_ref) | copy-start | bytes 28
  53.6 12.7 %copy-start.2 = (f32[15,128]{1,0:T(8,128)}, f32[15,128]{1,0:T(8,128)S(1)}, u32[]{:S(2)}) copy-start(f32[15,128]{1,0:T(8,128)S(1)} %get-tuple-element.6.keep_ref) | copy-start | bytes 23044

commit v3 on v2

--- a/solution.py
+++ b/solution.py
@@ -54,17 +54,19 @@
         )
         total = part if total is None else total + part
     total = total.astype(BF16)
-    half = out_ref.shape[0]
-    out_ref[...] = jnp.concatenate([total[:half], total[half:]], axis=1)
-
-
-def stem(genome_bases, stem_weight):
+    half = out_ref.shape[1]
+    packed = jnp.concatenate([total[:half], total[half:]], axis=1)
+    for slot in range(out_ref.shape[0]):
+        out_ref[slot] = packed
+
+
+def stem(genome_bases, stem_weight, slots):
     bins = genome_bases.shape[0] // BP
     channels, depth = stem_weight.shape
     chunks = 4
     return pl.pallas_call(
         functools.partial(stem_kernel, bins),
-        out_shape=jax.ShapeDtypeStruct((channels // 2, 2 * bins), BF16),
+        out_shape=jax.ShapeDtypeStruct((slots, channels // 2, 2 * bins), BF16),
         in_specs=[pl.BlockSpec(memory_space=pltpu.HBM)] * 2,
         out_specs=pl.BlockSpec(memory_space=pltpu.VMEM),
         scratch_shapes=[
@@ -138,12 +140,10 @@
         trunk_out,
         pair_weight,
         rate_ref,
-        conv_a,
-        conv_b,
-        mix_a,
-        mix_b,
-        head,
-        row_weight,
+        conv_ref,
+        mix_ref,
+        head_ref,
+        stitch_ref,
         stitched_ref,
         keep_ref,
         send_ref,
@@ -155,8 +155,13 @@
     margin = 2
     sizes, offsets, lanes = segments(margin)
     tower_row = place_ref[0] * height
-    channels = rate_ref.shape[0]
+    channels = rate_ref.shape[1]
     depth = 3 * channels
+    conv_a = banded(conv_ref[0], groups[0])
+    conv_b = banded(conv_ref[1], groups[1])
+    mix_a = block_diagonal(mix_ref[0], groups[0])
+    mix_b = block_diagonal(mix_ref[1], groups[1])
+    head = head_by_row(head_ref[...], height)
 
     starts = features.shape[0]
     blocks = []
@@ -191,7 +196,9 @@
         )
         inner = dot(trunk_in[layer], stacked)
         squeezed = jax.nn.relu(inner).astype(BF16)
-        stream = stream + dot(trunk_out[layer], squeezed)
+        stream = stream + lax.dot_general(
+            trunk_out[layer], squeezed, (((0,), (0,)), ((), ())), preferred_element_type=F32
+        )
     projected = dot(pair_weight[...], jax.nn.relu(stream).astype(BF16))
 
     lane = lax.broadcasted_iota(jnp.int32, (1, lanes), 1)
@@ -221,7 +228,10 @@
     if lanes > used:
         right.append(jnp.zeros((channels, lanes - used), F32))
     right = jnp.concatenate(right, axis=1)
-    rate = jnp.broadcast_to(rate_ref[...], (channels, LANES))
+    row = lax.broadcasted_iota(jnp.int32, (channels, channels), 0)
+    col = lax.broadcasted_iota(jnp.int32, (channels, channels), 1)
+    rate = jnp.sum(jnp.where(row == col, rate_ref[...], 0.0), axis=1, keepdims=True)
+    rate = jnp.broadcast_to(rate, (channels, LANES))
     rate = jnp.concatenate([rate] * (lanes // LANES), axis=1)
 
     def place_taps(ref, slot, act):
@@ -255,8 +265,8 @@
     span = groups[0]
     for group in range((height + 2) // span):
         first = group * span
-        conv = dot(conv_a[...], taps_a[pl.ds(first * depth, (span + 2) * depth), :])
-        update = dot(mix_a[...], jnp.maximum(conv, 0.0).astype(BF16))
+        conv = dot(conv_a, taps_a[pl.ds(first * depth, (span + 2) * depth), :])
+        update = dot(mix_a, jnp.maximum(conv, 0.0).astype(BF16))
         for r in range(span):
             row = first + r
             kept = taps_a[pl.ds((row + 1) * depth + channels, channels), :].astype(F32)
@@ -267,19 +277,21 @@
     span = groups[1]
     for group in range(height // span):
         first = group * span
-        conv = dot(conv_b[...], taps_b[pl.ds(first * depth, (span + 2) * depth), :])
-        update = dot(mix_b[...], jnp.maximum(conv, 0.0).astype(BF16))
+        conv = dot(conv_b, taps_b[pl.ds(first * depth, (span + 2) * depth), :])
+        update = dot(mix_b, jnp.maximum(conv, 0.0).astype(BF16))
         rows = pl.ds(first * channels, span * channels)
         final_ref[rows, :] = jnp.maximum(grid_ref[rows, :] + update, 0.0).astype(BF16)
     targets = head.shape[0] // height
-    contact = dot(head[...], final_ref[...]).reshape(targets, height, lanes)
+    contact = dot(head, final_ref[...]).reshape(targets, height, lanes)
 
     local = lax.broadcasted_iota(jnp.int32, (height, BINS), 0)
     ahead = lax.broadcasted_iota(jnp.int32, (height, BINS), 1)
     weight_sum = jnp.zeros((height, BINS), F32)
     weights = []
     for b in range(BLOCKS):
-        weight = jnp.concatenate([row_weight[b]] * (BINS // LANES), axis=1)
+        weight = jnp.where(ahead == STRIDE * b + tower_row + local, stitch_ref[...], 0)
+        weight = jnp.sum(weight.astype(F32), axis=1, keepdims=True)
+        weight = jnp.where(place_ref[1] >= b, weight, 0.0)
         reach = STRIDE * b + tower_row + local + ahead < BINS
         weight = jnp.where(reach, weight, 0.0)
         weights.append(weight)
@@ -331,10 +343,7 @@
         down_rows.append(jnp.sum(own, axis=0, keepdims=True))
     rows = by_row(square) + by_row(contact)
     keep_ref[...] = jnp.concatenate(rows + down_rows, axis=0)
-    send_ref[...] = jnp.zeros_like(send_ref)
     per_row = LANES // height
-    slots = send_ref.shape[0]
-    own = place_ref[1] * (STRIDE // height) + place_ref[0]
     first = lax.broadcasted_iota(jnp.int32, (per_row, LANES), 1) < height
     packs = [
         jnp.concatenate(
@@ -351,16 +360,14 @@
             turned = pltpu.roll(turned, 0, 1, stride=height, stride_axis=0)
             packed.append(jnp.sum(turned, axis=0, keepdims=True))
 
-        @pl.when(own + k < slots)
-        def _():
-            send_ref[own + k] = jnp.concatenate(packed, axis=0)
-
-
-def finish_kernel(height, place_ref, keep_ref, got_ref, out_ref):
+        send_ref[lax.rem(place_ref[0] + k, STRIDE // height)] = jnp.concatenate(packed, axis=0)
+
+
+def finish_kernel(height, place_ref, keep_ref, near_ref, far_ref, out_ref):
     targets = out_ref.shape[0]
     per_row = LANES // height
     keep = keep_ref[...][:, :height]
-    got = jnp.sum(got_ref[...], axis=0)
+    got = near_ref[...] + far_ref[...]
     rows = []
     for q in range(2 * targets):
         at = (q % per_row) * height
@@ -392,24 +399,13 @@
     height = STRIDE // towers
     tower_index = lax.axis_index("tower")
     genome_index = lax.axis_index("genome")
-    own = stem(genome_bases, stem_weight)
-    features = lax.all_gather(own, "genome")
+    own = stem(genome_bases, stem_weight, lax.axis_size("genome"))
+    features = lax.all_to_all(own, "genome", 0, 0, tiled=True)
     groups = (3, 4)
     channels = distance_rate.shape[0]
     targets = head_weight.shape[0]
-    conv_a = banded(tower_conv[0], groups[0])
-    conv_b = banded(tower_conv[1], groups[1])
-    mix_a = block_diagonal(tower_mix[0], groups[0])
-    mix_b = block_diagonal(tower_mix[1], groups[1])
-    head = head_by_row(head_weight, height)
-    row_weight = lax.dynamic_slice_in_dim(
-        stitch_weight.reshape(BLOCKS, STRIDE), tower_index * height, height, axis=1
-    )
-    row_weight = jnp.where(jnp.arange(BLOCKS)[:, None] <= genome_index, row_weight, 0)
-    row_weight = jnp.broadcast_to(row_weight.astype(F32)[:, :, None], (BLOCKS, height, LANES))
     place = jnp.stack([tower_index, genome_index]).astype(jnp.int32)
     lanes = segments(2)[2]
-    slots = lax.axis_size("genome") * towers
     packs = -(-2 * targets * height // LANES)
     vmem = pl.BlockSpec(memory_space=pltpu.VMEM)
     smem = pl.BlockSpec(memory_space=pltpu.SMEM)
@@ -418,9 +414,9 @@
         out_shape=[
             jax.ShapeDtypeStruct((targets, height, BINS), F32),
             jax.ShapeDtypeStruct((3 * targets, LANES), F32),
-            jax.ShapeDtypeStruct((slots, packs, LANES), F32),
+            jax.ShapeDtypeStruct((towers, packs, LANES), F32),
         ],
-        in_specs=[smem] + [vmem] * 11,
+        in_specs=[smem] + [vmem] * 9,
         out_specs=[vmem] * 3,
         scratch_shapes=[
             pltpu.VMEM(((height + 4) * 3 * channels, lanes), BF16),
@@ -434,24 +430,27 @@
         place,
         features,
         trunk_in,
-        trunk_out,
+        jnp.transpose(trunk_out, (0, 2, 1)),
         pair_weight,
-        distance_rate.reshape(channels, 1),
-        conv_a,
-        conv_b,
-        mix_a,
-        mix_b,
-        head,
-        row_weight,
+        distance_rate.reshape(1, channels),
+        tower_conv,
+        tower_mix,
+        head_weight,
+        stitch_weight.reshape(1, BINS),
     )
-    got = lax.all_to_all(send, ("genome", "tower"), 0, 0, tiled=True)
+    got = lax.all_to_all(send, "tower", 0, 0, tiled=True)
+    before = (jnp.arange(towers) < tower_index)[:, None, None]
+    near = jnp.sum(jnp.where(before, got, 0.0), axis=0)
+    far = jnp.sum(jnp.where(before, 0.0, got), axis=0)
+    starts = lax.axis_size("genome")
+    far = lax.ppermute(far, "genome", [(i, i + 1) for i in range(starts - 1)])
     scores = pl.pallas_call(
         functools.partial(finish_kernel, height),
         out_shape=jax.ShapeDtypeStruct((targets, 2, height), F32),
-        in_specs=[smem, vmem, vmem],
+        in_specs=[smem, vmem, vmem, vmem],
         out_specs=vmem,
         name="finish",
-    )(place, keep, got)
+    )(place, keep, near, far)
     return (stitched, jnp.transpose(scores, (1, 0, 2)))
 
 

time: 68.2 us -> 43.7 us (0.64)
  blocking collectives: 45.2 us -> 0 us
  starting transfers between devices: 0 us -> 12.7 us
  waiting for transfers between devices: 0 us -> 12.1 us
  local copies, waits for them, and re-layouts: 4.49 us -> 1.17 us
    all_gather x1 -> x0, blocking collectives: 32.5 us -> none  [per_device(): features = lax.all_gather(own, 'genome')]
    all_to_all x1 -> x0, blocking collectives: 12.7 us -> none  [per_device(): got = lax.all_to_all(send, ('genome', 'tower'), 0, 0, tiled=True)]
    all_to_all x0 -> x2, waiting for transfers between devices: none -> 10.8 us  [the longest x1 7.05 us: per_device(): features = lax.all_to_all(own, 'genome', 0, 0, tiled=True)]
    all_to_all x0 -> x2, starting transfers between devices: none -> 10.5 us  [the longest x1 7.3 us: per_device(): features = lax.all_to_all(own, 'genome', 0, 0, tiled=True)]
    ppermute x0 -> x1, starting transfers between devices: none -> 2.19 us  [per_device(): far = lax.ppermute(far, 'genome', [(i, i + 1) for i in range(starts - 1)])]
    concatenate x4 -> x0, local copies, waits for them, and re-layouts: 1.69 us -> none  [the longest x1 1.34 us: head_by_row(): wide = jnp.concatenate([head] * count, axis=1)]
    squeeze x2 -> x0, local copies, waits for them, and re-layouts: 1.59 us -> none  [the longest x1 0.87 us: banded(): flat = jnp.concatenate([kernel[u] for u in range(taps)], axis=1)]
    ppermute x0 -> x1, waiting for transfers between devices: none -> 1.28 us  [per_device(): far = lax.ppermute(far, 'genome', [(i, i + 1) for i in range(starts - 1)])]
  transfers between devices with their start and end apart: 0 -> 3, of which waited for: 0 -> 3; matrix products, arithmetic and copies ran while one was open for 0% -> 0% of each run, Pallas kernels for 0% -> 0%
where the time goes in v3:
time: 43.7 us; the launch traced here: 43.3 us
  Pallas kernels  15.9 us (36%)
  starting transfers between devices  12.7 us (29%)
  waiting for transfers between devices  12.1 us (28%)
  local copies, waits for them, and re-layouts  1.17 us (3%)
  between operations  0.78 us (2%)
  other arithmetic  0.7 us (2%)
    pallas_call x1, Pallas kernels, per_device(): pl.pallas_call(functools.partial(main_kernel, height, groups), out_shape=...  10.5 us
    all_to_all x1, starting transfers between devices, per_device(): features = lax.all_to_all(own, 'genome', 0, 0, tiled=True)  7.3 us
    all_to_all x1, waiting for transfers between devices, per_device(): features = lax.all_to_all(own, 'genome', 0, 0, tiled=True)  7.05 us
    pallas_call x1, Pallas kernels, stem(): pl.pallas_call(functools.partial(stem_kernel, bins), out_shape=jax.ShapeD...  3.86 us
    all_to_all x1, waiting for transfers between devices, per_device(): got = lax.all_to_all(send, 'tower', 0, 0, tiled=True)  3.74 us
    all_to_all x1, starting transfers between devices, per_device(): got = lax.all_to_all(send, 'tower', 0, 0, tiled=True)  3.25 us
    ppermute x1, starting transfers between devices, per_device(): far = lax.ppermute(far, 'genome', [(i, i + 1) for i in range(starts - 1)])  2.19 us
    pallas_call x1, Pallas kernels, per_device(): pl.pallas_call(functools.partial(finish_kernel, height), out_shape=jax.Sh...  1.48 us
  transfers between devices with their start and end apart: 3, of which 3 were waited for; matrix products, arithmetic and copies ran while one was open for 0% of the time, Pallas kernels for 0%

profile of v3, /device:TPU:0, one launch (start us, length us, event | category | flops | bytes accessed | tf_op | source)
XLA Modules:
  0.0 43.3 jit_solution(6385901564336401098)
XLA Ops:
  0.6 0.0 copy-start.6
  0.6 0.0 copy-start.4
  0.7 0.0 copy-start.1
  0.7 0.0 copy-start.9
  0.7 0.0 copy-start.3
  0.7 0.0 copy-start.2
  0.7 0.0 copy-start
  0.7 0.0 copy-start.8
  0.7 3.9 %stem.1 = bf16[8,48,128]{2,1,0:T(8,128)(2,1)} custom-call(s32[1024,128]{1,0:T(8,128)} %bitcast.10, bf16[96,8192]{1,0:T(8,128)(2,1)} %weight_hbm.1), custom_call_target="tpu_custom_call" | custom-call | tf_op jit(solution)/shard_map/stem/pallas_call | solution.py:67
  4.6 7.3 %all-to-all-start = ((bf16[8,48,128]{2,1,0:T(8,128)(2,1)}), bf16[8,48,128]{2,1,0:T(8,128)(2,1)S(1)}, u32[]{:S(2)}, u32[]{:S(2)}) async-start(bf16[8,48,128]{2,1,0:T(8,128)(2,1)} %stem.1), calls=%async_computation | async-start | bytes 196608 | tf_op jit(solution)/shard_map/all_to_all | solution.py:403
  11.9 0.1 pad_add_fusion.place_ref
  12.0 0.0 copy-start.7
  12.0 7.0 %all-to-all-done.refs_0_ = bf16[8,48,128]{2,1,0:T(8,128)(2,1)S(1)} async-done(((bf16[8,48,128]{2,1,0:T(8,128)(2,1)}), bf16[8,48,128]{2,1,0:T(8,128)(2,1)S(1)}, u32[]{:S(2)}, u32[]{:S(2)}) %all-to-all-start) | async-done | bytes 98336 | tf_op jit(solution)/shard_map/all_to_all | solution.py:403
  19.0 0.0 copy-done.6
  19.0 0.0 copy-done.4
  19.0 0.0 copy-done.1
  19.0 0.0 copy-done.9
  19.0 0.0 copy-done.3
  19.0 0.0 copy-done.2
  19.0 0.0 copy-done
  19.1 0.0 copy-done.8
  19.1 10.5 %windows.1 = (f32[5,16,256]{2,1,0:T(8,128)}, f32[15,128]{1,0:T(8,128)S(1)}, f32[4,2,128]{2,1,0:T(2,128)}) custom-call(s32[2]{0:T(128)S(1)} %pad_add_fusion.place_ref, bf16[8,48,128]{2,1,0:T(8,128)(2,1)S(1)} %all-to-all-done.refs_0_, bf16[6,48,288]{2,1,0:T(8,128)(2,1)S(1)} %copy-done, bf16[6,48,96]{2,1,0:T(8,128)(2,1)S(1)} %bitcast.7, ...), custom_call_target="tpu_custom_call" | custom-call | tf_op jit(solution)/shard_map/windows/pallas_call | solution.py:412
  29.6 0.0 copy-start.5
  29.6 0.6 %copy-done.5 = f32[15,128]{1,0:T(8,128)} copy-done((f32[15,128]{1,0:T(8,128)}, f32[15,128]{1,0:T(8,128)S(1)}, u32[]{:S(2)}) %copy-start.5) | copy-done | bytes 7704
  30.2 3.2 %all-to-all-start.1 = ((f32[4,2,128]{2,1,0:T(2,128)}), f32[4,2,128]{2,1,0:T(2,128)S(1)}, u32[]{:S(2)}, u32[]{:S(2)}) async-start(f32[4,2,128]{2,1,0:T(2,128)} %get-tuple-element.7), calls=%async_computation.1 | async-start | bytes 8192 | tf_op jit(solution)/shard_map/all_to_all | solution.py:441
  33.5 3.7 %all-to-all-done.1 = f32[4,2,128]{2,1,0:T(2,128)S(1)} async-done(((f32[4,2,128]{2,1,0:T(2,128)}), f32[4,2,128]{2,1,0:T(2,128)S(1)}, u32[]{:S(2)}, u32[]{:S(2)}) %all-to-all-start.1) | async-done | bytes 4128 | tf_op jit(solution)/shard_map/all_to_all | solution.py:441
  37.2 0.6 %select_reduce_fusion = (f32[2,128]{1,0:T(2,128)S(1)}, f32[2,128]{1,0:T(2,128)}) fusion(f32[4,2,128]{2,1,0:T(2,128)S(1)} %all-to-all-done.1, pred[4]{0:T(512)(128)(4,1)S(1)} %iota_compare_fusion), kind=kLoop, calls=%fused_computation | loop fusion | flops 3584 | bytes 6148 | tf_op jit(solution)/shard_map/reduce_sum | solution.py:444
  37.8 2.2 %collective-permute-start = (f32[2,128]{1,0:T(2,128)S(1)}, f32[2,128]{1,0:T(2,128)S(1)}, u32[]{:S(2)}, u32[]{:S(2)}) collective-permute-start(f32[2,128]{1,0:T(2,128)S(1)} %get-tuple-element.8), channel_id=1, source_target_pairs={{0,4},{4,8},{8,12},{12,16},{16,20},{20,24},{24,28},{1,5},{5,9},{9,... | collective-permute-start | bytes 3080 | tf_op jit(solution)/shard_map/ppermute | solution.py:446
  40.0 1.3 %collective-permute-done.far_ref = f32[2,128]{1,0:T(2,128)S(1)} collective-permute-done((f32[2,128]{1,0:T(2,128)S(1)}, f32[2,128]{1,0:T(2,128)S(1)}, u32[]{:S(2)}, u32[]{:S(2)}) %collective-permute-start) | collective-permute-done | bytes 1056 | tf_op jit(solution)/shard_map/ppermute | solution.py:446
  41.3 0.0 copy-start.10
  41.3 0.0 copy-done.7
  41.3 0.5 %copy-done.10 = f32[2,128]{1,0:T(2,128)} copy-done((f32[2,128]{1,0:T(2,128)}, f32[2,128]{1,0:T(2,128)S(1)}, u32[]{:S(2)}) %copy-start.10) | copy-done | bytes 1048
  41.8 1.5 %finish.1 = f32[5,2,16]{2,1,0:T(2,128)} custom-call(s32[2]{0:T(128)} %copy-done.7, f32[15,128]{1,0:T(8,128)} %copy-done.5, f32[2,128]{1,0:T(2,128)} %get-tuple-element.9.near_ref, f32[2,128]{1,0:T(2,128)} %copy-done.10), custom_call_target="tpu_custom_call" | custom-call | tf_op jit(solution)/shard_map/finish/pallas_call | solution.py:447
  (1 shorter events, 0.0 us)
Async XLA Ops:
  0.6 18.4 %copy-start.6 = (bf16[5,48]{1,0:T(8,128)(2,1)S(1)}, bf16[5,48]{1,0:T(8,128)(2,1)}, u32[]{:S(2)}) copy-start(bf16[5,48]{1,0:T(8,128)(2,1)} %refs_7_.1) | copy-start | bytes 1444
  0.6 18.4 %copy-start.4 = (bf16[2,48,48]{2,1,0:T(8,128)(2,1)S(1)}, bf16[2,48,48]{2,1,0:T(8,128)(2,1)}, u32[]{:S(2)}) copy-start(bf16[2,48,48]{2,1,0:T(8,128)(2,1)} %refs_6_.1) | copy-start | bytes 27652
  0.7 18.4 %copy-start.1 = (bf16[2,3,48,144]{3,2,1,0:T(8,128)(2,1)S(1)}, bf16[2,3,48,144]{3,2,1,0:T(8,128)(2,1)}, u32[]{:S(2)}) copy-start(bf16[2,3,48,144]{3,2,1,0:T(8,128)(2,1)} %refs_5_.1) | copy-start | bytes 248836
  0.7 18.4 %copy-start.9 = (f32[48]{0:T(128)S(1)}, f32[48]{0:T(128)}, u32[]{:S(2)}) copy-start(f32[48]{0:T(128)} %param.16) | copy-start | bytes 580
  0.7 18.4 %copy-start.3 = (bf16[96,96]{1,0:T(8,128)(2,1)S(1)}, bf16[96,96]{1,0:T(8,128)(2,1)}, u32[]{:S(2)}) copy-start(bf16[96,96]{1,0:T(8,128)(2,1)} %refs_3_.1) | copy-start | bytes 55300
  0.7 18.4 %copy-start.2 = (bf16[6,96,48]{1,2,0:T(8,128)(2,1)S(1)}, bf16[6,96,48]{1,2,0:T(8,128)(2,1)}, u32[]{:S(2)}) copy-start(bf16[6,96,48]{1,2,0:T(8,128)(2,1)} %param.14) | copy-start | bytes 165892
  0.7 18.4 %copy-start = (bf16[6,48,288]{2,1,0:T(8,128)(2,1)S(1)}, bf16[6,48,288]{2,1,0:T(8,128)(2,1)}, u32[]{:S(2)}) copy-start(bf16[6,48,288]{2,1,0:T(8,128)(2,1)} %refs_1_.1) | copy-start | bytes 497668
  0.7 18.4 %copy-start.8 = (s32[256]{0:T(256)S(1)}, s32[256]{0:T(256)}, u32[]{:S(2)}) copy-start(s32[256]{0:T(256)} %param.11) | copy-start | bytes 3076
  4.6 14.4 %all-to-all-start = ((bf16[8,48,128]{2,1,0:T(8,128)(2,1)}), bf16[8,48,128]{2,1,0:T(8,128)(2,1)S(1)}, u32[]{:S(2)}, u32[]{:S(2)}) async-start(bf16[8,48,128]{2,1,0:T(8,128)(2,1)} %stem.1), calls=%async_computation | async-start | bytes 196608 | tf_op jit(solution)/shard_map/all_to_all | solution.py:403
  12.0 29.3 %copy-start.7 = (s32[2]{0:T(128)}, s32[2]{0:T(128)S(1)}, u32[]{:S(2)}) copy-start(s32[2]{0:T(128)S(1)} %pad_add_fusion.place_ref) | copy-start | bytes 28
  29.6 0.6 %copy-start.5 = (f32[15,128]{1,0:T(8,128)}, f32[15,128]{1,0:T(8,128)S(1)}, u32[]{:S(2)}) copy-start(f32[15,128]{1,0:T(8,128)S(1)} %get-tuple-element.6.keep_ref) | copy-start | bytes 23044
  30.2 7.0 %all-to-all-start.1 = ((f32[4,2,128]{2,1,0:T(2,128)}), f32[4,2,128]{2,1,0:T(2,128)S(1)}, u32[]{:S(2)}, u32[]{:S(2)}) async-start(f32[4,2,128]{2,1,0:T(2,128)} %get-tuple-element.7), calls=%async_computation.1 | async-start | bytes 8192 | tf_op jit(solution)/shard_map/all_to_all | solution.py:441
  37.8 3.5 %collective-permute-start = (f32[2,128]{1,0:T(2,128)S(1)}, f32[2,128]{1,0:T(2,128)S(1)}, u32[]{:S(2)}, u32[]{:S(2)}) collective-permute-start(f32[2,128]{1,0:T(2,128)S(1)} %get-tuple-element.8), channel_id=1, source_target_pairs={{0,4},{4,8},{8,12},{12,16},{16,20},{20,24},{24,28},{1,5},{5,9},{9,... | collective-permute-start | bytes 3080 | tf_op jit(solution)/shard_map/ppermute | solution.py:446
  41.3 0.5 %copy-start.10 = (f32[2,128]{1,0:T(2,128)}, f32[2,128]{1,0:T(2,128)S(1)}, u32[]{:S(2)}) copy-start(f32[2,128]{1,0:T(2,128)S(1)} %collective-permute-done.far_ref) | copy-start | bytes 3076

commit v4 on v3

--- a/solution.py
+++ b/solution.py
@@ -157,10 +157,12 @@
     tower_row = place_ref[0] * height
     channels = rate_ref.shape[1]
     depth = 3 * channels
-    conv_a = banded(conv_ref[0], groups[0])
-    conv_b = banded(conv_ref[1], groups[1])
-    mix_a = block_diagonal(mix_ref[0], groups[0])
-    mix_b = block_diagonal(mix_ref[1], groups[1])
+    spans_a = {groups, (height + 2) % groups} - {0}
+    spans_b = {groups, height % groups} - {0}
+    conv_a = {span: banded(conv_ref[0], span) for span in sorted(spans_a)}
+    conv_b = {span: banded(conv_ref[1], span) for span in sorted(spans_b)}
+    mix_a = {span: block_diagonal(mix_ref[0], span) for span in sorted(spans_a)}
+    mix_b = {span: block_diagonal(mix_ref[1], span) for span in sorted(spans_b)}
     head = head_by_row(head_ref[...], height)
 
     starts = features.shape[0]
@@ -262,11 +264,10 @@
         mixed = jnp.concatenate(tiles, axis=1) + right - rate * decay
         place_taps(taps_a, row, jnp.where(inside(row), jnp.maximum(mixed, 0.0), 0.0))
 
-    span = groups[0]
-    for group in range((height + 2) // span):
-        first = group * span
-        conv = dot(conv_a, taps_a[pl.ds(first * depth, (span + 2) * depth), :])
-        update = dot(mix_a, jnp.maximum(conv, 0.0).astype(BF16))
+    for first in range(0, height + 2, groups):
+        span = min(groups, height + 2 - first)
+        conv = dot(conv_a[span], taps_a[pl.ds(first * depth, (span + 2) * depth), :])
+        update = dot(mix_a[span], jnp.maximum(conv, 0.0).astype(BF16))
         for r in range(span):
             row = first + r
             kept = taps_a[pl.ds((row + 1) * depth + channels, channels), :].astype(F32)
@@ -274,11 +275,10 @@
             if 1 <= row <= height:
                 grid_ref[pl.ds((row - 1) * channels, channels), :] = grid
             place_taps(taps_b, row, jnp.where(inside(row + 1), jnp.maximum(grid, 0.0), 0.0))
-    span = groups[1]
-    for group in range(height // span):
-        first = group * span
-        conv = dot(conv_b, taps_b[pl.ds(first * depth, (span + 2) * depth), :])
-        update = dot(mix_b, jnp.maximum(conv, 0.0).astype(BF16))
+    for first in range(0, height, groups):
+        span = min(groups, height - first)
+        conv = dot(conv_b[span], taps_b[pl.ds(first * depth, (span + 2) * depth), :])
+        update = dot(mix_b[span], jnp.maximum(conv, 0.0).astype(BF16))
         rows = pl.ds(first * channels, span * channels)
         final_ref[rows, :] = jnp.maximum(grid_ref[rows, :] + update, 0.0).astype(BF16)
     targets = head.shape[0] // height
@@ -363,11 +363,11 @@
         send_ref[lax.rem(place_ref[0] + k, STRIDE // height)] = jnp.concatenate(packed, axis=0)
 
 
-def finish_kernel(height, place_ref, keep_ref, near_ref, far_ref, out_ref):
+def finish_kernel(height, place_ref, keep_ref, got_ref, out_ref):
     targets = out_ref.shape[0]
     per_row = LANES // height
     keep = keep_ref[...][:, :height]
-    got = near_ref[...] + far_ref[...]
+    got = jnp.sum(got_ref[...], axis=0)
     rows = []
     for q in range(2 * targets):
         at = (q % per_row) * height
@@ -401,7 +401,7 @@
     genome_index = lax.axis_index("genome")
     own = stem(genome_bases, stem_weight, lax.axis_size("genome"))
     features = lax.all_to_all(own, "genome", 0, 0, tiled=True)
-    groups = (3, 4)
+    groups = 3
     channels = distance_rate.shape[0]
     targets = head_weight.shape[0]
     place = jnp.stack([tower_index, genome_index]).astype(jnp.int32)
@@ -438,19 +438,18 @@
         head_weight,
         stitch_weight.reshape(1, BINS),
     )
-    got = lax.all_to_all(send, "tower", 0, 0, tiled=True)
-    before = (jnp.arange(towers) < tower_index)[:, None, None]
-    near = jnp.sum(jnp.where(before, got, 0.0), axis=0)
-    far = jnp.sum(jnp.where(before, 0.0, got), axis=0)
     starts = lax.axis_size("genome")
-    far = lax.ppermute(far, "genome", [(i, i + 1) for i in range(starts - 1)])
+    passed = lax.ppermute(send, "genome", [(i, i + 1) for i in range(starts - 1)])
+    ahead = (jnp.arange(towers) > tower_index)[:, None, None]
+    got = lax.all_to_all(jnp.where(ahead, send, passed), "tower", 0, 0, tiled=True)
     scores = pl.pallas_call(
         functools.partial(finish_kernel, height),
         out_shape=jax.ShapeDtypeStruct((targets, 2, height), F32),
-        in_specs=[smem, vmem, vmem, vmem],
+        in_specs=[smem, vmem, vmem],
         out_specs=vmem,
+        compiler_params=pltpu.CompilerParams(vmem_limit_bytes=2 * 1024 * 1024),
         name="finish",
-    )(place, keep, near, far)
+    )(place, keep, got)
     return (stitched, jnp.transpose(scores, (1, 0, 2)))
 
 

time: 43.7 us -> 40.7 us (0.931)
  blocking collectives: 0 us -> 6.34 us
  waiting for transfers between devices: 12.1 us -> 8.35 us
  starting transfers between devices: 12.7 us -> 9.49 us
  local copies, waits for them, and re-layouts: 1.17 us -> 0.03 us
  Pallas kernels: 15.9 us -> 15.2 us
  other arithmetic: 0.7 us -> 0.15 us
    all_to_all x0 -> x1, blocking collectives: none -> 6.34 us  [per_device(): lax.all_to_all(jnp.where(ahead, send, passed), 'tower', 0, 0, tiled=True)]
    all_to_all x1 -> x0, waiting for transfers between devices: 3.74 us -> none  [per_device(): got = lax.all_to_all(send, 'tower', 0, 0, tiled=True)]
    all_to_all x1 -> x0, starting transfers between devices: 3.25 us -> none  [per_device(): got = lax.all_to_all(send, 'tower', 0, 0, tiled=True)]
    unnamed x22 -> x16, local copies, waits for them, and re-layouts: 1.17 us -> 0.03 us
    reduce_sum x1 -> x0, other arithmetic: 0.62 us -> none  [per_device(): far = jnp.sum(jnp.where(before, 0.0, got), axis=0)]
  transfers between devices with their start and end apart: 3 -> 2, of which waited for: 3 -> 2; matrix products, arithmetic and copies ran while one was open for 0% -> 0% of each run, Pallas kernels for 0% -> 0%
where the time goes in v4:
time: 40.7 us; the launch traced here: 40.4 us
  Pallas kernels  15.2 us (37%)
  starting transfers between devices  9.49 us (23%)
  waiting for transfers between devices  8.35 us (21%)
  blocking collectives  6.34 us (16%)
  between operations  0.77 us (2%)
    pallas_call x1, Pallas kernels, per_device(): pl.pallas_call(functools.partial(main_kernel, height, groups), out_shape=...  10.1 us
    all_to_all x1, starting transfers between devices, per_device(): features = lax.all_to_all(own, 'genome', 0, 0, tiled=True)  7.3 us
    all_to_all x1, waiting for transfers between devices, per_device(): features = lax.all_to_all(own, 'genome', 0, 0, tiled=True)  7.05 us
    all_to_all x1, blocking collectives, per_device(): lax.all_to_all(jnp.where(ahead, send, passed), 'tower', 0, 0, tiled=True)  6.34 us
    pallas_call x1, Pallas kernels, stem(): pl.pallas_call(functools.partial(stem_kernel, bins), out_shape=jax.ShapeD...  3.86 us
    ppermute x1, starting transfers between devices, per_device(): lax.ppermute(send, 'genome', [(i, i + 1) for i in range(starts - 1)])  2.19 us
    ppermute x1, waiting for transfers between devices, per_device(): lax.ppermute(send, 'genome', [(i, i + 1) for i in range(starts - 1)])  1.3 us
    pallas_call x1, Pallas kernels, per_device(): pl.pallas_call(functools.partial(finish_kernel, height), out_shape=jax.Sh...  1.23 us
  transfers between devices with their start and end apart: 2, of which 2 were waited for; matrix products, arithmetic and copies ran while one was open for 0% of the time, Pallas kernels for 0%

profile of v4, /device:TPU:0, one launch (start us, length us, event | category | flops | bytes accessed | tf_op | source)
XLA Modules:
  0.0 40.4 jit_solution(10517560232248350359)
XLA Ops:
  0.6 0.0 copy-start.5
  0.6 0.0 copy-start.4
  0.7 0.0 copy-start.1
  0.7 0.0 copy-start.7
  0.7 0.0 copy-start.3
  0.7 0.0 copy-start.2
  0.7 0.0 copy-start
  0.7 0.0 copy-start.6
  0.7 3.9 %stem.1 = bf16[8,48,128]{2,1,0:T(8,128)(2,1)} custom-call(s32[1024,128]{1,0:T(8,128)} %bitcast.10, bf16[96,8192]{1,0:T(8,128)(2,1)} %weight_hbm.1), custom_call_target="tpu_custom_call" | custom-call | tf_op jit(solution)/shard_map/stem/pallas_call | solution.py:67
  4.6 7.3 %all-to-all-start = ((bf16[8,48,128]{2,1,0:T(8,128)(2,1)}), bf16[8,48,128]{2,1,0:T(8,128)(2,1)S(1)}, u32[]{:S(2)}, u32[]{:S(2)}) async-start(bf16[8,48,128]{2,1,0:T(8,128)(2,1)} %stem.1), calls=%async_computation | async-start | bytes 196608 | tf_op jit(solution)/shard_map/all_to_all | solution.py:403
  11.9 0.1 pad_add_fusion.place_ref
  12.0 7.0 %all-to-all-done.refs_0_ = bf16[8,48,128]{2,1,0:T(8,128)(2,1)S(1)} async-done(((bf16[8,48,128]{2,1,0:T(8,128)(2,1)}), bf16[8,48,128]{2,1,0:T(8,128)(2,1)S(1)}, u32[]{:S(2)}, u32[]{:S(2)}) %all-to-all-start) | async-done | bytes 98336 | tf_op jit(solution)/shard_map/all_to_all | solution.py:403
  19.0 0.0 copy-done.5
  19.0 0.0 copy-done.4
  19.0 0.0 copy-done.1
  19.0 0.0 copy-done.7
  19.0 0.0 copy-done.3
  19.0 0.0 copy-done.2
  19.0 0.0 copy-done
  19.1 0.0 copy-done.6
  19.1 10.1 %windows.1 = (f32[5,16,256]{2,1,0:T(8,128)}, f32[15,128]{1,0:T(8,128)S(1)}, f32[4,2,128]{2,1,0:T(2,128)S(1)}) custom-call(s32[2]{0:T(128)S(1)} %pad_add_fusion.place_ref, bf16[8,48,128]{2,1,0:T(8,128)(2,1)S(1)} %all-to-all-done.refs_0_, bf16[6,48,288]{2,1,0:T(8,128)(2,1)S(1)} %copy-done, bf16[6,48,96]{2,1,0:T(8,128)(2,1)S(1)} %bitcast.7, ...), custom_call_target="tpu_custom_call" | custom-call | tf_op jit(solution)/shard_map/windows/pallas_call | solution.py:412
  29.2 2.2 %collective-permute-start = (f32[4,2,128]{2,1,0:T(2,128)S(1)}, f32[4,2,128]{2,1,0:T(2,128)S(1)}, u32[]{:S(2)}, u32[]{:S(2)}) collective-permute-start(f32[4,2,128]{2,1,0:T(2,128)S(1)} %get-tuple-element.7), channel_id=1, source_target_pairs={{0,4},{4,8},{8,12},{12,16},{16,20},{20,24},{24,28},{1,5},{5,9},{9,... | collective-permute-start | bytes 12296 | tf_op jit(solution)/shard_map/ppermute | solution.py:442
  31.4 1.3 %collective-permute-done = f32[4,2,128]{2,1,0:T(2,128)S(1)} collective-permute-done((f32[4,2,128]{2,1,0:T(2,128)S(1)}, f32[4,2,128]{2,1,0:T(2,128)S(1)}, u32[]{:S(2)}, u32[]{:S(2)}) %collective-permute-start) | collective-permute-done | bytes 4128 | tf_op jit(solution)/shard_map/ppermute | solution.py:442
  32.7 0.1 broadcast_select_fusion
  32.8 6.3 %all_to_all.10.got_ref = f32[4,2,128]{2,1,0:T(2,128)S(1)} all-to-all(f32[4,2,128]{2,1,0:T(2,128)S(1)} %broadcast_select_fusion), channel_id=1, replica_groups=mesh['genome'=8,'tower'=4] {'tower'}, dimensions={0} | all-to-all | bytes 8192 | tf_op jit(solution)/shard_map/all_to_all | solution.py:444
  39.1 1.2 %finish.1 = f32[5,2,16]{2,1,0:T(2,128)} custom-call(s32[2]{0:T(128)S(1)} %pad_add_fusion.place_ref, f32[15,128]{1,0:T(8,128)S(1)} %get-tuple-element.6.keep_ref, f32[4,2,128]{2,1,0:T(2,128)S(1)} %all_to_all.10.got_ref), custom_call_target="tpu_custom_call" | custom-call | tf_op jit(solution)/shard_map/finish/pallas_call | solution.py:445
  (1 shorter events, 0.0 us)
Async XLA Ops:
  0.6 18.4 %copy-start.5 = (bf16[5,48]{1,0:T(8,128)(2,1)S(1)}, bf16[5,48]{1,0:T(8,128)(2,1)}, u32[]{:S(2)}) copy-start(bf16[5,48]{1,0:T(8,128)(2,1)} %refs_7_.1) | copy-start | bytes 1444
  0.6 18.4 %copy-start.4 = (bf16[2,48,48]{2,1,0:T(8,128)(2,1)S(1)}, bf16[2,48,48]{2,1,0:T(8,128)(2,1)}, u32[]{:S(2)}) copy-start(bf16[2,48,48]{2,1,0:T(8,128)(2,1)} %refs_6_.1) | copy-start | bytes 27652
  0.7 18.4 %copy-start.1 = (bf16[2,3,48,144]{3,2,1,0:T(8,128)(2,1)S(1)}, bf16[2,3,48,144]{3,2,1,0:T(8,128)(2,1)}, u32[]{:S(2)}) copy-start(bf16[2,3,48,144]{3,2,1,0:T(8,128)(2,1)} %refs_5_.1) | copy-start | bytes 248836
  0.7 18.4 %copy-start.7 = (f32[48]{0:T(128)S(1)}, f32[48]{0:T(128)}, u32[]{:S(2)}) copy-start(f32[48]{0:T(128)} %param.16) | copy-start | bytes 580
  0.7 18.4 %copy-start.3 = (bf16[96,96]{1,0:T(8,128)(2,1)S(1)}, bf16[96,96]{1,0:T(8,128)(2,1)}, u32[]{:S(2)}) copy-start(bf16[96,96]{1,0:T(8,128)(2,1)} %refs_3_.1) | copy-start | bytes 55300
  0.7 18.4 %copy-start.2 = (bf16[6,96,48]{1,2,0:T(8,128)(2,1)S(1)}, bf16[6,96,48]{1,2,0:T(8,128)(2,1)}, u32[]{:S(2)}) copy-start(bf16[6,96,48]{1,2,0:T(8,128)(2,1)} %param.14) | copy-start | bytes 165892
  0.7 18.4 %copy-start = (bf16[6,48,288]{2,1,0:T(8,128)(2,1)S(1)}, bf16[6,48,288]{2,1,0:T(8,128)(2,1)}, u32[]{:S(2)}) copy-start(bf16[6,48,288]{2,1,0:T(8,128)(2,1)} %refs_1_.1) | copy-start | bytes 497668
  0.7 18.4 %copy-start.6 = (s32[256]{0:T(256)S(1)}, s32[256]{0:T(256)}, u32[]{:S(2)}) copy-start(s32[256]{0:T(256)} %param.11) | copy-start | bytes 3076
  4.6 14.4 %all-to-all-start = ((bf16[8,48,128]{2,1,0:T(8,128)(2,1)}), bf16[8,48,128]{2,1,0:T(8,128)(2,1)S(1)}, u32[]{:S(2)}, u32[]{:S(2)}) async-start(bf16[8,48,128]{2,1,0:T(8,128)(2,1)} %stem.1), calls=%async_computation | async-start | bytes 196608 | tf_op jit(solution)/shard_map/all_to_all | solution.py:403
  29.2 3.5 %collective-permute-start = (f32[4,2,128]{2,1,0:T(2,128)S(1)}, f32[4,2,128]{2,1,0:T(2,128)S(1)}, u32[]{:S(2)}, u32[]{:S(2)}) collective-permute-start(f32[4,2,128]{2,1,0:T(2,128)S(1)} %get-tuple-element.7), channel_id=1, source_target_pairs={{0,4},{4,8},{8,12},{12,16},{16,20},{20,24},{24,28},{1,5},{5,9},{9,... | collective-permute-start | bytes 12296 | tf_op jit(solution)/shard_map/ppermute | solution.py:442

commit v5 on v4

--- a/solution.py
+++ b/solution.py
@@ -187,16 +187,20 @@
     layers = trunk_in.shape[0]
     for layer in range(layers):
         dilation = max(1, extent // 2 ** (layers - layer))
-        active = jax.nn.relu(stream)
-        parts = [active[:, b * BINS : (b + 1) * BINS] for b in range(BLOCKS)]
-        stacked = jnp.concatenate(
+        active = jnp.maximum(stream, 0.0).astype(BF16)
+        width = active.shape[0]
+        flat = trunk_in[layer]
+        mid = flat.shape[0]
+        tall = jnp.concatenate([flat[:, q * width : (q + 1) * width] for q in range(3)], axis=0)
+        taps = dot(tall, active)
+        inner = taps[mid : 2 * mid] + jnp.concatenate(
             [
-                jnp.concatenate([shifted(p, o) for p in parts], axis=1).astype(BF16)
-                for o in (-dilation, 0, dilation)
+                shifted(taps[:mid, b * BINS : (b + 1) * BINS], -dilation)
+                + shifted(taps[2 * mid :, b * BINS : (b + 1) * BINS], dilation)
+                for b in range(BLOCKS)
             ],
-            axis=0,
+            axis=1,
         )
-        inner = dot(trunk_in[layer], stacked)
         squeezed = jax.nn.relu(inner).astype(BF16)
         stream = stream + lax.dot_general(
             trunk_out[layer], squeezed, (((0,), (0,)), ((), ())), preferred_element_type=F32
@@ -237,11 +241,10 @@
     rate = jnp.concatenate([rate] * (lanes // LANES), axis=1)
 
     def place_taps(ref, slot, act):
-        before = pltpu.roll(act, 1, 1)
-        after = pltpu.roll(act, lanes - 1, 1)
-        ref[pl.ds(slot * depth, channels), :] = before.astype(BF16)
-        ref[pl.ds(slot * depth + channels, channels), :] = act.astype(BF16)
-        ref[pl.ds(slot * depth + 2 * channels, channels), :] = after.astype(BF16)
+        act = act.astype(BF16)
+        ref[pl.ds(slot * depth, channels), :] = pltpu.roll(act, 1, 1)
+        ref[pl.ds(slot * depth + channels, channels), :] = act
+        ref[pl.ds(slot * depth + 2 * channels, channels), :] = pltpu.roll(act, lanes - 1, 1)
 
     def inside(row):
         at = first_row + row

time: 40.7 us -> 40.1 us (0.985)
  Pallas kernels: 15.2 us -> 14.7 us
    pallas_call x1, Pallas kernels: 10.1 us -> 9.62 us  [per_device(): pl.pallas_call(functools.partial(main_kernel, height, groups), out_shape=...]
where the time goes in v5:
time: 40.1 us; the launch traced here: 39.8 us
  Pallas kernels  14.7 us (37%)
  starting transfers between devices  9.5 us (24%)
  waiting for transfers between devices  8.35 us (21%)
  blocking collectives  6.33 us (16%)
  between operations  0.77 us (2%)
    pallas_call x1, Pallas kernels, per_device(): pl.pallas_call(functools.partial(main_kernel, height, groups), out_shape=...  9.62 us
    all_to_all x1, starting transfers between devices, per_device(): features = lax.all_to_all(own, 'genome', 0, 0, tiled=True)  7.3 us
    all_to_all x1, waiting for transfers between devices, per_device(): features = lax.all_to_all(own, 'genome', 0, 0, tiled=True)  7.05 us
    all_to_all x1, blocking collectives, per_device(): lax.all_to_all(jnp.where(ahead, send, passed), 'tower', 0, 0, tiled=True)  6.33 us
    pallas_call x1, Pallas kernels, stem(): pl.pallas_call(functools.partial(stem_kernel, bins), out_shape=jax.ShapeD...  3.86 us
    ppermute x1, starting transfers between devices, per_device(): lax.ppermute(send, 'genome', [(i, i + 1) for i in range(starts - 1)])  2.2 us
    ppermute x1, waiting for transfers between devices, per_device(): lax.ppermute(send, 'genome', [(i, i + 1) for i in range(starts - 1)])  1.3 us
    pallas_call x1, Pallas kernels, per_device(): pl.pallas_call(functools.partial(finish_kernel, height), out_shape=jax.Sh...  1.23 us
  transfers between devices with their start and end apart: 2, of which 2 were waited for; matrix products, arithmetic and copies ran while one was open for 0% of the time, Pallas kernels for 0%

profile of v5, /device:TPU:0, one launch (start us, length us, event | category | flops | bytes accessed | tf_op | source)
XLA Modules:
  0.0 39.8 jit_solution(3477372348907528478)
XLA Ops:
  0.6 0.0 copy-start.5
  0.6 0.0 copy-start.4
  0.7 0.0 copy-start.1
  0.7 0.0 copy-start.7
  0.7 0.0 copy-start.3
  0.7 0.0 copy-start.2
  0.7 0.0 copy-start
  0.7 0.0 copy-start.6
  0.7 3.9 %stem.1 = bf16[8,48,128]{2,1,0:T(8,128)(2,1)} custom-call(s32[1024,128]{1,0:T(8,128)} %bitcast.10, bf16[96,8192]{1,0:T(8,128)(2,1)} %weight_hbm.1), custom_call_target="tpu_custom_call" | custom-call | tf_op jit(solution)/shard_map/stem/pallas_call | solution.py:67
  4.6 7.3 %all-to-all-start = ((bf16[8,48,128]{2,1,0:T(8,128)(2,1)}), bf16[8,48,128]{2,1,0:T(8,128)(2,1)S(1)}, u32[]{:S(2)}, u32[]{:S(2)}) async-start(bf16[8,48,128]{2,1,0:T(8,128)(2,1)} %stem.1), calls=%async_computation | async-start | bytes 196608 | tf_op jit(solution)/shard_map/all_to_all | solution.py:406
  11.9 0.1 pad_add_fusion.place_ref
  12.0 7.0 %all-to-all-done.refs_0_ = bf16[8,48,128]{2,1,0:T(8,128)(2,1)S(1)} async-done(((bf16[8,48,128]{2,1,0:T(8,128)(2,1)}), bf16[8,48,128]{2,1,0:T(8,128)(2,1)S(1)}, u32[]{:S(2)}, u32[]{:S(2)}) %all-to-all-start) | async-done | bytes 98336 | tf_op jit(solution)/shard_map/all_to_all | solution.py:406
  19.0 0.0 copy-done.5
  19.0 0.0 copy-done.4
  19.0 0.0 copy-done.1
  19.0 0.0 copy-done.7
  19.0 0.0 copy-done.3
  19.0 0.0 copy-done.2
  19.0 0.0 copy-done
  19.1 0.0 copy-done.6
  19.1 9.6 %windows.1 = (f32[5,16,256]{2,1,0:T(8,128)}, f32[15,128]{1,0:T(8,128)S(1)}, f32[4,2,128]{2,1,0:T(2,128)S(1)}) custom-call(s32[2]{0:T(128)S(1)} %pad_add_fusion.place_ref, bf16[8,48,128]{2,1,0:T(8,128)(2,1)S(1)} %all-to-all-done.refs_0_, bf16[6,48,288]{2,1,0:T(8,128)(2,1)S(1)} %copy-done, bf16[6,48,96]{2,1,0:T(8,128)(2,1)S(1)} %bitcast.7, ...), custom_call_target="tpu_custom_call" | custom-call | tf_op jit(solution)/shard_map/windows/pallas_call | solution.py:415
  28.7 2.2 %collective-permute-start = (f32[4,2,128]{2,1,0:T(2,128)S(1)}, f32[4,2,128]{2,1,0:T(2,128)S(1)}, u32[]{:S(2)}, u32[]{:S(2)}) collective-permute-start(f32[4,2,128]{2,1,0:T(2,128)S(1)} %get-tuple-element.7), channel_id=1, source_target_pairs={{0,4},{4,8},{8,12},{12,16},{16,20},{20,24},{24,28},{1,5},{5,9},{9,... | collective-permute-start | bytes 12296 | tf_op jit(solution)/shard_map/ppermute | solution.py:445
  30.9 1.3 %collective-permute-done = f32[4,2,128]{2,1,0:T(2,128)S(1)} collective-permute-done((f32[4,2,128]{2,1,0:T(2,128)S(1)}, f32[4,2,128]{2,1,0:T(2,128)S(1)}, u32[]{:S(2)}, u32[]{:S(2)}) %collective-permute-start) | collective-permute-done | bytes 4128 | tf_op jit(solution)/shard_map/ppermute | solution.py:445
  32.2 0.1 broadcast_select_fusion
  32.3 6.3 %all_to_all.10.got_ref = f32[4,2,128]{2,1,0:T(2,128)S(1)} all-to-all(f32[4,2,128]{2,1,0:T(2,128)S(1)} %broadcast_select_fusion), channel_id=1, replica_groups=mesh['genome'=8,'tower'=4] {'tower'}, dimensions={0} | all-to-all | bytes 8192 | tf_op jit(solution)/shard_map/all_to_all | solution.py:447
  38.6 1.2 %finish.1 = f32[5,2,16]{2,1,0:T(2,128)} custom-call(s32[2]{0:T(128)S(1)} %pad_add_fusion.place_ref, f32[15,128]{1,0:T(8,128)S(1)} %get-tuple-element.6.keep_ref, f32[4,2,128]{2,1,0:T(2,128)S(1)} %all_to_all.10.got_ref), custom_call_target="tpu_custom_call" | custom-call | tf_op jit(solution)/shard_map/finish/pallas_call | solution.py:448
  (1 shorter events, 0.0 us)
Async XLA Ops:
  0.6 18.4 %copy-start.5 = (bf16[5,48]{1,0:T(8,128)(2,1)S(1)}, bf16[5,48]{1,0:T(8,128)(2,1)}, u32[]{:S(2)}) copy-start(bf16[5,48]{1,0:T(8,128)(2,1)} %refs_7_.1) | copy-start | bytes 1444
  0.6 18.4 %copy-start.4 = (bf16[2,48,48]{2,1,0:T(8,128)(2,1)S(1)}, bf16[2,48,48]{2,1,0:T(8,128)(2,1)}, u32[]{:S(2)}) copy-start(bf16[2,48,48]{2,1,0:T(8,128)(2,1)} %refs_6_.1) | copy-start | bytes 27652
  0.7 18.4 %copy-start.1 = (bf16[2,3,48,144]{3,2,1,0:T(8,128)(2,1)S(1)}, bf16[2,3,48,144]{3,2,1,0:T(8,128)(2,1)}, u32[]{:S(2)}) copy-start(bf16[2,3,48,144]{3,2,1,0:T(8,128)(2,1)} %refs_5_.1) | copy-start | bytes 248836
  0.7 18.4 %copy-start.7 = (f32[48]{0:T(128)S(1)}, f32[48]{0:T(128)}, u32[]{:S(2)}) copy-start(f32[48]{0:T(128)} %param.16) | copy-start | bytes 580
  0.7 18.4 %copy-start.3 = (bf16[96,96]{1,0:T(8,128)(2,1)S(1)}, bf16[96,96]{1,0:T(8,128)(2,1)}, u32[]{:S(2)}) copy-start(bf16[96,96]{1,0:T(8,128)(2,1)} %refs_3_.1) | copy-start | bytes 55300
  0.7 18.4 %copy-start.2 = (bf16[6,96,48]{1,2,0:T(8,128)(2,1)S(1)}, bf16[6,96,48]{1,2,0:T(8,128)(2,1)}, u32[]{:S(2)}) copy-start(bf16[6,96,48]{1,2,0:T(8,128)(2,1)} %param.14) | copy-start | bytes 165892
  0.7 18.4 %copy-start = (bf16[6,48,288]{2,1,0:T(8,128)(2,1)S(1)}, bf16[6,48,288]{2,1,0:T(8,128)(2,1)}, u32[]{:S(2)}) copy-start(bf16[6,48,288]{2,1,0:T(8,128)(2,1)} %refs_1_.1) | copy-start | bytes 497668
  0.7 18.4 %copy-start.6 = (s32[256]{0:T(256)S(1)}, s32[256]{0:T(256)}, u32[]{:S(2)}) copy-start(s32[256]{0:T(256)} %param.11) | copy-start | bytes 3076
  4.6 14.4 %all-to-all-start = ((bf16[8,48,128]{2,1,0:T(8,128)(2,1)}), bf16[8,48,128]{2,1,0:T(8,128)(2,1)S(1)}, u32[]{:S(2)}, u32[]{:S(2)}) async-start(bf16[8,48,128]{2,1,0:T(8,128)(2,1)} %stem.1), calls=%async_computation | async-start | bytes 196608 | tf_op jit(solution)/shard_map/all_to_all | solution.py:406
  28.7 3.5 %collective-permute-start = (f32[4,2,128]{2,1,0:T(2,128)S(1)}, f32[4,2,128]{2,1,0:T(2,128)S(1)}, u32[]{:S(2)}, u32[]{:S(2)}) collective-permute-start(f32[4,2,128]{2,1,0:T(2,128)S(1)} %get-tuple-element.7), channel_id=1, source_target_pairs={{0,4},{4,8},{8,12},{12,16},{16,20},{20,24},{24,28},{1,5},{5,9},{9,... | collective-permute-start | bytes 12296 | tf_op jit(solution)/shard_map/ppermute | solution.py:445

commit v6 on v4

--- a/solution.py
+++ b/solution.py
@@ -14,7 +14,7 @@
 LANES = 128
 F32 = jnp.float32
 BF16 = jnp.bfloat16
-VMEM_BYTES = 48 * 1024 * 1024
+VMEM_BYTES = 40 * 1024 * 1024
 
 
 def dot(a, b):
@@ -111,9 +111,17 @@
     return jnp.where(row == col, tall, jnp.zeros((), BF16)).reshape(targets * count, count * width)
 
 
-def segments(margin):
-    sizes = [BINS - STRIDE * b + margin + 1 for b in range(BLOCKS)]
-    offsets = [sum(sizes[:b]) for b in range(BLOCKS)]
+MARGIN = 2
+NEAR = 2 * STRIDE
+
+
+def segments(begin, height):
+    sizes = []
+    for b in range(BLOCKS):
+        size = BINS - STRIDE * b + MARGIN + 1 - begin
+        if size > MARGIN + 1:
+            sizes.append(min(size, NEAR + height - 1 + 2 * MARGIN))
+    offsets = [sum(sizes[:b]) for b in range(len(sizes))]
     lanes = -(-sum(sizes) // LANES) * LANES
     return sizes, offsets, lanes
 
@@ -128,32 +136,10 @@
     return jnp.concatenate([edge, values[:, : extent + offset]], axis=1)
 
 
-def main_kernel(
-    height,
-    groups,
-    place_ref,
-    *refs,
-):
-    (
-        features,
-        trunk_in,
-        trunk_out,
-        pair_weight,
-        rate_ref,
-        conv_ref,
-        mix_ref,
-        head_ref,
-        stitch_ref,
-        stitched_ref,
-        keep_ref,
-        send_ref,
-        taps_a,
-        taps_b,
-        grid_ref,
-        final_ref,
-    ) = refs
-    margin = 2
-    sizes, offsets, lanes = segments(margin)
+def tower_band(height, groups, begin, place_ref, left, right, weight_refs, scratch):
+    rate_ref, conv_ref, mix_ref, head_ref, stitch_ref = weight_refs
+    taps_a, taps_b, grid_ref, final_ref = scratch
+    sizes, offsets, lanes = segments(begin, height)
     tower_row = place_ref[0] * height
     channels = rate_ref.shape[1]
     depth = 3 * channels
@@ -164,6 +150,129 @@
     mix_a = {span: block_diagonal(mix_ref[0], span) for span in sorted(spans_a)}
     mix_b = {span: block_diagonal(mix_ref[1], span) for span in sorted(spans_b)}
     head = head_by_row(head_ref[...], height)
+
+    lane = lax.broadcasted_iota(jnp.int32, (1, lanes), 1)
+    block_of = jnp.zeros((1, lanes), jnp.int32)
+    start_of = jnp.zeros((1, lanes), jnp.int32)
+    for b in range(1, len(sizes)):
+        block_of = jnp.where(lane >= offsets[b], b, block_of)
+        start_of = jnp.where(lane >= offsets[b], offsets[b], start_of)
+    step = lane - start_of
+    first_row = STRIDE * block_of + tower_row - MARGIN
+    column = first_row + begin + step
+    in_column = (column < BINS) & (column >= 0)
+
+    row = lax.broadcasted_iota(jnp.int32, (channels, channels), 0)
+    col = lax.broadcasted_iota(jnp.int32, (channels, channels), 1)
+    rate = jnp.sum(jnp.where(row == col, rate_ref[...], 0.0), axis=1, keepdims=True)
+    rate = jnp.broadcast_to(rate, (channels, LANES))
+    rate = jnp.concatenate([rate] * (lanes // LANES), axis=1)
+
+    def place_taps(ref, slot, act):
+        act = act.astype(BF16)
+        ref[pl.ds(slot * depth, channels), :] = pltpu.roll(act, 1, 1)
+        ref[pl.ds(slot * depth + channels, channels), :] = act
+        ref[pl.ds(slot * depth + 2 * channels, channels), :] = pltpu.roll(act, lanes - 1, 1)
+
+    def inside(row):
+        at = first_row + row
+        return in_column & (at >= 0) & (at < BINS)
+
+    for row in range(height + 2 * MARGIN):
+        apart = jnp.abs(begin + step - row).astype(F32)
+        decay = jnp.log1p(apart)
+        tiles = []
+        for tile in range(lanes // LANES):
+            piece = None
+            here = lane[:, tile * LANES : (tile + 1) * LANES]
+            for b in range(len(sizes)):
+                low, high = offsets[b], offsets[b] + sizes[b]
+                if high <= tile * LANES or low >= (tile + 1) * LANES:
+                    continue
+                spread = jnp.broadcast_to(left[b][:, row : row + 1], (channels, LANES))
+                piece = spread if piece is None else jnp.where(here >= low, spread, piece)
+            tiles.append(piece)
+        mixed = jnp.concatenate(tiles, axis=1) + right - rate * decay
+        place_taps(taps_a, row, jnp.where(inside(row), jnp.maximum(mixed, 0.0), 0.0))
+
+    for first in range(0, height + 2, groups):
+        span = min(groups, height + 2 - first)
+        conv = dot(conv_a[span], taps_a[pl.ds(first * depth, (span + 2) * depth), :])
+        update = dot(mix_a[span], jnp.maximum(conv, 0.0).astype(BF16))
+        for r in range(span):
+            row = first + r
+            kept = taps_a[pl.ds((row + 1) * depth + channels, channels), :].astype(F32)
+            grid = kept + update[r * channels : (r + 1) * channels]
+            if 1 <= row <= height:
+                grid_ref[pl.ds((row - 1) * channels, channels), :] = grid
+            place_taps(taps_b, row, jnp.where(inside(row + 1), jnp.maximum(grid, 0.0), 0.0))
+    for first in range(0, height, groups):
+        span = min(groups, height - first)
+        conv = dot(conv_b[span], taps_b[pl.ds(first * depth, (span + 2) * depth), :])
+        update = dot(mix_b[span], jnp.maximum(conv, 0.0).astype(BF16))
+        rows = pl.ds(first * channels, span * channels)
+        final_ref[rows, :] = jnp.maximum(grid_ref[rows, :] + update, 0.0).astype(BF16)
+    targets = head.shape[0] // height
+    contact = dot(head, final_ref[...]).reshape(targets, height, lanes)
+
+    at = lax.broadcasted_iota(jnp.int32, (height, BINS), 0)
+    bin_of = lax.broadcasted_iota(jnp.int32, (height, BINS), 1)
+    local = lax.broadcasted_iota(jnp.int32, (height, NEAR), 0)
+    ahead = lax.broadcasted_iota(jnp.int32, (height, NEAR), 1) + begin
+    weight_sum = jnp.zeros((height, NEAR), F32)
+    weights = []
+    for b in range(len(sizes)):
+        weight = jnp.where(bin_of == STRIDE * b + tower_row + at, stitch_ref[...], 0)
+        weight = jnp.sum(weight.astype(F32), axis=1, keepdims=True)
+        weight = jnp.where(place_ref[1] >= b, weight, 0.0)
+        reach = STRIDE * b + tower_row + local + ahead < BINS
+        weight = jnp.where(reach, weight, 0.0)
+        weights.append(weight)
+        weight_sum = weight_sum + weight
+    scale = 1.0 / jnp.maximum(weight_sum, 1.0)
+    weights = [w * scale for w in weights]
+    bands = []
+    map_row = lax.broadcasted_iota(jnp.int32, (height, lanes), 0)
+    for t in range(targets):
+        band = None
+        skewed = contact[t]
+        for bit in range((height - 1).bit_length()):
+            turned = pltpu.roll(skewed, lanes - (1 << bit), 1)
+            skewed = jnp.where((map_row >> bit) & 1 == 1, turned, skewed)
+        for b in range(len(sizes)):
+            first, reach = offsets[b] + MARGIN, min(NEAR, BINS - STRIDE * b - begin)
+            piece = skewed[:, first : first + reach]
+            if reach < NEAR:
+                piece = jnp.concatenate([piece, jnp.zeros((height, NEAR - reach), F32)], axis=1)
+            piece = piece * weights[b]
+            band = piece if band is None else band + piece
+        bands.append(band)
+    return bands
+
+
+def near_kernel(
+    height,
+    groups,
+    place_ref,
+    features,
+    trunk_in,
+    trunk_out,
+    pair_weight,
+    rate_ref,
+    conv_ref,
+    mix_ref,
+    head_ref,
+    stitch_ref,
+    near_ref,
+    keep_ref,
+    send_ref,
+    left_ref,
+    right_ref,
+    *scratch,
+):
+    tower_row = place_ref[0] * height
+    channels = rate_ref.shape[1]
+    targets = head_ref.shape[0]
 
     starts = features.shape[0]
     blocks = []
@@ -187,134 +296,52 @@
     layers = trunk_in.shape[0]
     for layer in range(layers):
         dilation = max(1, extent // 2 ** (layers - layer))
-        active = jax.nn.relu(stream)
-        parts = [active[:, b * BINS : (b + 1) * BINS] for b in range(BLOCKS)]
-        stacked = jnp.concatenate(
+        active = jnp.maximum(stream, 0.0).astype(BF16)
+        width = active.shape[0]
+        flat = trunk_in[layer]
+        mid = flat.shape[0]
+        tall = jnp.concatenate([flat[:, q * width : (q + 1) * width] for q in range(3)], axis=0)
+        taps = dot(tall, active)
+        inner = taps[mid : 2 * mid] + jnp.concatenate(
             [
-                jnp.concatenate([shifted(p, o) for p in parts], axis=1).astype(BF16)
-                for o in (-dilation, 0, dilation)
+                shifted(taps[:mid, b * BINS : (b + 1) * BINS], -dilation)
+                + shifted(taps[2 * mid :, b * BINS : (b + 1) * BINS], dilation)
+                for b in range(BLOCKS)
             ],
-            axis=0,
+            axis=1,
         )
-        inner = dot(trunk_in[layer], stacked)
         squeezed = jax.nn.relu(inner).astype(BF16)
         stream = stream + lax.dot_general(
             trunk_out[layer], squeezed, (((0,), (0,)), ((), ())), preferred_element_type=F32
         )
     projected = dot(pair_weight[...], jax.nn.relu(stream).astype(BF16))
 
-    lane = lax.broadcasted_iota(jnp.int32, (1, lanes), 1)
-    block_of = jnp.zeros((1, lanes), jnp.int32)
-    start_of = jnp.zeros((1, lanes), jnp.int32)
-    for b in range(1, BLOCKS):
-        block_of = jnp.where(lane >= offsets[b], b, block_of)
-        start_of = jnp.where(lane >= offsets[b], offsets[b], start_of)
-    step = lane - start_of
-    first_row = STRIDE * block_of + tower_row - margin
-    column = first_row + step
-    in_column = (column < BINS) & (column >= 0)
-
-    right = []
     left = []
+    parts = {0: [], NEAR: []}
     for b in range(BLOCKS):
-        begin = STRIDE * b + tower_row - margin
-        turn = jnp.where(begin > 0, BINS - begin, -begin)
-        terms = projected[:, b * BINS : (b + 1) * BINS]
-        turned = pltpu.roll(terms, turn, 1)
+        start = STRIDE * b + tower_row - MARGIN
+        turn = jnp.where(start > 0, BINS - start, -start)
+        turned = pltpu.roll(projected[:, b * BINS : (b + 1) * BINS], turn, 1)
         left.append(turned[:channels, :LANES])
-        own = turned[channels:]
-        if sizes[b] > BINS:
-            own = jnp.concatenate([own, own[:, : sizes[b] - BINS]], axis=1)
-        right.append(own[:, : sizes[b]])
-    used = sum(sizes)
-    if lanes > used:
-        right.append(jnp.zeros((channels, lanes - used), F32))
-    right = jnp.concatenate(right, axis=1)
-    row = lax.broadcasted_iota(jnp.int32, (channels, channels), 0)
-    col = lax.broadcasted_iota(jnp.int32, (channels, channels), 1)
-    rate = jnp.sum(jnp.where(row == col, rate_ref[...], 0.0), axis=1, keepdims=True)
-    rate = jnp.broadcast_to(rate, (channels, LANES))
-    rate = jnp.concatenate([rate] * (lanes // LANES), axis=1)
-
-    def place_taps(ref, slot, act):
-        before = pltpu.roll(act, 1, 1)
-        after = pltpu.roll(act, lanes - 1, 1)
-        ref[pl.ds(slot * depth, channels), :] = before.astype(BF16)
-        ref[pl.ds(slot * depth + channels, channels), :] = act.astype(BF16)
-        ref[pl.ds(slot * depth + 2 * channels, channels), :] = after.astype(BF16)
-
-    def inside(row):
-        at = first_row + row
-        return in_column & (at >= 0) & (at < BINS)
-
-    for row in range(height + 2 * margin):
-        apart = jnp.abs(step - row).astype(F32)
-        decay = jnp.log1p(apart)
-        tiles = []
-        for tile in range(lanes // LANES):
-            piece = None
-            here = lane[:, tile * LANES : (tile + 1) * LANES]
-            for b in range(BLOCKS):
-                low, high = offsets[b], offsets[b] + sizes[b]
-                if high <= tile * LANES or low >= (tile + 1) * LANES:
-                    continue
-                spread = jnp.broadcast_to(left[b][:, row : row + 1], (channels, LANES))
-                piece = spread if piece is None else jnp.where(here >= low, spread, piece)
-            tiles.append(piece)
-        mixed = jnp.concatenate(tiles, axis=1) + right - rate * decay
-        place_taps(taps_a, row, jnp.where(inside(row), jnp.maximum(mixed, 0.0), 0.0))
-
-    for first in range(0, height + 2, groups):
-        span = min(groups, height + 2 - first)
-        conv = dot(conv_a[span], taps_a[pl.ds(first * depth, (span + 2) * depth), :])
-        update = dot(mix_a[span], jnp.maximum(conv, 0.0).astype(BF16))
-        for r in range(span):
-            row = first + r
-            kept = taps_a[pl.ds((row + 1) * depth + channels, channels), :].astype(F32)
-            grid = kept + update[r * channels : (r + 1) * channels]
-            if 1 <= row <= height:
-                grid_ref[pl.ds((row - 1) * channels, channels), :] = grid
-            place_taps(taps_b, row, jnp.where(inside(row + 1), jnp.maximum(grid, 0.0), 0.0))
-    for first in range(0, height, groups):
-        span = min(groups, height - first)
-        conv = dot(conv_b[span], taps_b[pl.ds(first * depth, (span + 2) * depth), :])
-        update = dot(mix_b[span], jnp.maximum(conv, 0.0).astype(BF16))
-        rows = pl.ds(first * channels, span * channels)
-        final_ref[rows, :] = jnp.maximum(grid_ref[rows, :] + update, 0.0).astype(BF16)
-    targets = head.shape[0] // height
-    contact = dot(head, final_ref[...]).reshape(targets, height, lanes)
-
-    local = lax.broadcasted_iota(jnp.int32, (height, BINS), 0)
-    ahead = lax.broadcasted_iota(jnp.int32, (height, BINS), 1)
-    weight_sum = jnp.zeros((height, BINS), F32)
-    weights = []
-    for b in range(BLOCKS):
-        weight = jnp.where(ahead == STRIDE * b + tower_row + local, stitch_ref[...], 0)
-        weight = jnp.sum(weight.astype(F32), axis=1, keepdims=True)
-        weight = jnp.where(place_ref[1] >= b, weight, 0.0)
-        reach = STRIDE * b + tower_row + local + ahead < BINS
-        weight = jnp.where(reach, weight, 0.0)
-        weights.append(weight)
-        weight_sum = weight_sum + weight
-    scale = 1.0 / jnp.maximum(weight_sum, 1.0)
-    weights = [w * scale for w in weights]
-    stitched = []
-    map_row = lax.broadcasted_iota(jnp.int32, (height, lanes), 0)
+        own = jnp.concatenate([turned[channels:], turned[channels:, :LANES]], axis=1)
+        for begin, terms in parts.items():
+            sizes = segments(begin, height)[0]
+            if b < len(sizes):
+                terms.append(own[:, begin : begin + sizes[b]])
+    for begin, terms in parts.items():
+        sizes, _, lanes = segments(begin, height)
+        if lanes > sum(sizes):
+            terms.append(jnp.zeros((channels, lanes - sum(sizes)), F32))
+        parts[begin] = jnp.concatenate(terms, axis=1)
+    right_ref[...] = parts[NEAR]
+    for b in range(left_ref.shape[0]):
+        left_ref[b] = left[b]
+    weight_refs = (rate_ref, conv_ref, mix_ref, head_ref, stitch_ref)
+    stitched = tower_band(
+        height, groups, 0, place_ref, left, parts[0], weight_refs, scratch
+    )
     for t in range(targets):
-        band = None
-        skewed = contact[t]
-        for bit in range((height - 1).bit_length()):
-            turned = pltpu.roll(skewed, lanes - (1 << bit), 1)
-            skewed = jnp.where((map_row >> bit) & 1 == 1, turned, skewed)
-        for b in range(BLOCKS):
-            first, reach = offsets[b] + margin, BINS - STRIDE * b
-            piece = skewed[:, first : first + reach]
-            if reach < BINS:
-                piece = jnp.concatenate([piece, jnp.zeros((height, BINS - reach), F32)], axis=1)
-            piece = piece * weights[b]
-            band = piece if band is None else band + piece
-        stitched_ref[t] = band
-        stitched.append(band[:, : 2 * STRIDE])
+        near_ref[t] = stitched[t]
 
     near = jnp.concatenate(stitched, axis=0)
     wide = 2 * STRIDE
@@ -363,6 +390,30 @@
         send_ref[lax.rem(place_ref[0] + k, STRIDE // height)] = jnp.concatenate(packed, axis=0)
 
 
+def far_kernel(
+    height,
+    groups,
+    place_ref,
+    near_ref,
+    left_ref,
+    right_ref,
+    rate_ref,
+    conv_ref,
+    mix_ref,
+    head_ref,
+    stitch_ref,
+    stitched_ref,
+    *scratch,
+):
+    left = [left_ref[b] for b in range(left_ref.shape[0])]
+    weight_refs = (rate_ref, conv_ref, mix_ref, head_ref, stitch_ref)
+    bands = tower_band(
+        height, groups, NEAR, place_ref, left, right_ref[...], weight_refs, scratch
+    )
+    for t in range(stitched_ref.shape[0]):
+        stitched_ref[t] = jnp.concatenate([near_ref[t], bands[t]], axis=1)
+
+
 def finish_kernel(height, place_ref, keep_ref, got_ref, out_ref):
     targets = out_ref.shape[0]
     per_row = LANES // height
@@ -405,39 +456,63 @@
     channels = distance_rate.shape[0]
     targets = head_weight.shape[0]
     place = jnp.stack([tower_index, genome_index]).astype(jnp.int32)
-    lanes = segments(2)[2]
     packs = -(-2 * targets * height // LANES)
     vmem = pl.BlockSpec(memory_space=pltpu.VMEM)
     smem = pl.BlockSpec(memory_space=pltpu.SMEM)
-    stitched, keep, send = pl.pallas_call(
-        functools.partial(main_kernel, height, groups),
-        out_shape=[
-            jax.ShapeDtypeStruct((targets, height, BINS), F32),
-            jax.ShapeDtypeStruct((3 * targets, LANES), F32),
-            jax.ShapeDtypeStruct((towers, packs, LANES), F32),
-        ],
-        in_specs=[smem] + [vmem] * 9,
-        out_specs=[vmem] * 3,
-        scratch_shapes=[
+
+    def scratch(begin):
+        lanes = segments(begin, height)[2]
+        return [
             pltpu.VMEM(((height + 4) * 3 * channels, lanes), BF16),
             pltpu.VMEM(((height + 2) * 3 * channels, lanes), BF16),
             pltpu.VMEM((height * channels, lanes), F32),
             pltpu.VMEM((height * channels, lanes), BF16),
+        ]
+
+    weights = (
+        distance_rate.reshape(1, channels),
+        tower_conv,
+        tower_mix,
+        head_weight,
+        stitch_weight.reshape(1, BINS),
+    )
+    far_sizes, _, far_lanes = segments(NEAR, height)
+    near, keep, send, left, right = pl.pallas_call(
+        functools.partial(near_kernel, height, groups),
+        out_shape=[
+            jax.ShapeDtypeStruct((targets, height, NEAR), F32),
+            jax.ShapeDtypeStruct((3 * targets, LANES), F32),
+            jax.ShapeDtypeStruct((towers, packs, LANES), F32),
+            jax.ShapeDtypeStruct((len(far_sizes), channels, LANES), F32),
+            jax.ShapeDtypeStruct((channels, far_lanes), F32),
         ],
+        in_specs=[smem] + [vmem] * 9,
+        out_specs=[vmem] * 5,
+        scratch_shapes=scratch(0),
         compiler_params=pltpu.CompilerParams(vmem_limit_bytes=VMEM_BYTES),
-        name="windows",
+        name="near",
     )(
         place,
         features,
         trunk_in,
         jnp.transpose(trunk_out, (0, 2, 1)),
         pair_weight,
-        distance_rate.reshape(1, channels),
-        tower_conv,
-        tower_mix,
-        head_weight,
-        stitch_weight.reshape(1, BINS),
+        *weights,
     )
+    stitched = pl.pallas_call(
+        functools.partial(far_kernel, height, groups),
+        out_shape=jax.ShapeDtypeStruct((targets, height, BINS), F32),
+        in_specs=[smem] + [vmem] * 8,
+        out_specs=vmem,
+        scratch_shapes=scratch(NEAR),
+        compiler_params=pltpu.CompilerParams(vmem_limit_bytes=VMEM_BYTES),
+        cost_estimate=pl.CostEstimate(
+            flops=2 * (2 * height + 2) * far_lanes * channels * channels * 40,
+            bytes_accessed=1 << 20,
+            transcendentals=0,
+        ),
+        name="far",
+    )(place, near, left, right, *weights)
     starts = lax.axis_size("genome")
     passed = lax.ppermute(send, "genome", [(i, i + 1) for i in range(starts - 1)])
     ahead = (jnp.arange(towers) > tower_index)[:, None, None]

time: 40.7 us -> 42.6 us (1.047)
  the two profiles are of different devices: /device:TPU:0 before, /device:TPU:11 now
where the time goes in v6:
time: 42.6 us; the launch traced here: 42.3 us
  Pallas kernels  18.9 us (44%)
  starting transfers between devices  15.5 us (36%)
  waiting for transfers between devices  6.28 us (15%)
  between operations  0.78 us (2%)
  other arithmetic  0.75 us (2%)
    pallas_call x1, Pallas kernels, per_device(): pl.pallas_call(functools.partial(near_kernel, height, groups), out_shape=...  8.61 us
    all_to_all x1, starting transfers between devices, per_device(): lax.all_to_all(jnp.where(ahead, send, passed), 'tower', 0, 0, tiled=True)  6.65 us
    all_to_all x1, starting transfers between devices, per_device(): features = lax.all_to_all(own, 'genome', 0, 0, tiled=True)  5.73 us
    pallas_call x1, Pallas kernels, per_device(): pl.pallas_call(functools.partial(far_kernel, height, groups), out_shape=j...  5.25 us
    all_to_all x1, waiting for transfers between devices, per_device(): features = lax.all_to_all(own, 'genome', 0, 0, tiled=True)  4.2 us
    pallas_call x1, Pallas kernels, stem(): pl.pallas_call(functools.partial(stem_kernel, bins), out_shape=jax.ShapeD...  3.85 us
    ppermute x1, starting transfers between devices, per_device(): lax.ppermute(send, 'genome', [(i, i + 1) for i in range(starts - 1)])  3.15 us
    ppermute x1, waiting for transfers between devices, per_device(): lax.ppermute(send, 'genome', [(i, i + 1) for i in range(starts - 1)])  2.08 us
  transfers between devices with their start and end apart: 3, of which 2 were waited for; matrix products, arithmetic and copies ran while one was open for 0% of the time, Pallas kernels for 12%

profile of v6, /device:TPU:11, one launch (start us, length us, event | category | flops | bytes accessed | tf_op | source)
XLA Modules:
  0.0 42.3 jit_solution(17259574921717459993)
XLA Ops:
  0.6 0.0 copy-start.5
  0.6 0.0 copy-start.4
  0.7 0.0 copy-start.1
  0.7 0.0 copy-start.7
  0.7 0.0 copy-start.3
  0.7 0.0 copy-start.2
  0.7 0.0 copy-start
  0.7 0.0 copy-start.6
  0.7 3.9 %stem.1 = bf16[8,48,128]{2,1,0:T(8,128)(2,1)} custom-call(s32[1024,128]{1,0:T(8,128)} %bitcast.12, bf16[96,8192]{1,0:T(8,128)(2,1)} %weight_hbm.1), custom_call_target="tpu_custom_call" | custom-call | tf_op jit(solution)/shard_map/stem/pallas_call | solution.py:67
  4.6 5.7 %all-to-all-start = ((bf16[8,48,128]{2,1,0:T(8,128)(2,1)}), bf16[8,48,128]{2,1,0:T(8,128)(2,1)S(1)}, u32[]{:S(2)}, u32[]{:S(2)}) async-start(bf16[8,48,128]{2,1,0:T(8,128)(2,1)} %stem.1), calls=%async_computation | async-start | bytes 196608 | tf_op jit(solution)/shard_map/all_to_all | solution.py:454
  10.3 0.1 pad_add_fusion.place_ref
  10.4 4.2 %all-to-all-done.features = bf16[8,48,128]{2,1,0:T(8,128)(2,1)S(1)} async-done(((bf16[8,48,128]{2,1,0:T(8,128)(2,1)}), bf16[8,48,128]{2,1,0:T(8,128)(2,1)S(1)}, u32[]{:S(2)}, u32[]{:S(2)}) %all-to-all-start) | async-done | bytes 98336 | tf_op jit(solution)/shard_map/all_to_all | solution.py:454
  14.6 0.0 copy-done.5
  14.6 0.0 copy-done.4
  14.6 0.0 copy-done.1
  14.6 0.0 copy-done.7
  14.6 0.0 copy-done.3
  14.6 0.0 copy-done.2
  14.6 0.0 copy-done
  14.6 0.0 copy-done.6
  14.6 8.6 %near.1 = (f32[5,16,128]{2,1,0:T(8,128)S(1)}, f32[15,128]{1,0:T(8,128)S(1)}, f32[4,2,128]{2,1,0:T(2,128)S(1)}, f32[2,48,128]{2,1,0:T(8,128)S(1)}, f32[48,256]{1,0:T(8,128)S(1)}) custom-call(s32[2]{0:T(128)S(1)} %pad_add_fusion.place_ref, bf16[8,48,128]{2,1,0:T(8,128)(2,1)S(1)} %all-to-all-done.features, bf16[6,48,288]{2,1,0:T(8,128)(2,1)S(1)} %copy-done, ...), custom_call_target="tpu_custom_call" | custom-call | tf_op jit(solution)/shard_map/near/pallas_call | solution.py:480
  23.3 3.1 %collective-permute-start = (f32[4,2,128]{2,1,0:T(2,128)S(1)}, f32[4,2,128]{2,1,0:T(2,128)S(1)}, u32[]{:S(2)}, u32[]{:S(2)}) collective-permute-start(f32[4,2,128]{2,1,0:T(2,128)S(1)} %get-tuple-element.11), channel_id=1, source_target_pairs={{0,4},{4,8},{8,12},{12,16},{16,20},{20,24},{24,28},{1,5},{5,9},{9,... | collective-permute-start | bytes 12296 | tf_op jit(solution)/shard_map/ppermute | solution.py:517
  26.4 2.1 %collective-permute-done = f32[4,2,128]{2,1,0:T(2,128)S(1)} collective-permute-done((f32[4,2,128]{2,1,0:T(2,128)S(1)}, f32[4,2,128]{2,1,0:T(2,128)S(1)}, u32[]{:S(2)}, u32[]{:S(2)}) %collective-permute-start) | collective-permute-done | bytes 4128 | tf_op jit(solution)/shard_map/ppermute | solution.py:517
  28.5 0.7 %broadcast_select_fusion = f32[4,2,128]{2,1,0:T(2,128)} fusion(f32[4,2,128]{2,1,0:T(2,128)S(1)} %get-tuple-element.11, f32[4,2,128]{2,1,0:T(2,128)S(1)} %collective-permute-done, pred[4]{0:T(512)(128)(4,1)S(1)} %iota_compare_fusion), kind=kLoop, calls=%fused_computation | loop fusion | flops 1024 | bytes 12292 | tf_op jit(solution)/shard_map/jit(_where)/select_n | solution.py:519
  29.2 6.6 %all-to-all-start.1 = ((f32[4,2,128]{2,1,0:T(2,128)}), f32[4,2,128]{2,1,0:T(2,128)S(1)}, u32[]{:S(2)}, u32[]{:S(2)}) async-start(f32[4,2,128]{2,1,0:T(2,128)} %broadcast_select_fusion), calls=%async_computation.1 | async-start | bytes 8192 | tf_op jit(solution)/shard_map/all_to_all | solution.py:519
  35.8 5.2 %far.1 = f32[5,16,256]{2,1,0:T(8,128)} custom-call(s32[2]{0:T(128)S(1)} %pad_add_fusion.place_ref, f32[5,16,128]{2,1,0:T(8,128)S(1)} %get-tuple-element.7.near_ref, f32[2,48,128]{2,1,0:T(8,128)S(1)} %get-tuple-element.8.left_ref, f32[48,256]{1,0:T(8,128)S(1)} %get-tuple-element.9.right_ref, f32[1,48]{1,0:T(1,128)S(1)} %bitcast.11, ...), custom_call_target="tpu_custom_call" | custom-call | flops 1604321280 | bytes 1048576 | tf_op jit(solution)/shard_map/far/pallas_call | solution.py:502
  41.1 0.0 all-to-all-done.1.got_ref
  41.1 1.2 %finish.1 = f32[5,2,16]{2,1,0:T(2,128)} custom-call(s32[2]{0:T(128)S(1)} %pad_add_fusion.place_ref, f32[15,128]{1,0:T(8,128)S(1)} %get-tuple-element.10.keep_ref, f32[4,2,128]{2,1,0:T(2,128)S(1)} %all-to-all-done.1.got_ref), custom_call_target="tpu_custom_call" | custom-call | tf_op jit(solution)/shard_map/finish/pallas_call | solution.py:520
  (1 shorter events, 0.0 us)
Async XLA Ops:
  0.6 13.9 %copy-start.5 = (bf16[5,48]{1,0:T(8,128)(2,1)S(1)}, bf16[5,48]{1,0:T(8,128)(2,1)}, u32[]{:S(2)}) copy-start(bf16[5,48]{1,0:T(8,128)(2,1)} %head_ref.3) | copy-start | bytes 1444
  0.6 13.9 %copy-start.4 = (bf16[2,48,48]{2,1,0:T(8,128)(2,1)S(1)}, bf16[2,48,48]{2,1,0:T(8,128)(2,1)}, u32[]{:S(2)}) copy-start(bf16[2,48,48]{2,1,0:T(8,128)(2,1)} %mix_ref.3) | copy-start | bytes 27652
  0.7 13.9 %copy-start.1 = (bf16[2,3,48,144]{3,2,1,0:T(8,128)(2,1)S(1)}, bf16[2,3,48,144]{3,2,1,0:T(8,128)(2,1)}, u32[]{:S(2)}) copy-start(bf16[2,3,48,144]{3,2,1,0:T(8,128)(2,1)} %conv_ref.3) | copy-start | bytes 248836
  0.7 13.9 %copy-start.7 = (f32[48]{0:T(128)S(1)}, f32[48]{0:T(128)}, u32[]{:S(2)}) copy-start(f32[48]{0:T(128)} %param.16) | copy-start | bytes 580
  0.7 13.9 %copy-start.3 = (bf16[96,96]{1,0:T(8,128)(2,1)S(1)}, bf16[96,96]{1,0:T(8,128)(2,1)}, u32[]{:S(2)}) copy-start(bf16[96,96]{1,0:T(8,128)(2,1)} %pair_weight.1) | copy-start | bytes 55300
  0.7 13.9 %copy-start.2 = (bf16[6,96,48]{1,2,0:T(8,128)(2,1)S(1)}, bf16[6,96,48]{1,2,0:T(8,128)(2,1)}, u32[]{:S(2)}) copy-start(bf16[6,96,48]{1,2,0:T(8,128)(2,1)} %param.14) | copy-start | bytes 165892
  0.7 13.9 %copy-start = (bf16[6,48,288]{2,1,0:T(8,128)(2,1)S(1)}, bf16[6,48,288]{2,1,0:T(8,128)(2,1)}, u32[]{:S(2)}) copy-start(bf16[6,48,288]{2,1,0:T(8,128)(2,1)} %trunk_in.1) | copy-start | bytes 497668
  0.7 13.9 %copy-start.6 = (s32[256]{0:T(256)S(1)}, s32[256]{0:T(256)}, u32[]{:S(2)}) copy-start(s32[256]{0:T(256)} %param.11) | copy-start | bytes 3076
  4.6 10.0 %all-to-all-start = ((bf16[8,48,128]{2,1,0:T(8,128)(2,1)}), bf16[8,48,128]{2,1,0:T(8,128)(2,1)S(1)}, u32[]{:S(2)}, u32[]{:S(2)}) async-start(bf16[8,48,128]{2,1,0:T(8,128)(2,1)} %stem.1), calls=%async_computation | async-start | bytes 196608 | tf_op jit(solution)/shard_map/all_to_all | solution.py:454
  23.3 5.3 %collective-permute-start = (f32[4,2,128]{2,1,0:T(2,128)S(1)}, f32[4,2,128]{2,1,0:T(2,128)S(1)}, u32[]{:S(2)}, u32[]{:S(2)}) collective-permute-start(f32[4,2,128]{2,1,0:T(2,128)S(1)} %get-tuple-element.11), channel_id=1, source_target_pairs={{0,4},{4,8},{8,12},{12,16},{16,20},{20,24},{24,28},{1,5},{5,9},{9,... | collective-permute-start | bytes 12296 | tf_op jit(solution)/shard_map/ppermute | solution.py:517
  29.2 11.9 %all-to-all-start.1 = ((f32[4,2,128]{2,1,0:T(2,128)}), f32[4,2,128]{2,1,0:T(2,128)S(1)}, u32[]{:S(2)}, u32[]{:S(2)}) async-start(f32[4,2,128]{2,1,0:T(2,128)} %broadcast_select_fusion), calls=%async_computation.1 | async-start | bytes 8192 | tf_op jit(solution)/shard_map/all_to_all | solution.py:519

commit v7 on v5

--- a/solution.py
+++ b/solution.py
@@ -14,7 +14,7 @@
 LANES = 128
 F32 = jnp.float32
 BF16 = jnp.bfloat16
-VMEM_BYTES = 48 * 1024 * 1024
+VMEM_BYTES = 40 * 1024 * 1024
 
 
 def dot(a, b):
@@ -128,42 +128,111 @@
     return jnp.concatenate([edge, values[:, : extent + offset]], axis=1)
 
 
+def spans_of(rows, groups):
+    return sorted({groups, rows % groups} - {0})
+
+
+def prepare_kernel(
+    height,
+    groups,
+    place_ref,
+    _,
+    trunk_in,
+    rate_in,
+    conv_in,
+    mix_in,
+    head_in,
+    stitch_in,
+    trunk_ref,
+    rate_ref,
+    decay_ref,
+    inside_ref,
+    head_ref,
+    stitch_ref,
+    *conv_refs,
+):
+    margin = 2
+    sizes, offsets, lanes = segments(margin)
+    tower_row = place_ref[0] * height
+    for layer in range(trunk_in.shape[0]):
+        flat = trunk_in[layer]
+        width = flat.shape[1] // 3
+        trunk_ref[layer] = jnp.concatenate(
+            [flat[:, q * width : (q + 1) * width] for q in range(3)], axis=0
+        )
+    at = 0
+    for block, rows in enumerate((height + 2, height)):
+        for span in spans_of(rows, groups):
+            conv_refs[at][...] = banded(conv_in[block], span)
+            conv_refs[at + 1][...] = block_diagonal(mix_in[block], span)
+            at += 2
+    head_ref[...] = head_by_row(head_in[...], height)
+    channels = rate_in.shape[1]
+    row = lax.broadcasted_iota(jnp.int32, (channels, channels), 0)
+    col = lax.broadcasted_iota(jnp.int32, (channels, channels), 1)
+    rate = jnp.sum(jnp.where(row == col, rate_in[...], 0.0), axis=1, keepdims=True)
+    rate_ref[...] = jnp.broadcast_to(rate, rate_ref.shape)
+
+    lane = lax.broadcasted_iota(jnp.int32, (height + 2 * margin, lanes), 1)
+    block_of = jnp.zeros((height + 2 * margin, lanes), jnp.int32)
+    start_of = jnp.zeros((height + 2 * margin, lanes), jnp.int32)
+    for b in range(1, BLOCKS):
+        block_of = jnp.where(lane >= offsets[b], b, block_of)
+        start_of = jnp.where(lane >= offsets[b], offsets[b], start_of)
+    step = lane - start_of
+    first_row = STRIDE * block_of + tower_row - margin
+    column = first_row + step
+    in_column = (column < BINS) & (column >= 0)
+
+    row = lax.broadcasted_iota(jnp.int32, (height + 2 * margin, lanes), 0)
+    decay_ref[...] = jnp.log1p(jnp.abs(step - row).astype(F32))
+    at = first_row + row
+    inside_ref[...] = jnp.where(in_column & (at >= 0) & (at < BINS), 1.0, 0.0)
+
+    local = lax.broadcasted_iota(jnp.int32, (height, BINS), 0)
+    ahead = lax.broadcasted_iota(jnp.int32, (height, BINS), 1)
+    weight_sum = jnp.zeros((height, BINS), F32)
+    weights = []
+    for b in range(BLOCKS):
+        weight = jnp.where(ahead == STRIDE * b + tower_row + local, stitch_in[...], 0)
+        weight = jnp.sum(weight.astype(F32), axis=1, keepdims=True)
+        weight = jnp.where(place_ref[1] >= b, weight, 0.0)
+        reach = STRIDE * b + tower_row + local + ahead < BINS
+        weight = jnp.where(reach, weight, 0.0)
+        weights.append(weight)
+        weight_sum = weight_sum + weight
+    scale = 1.0 / jnp.maximum(weight_sum, 1.0)
+    for b in range(BLOCKS):
+        stitch_ref[b] = weights[b] * scale
+
+
 def main_kernel(
     height,
     groups,
     place_ref,
-    *refs,
+    features,
+    trunk_out,
+    pair_weight,
+    trunk_in,
+    rate_ref,
+    decay_ref,
+    inside_ref,
+    head_ref,
+    stitch_ref,
+    *rest,
 ):
-    (
-        features,
-        trunk_in,
-        trunk_out,
-        pair_weight,
-        rate_ref,
-        conv_ref,
-        mix_ref,
-        head_ref,
-        stitch_ref,
-        stitched_ref,
-        keep_ref,
-        send_ref,
-        taps_a,
-        taps_b,
-        grid_ref,
-        final_ref,
-    ) = refs
     margin = 2
     sizes, offsets, lanes = segments(margin)
     tower_row = place_ref[0] * height
-    channels = rate_ref.shape[1]
+    channels = rate_ref.shape[0]
     depth = 3 * channels
-    spans_a = {groups, (height + 2) % groups} - {0}
-    spans_b = {groups, height % groups} - {0}
-    conv_a = {span: banded(conv_ref[0], span) for span in sorted(spans_a)}
-    conv_b = {span: banded(conv_ref[1], span) for span in sorted(spans_b)}
-    mix_a = {span: block_diagonal(mix_ref[0], span) for span in sorted(spans_a)}
-    mix_b = {span: block_diagonal(mix_ref[1], span) for span in sorted(spans_b)}
-    head = head_by_row(head_ref[...], height)
+    rest = list(rest)
+    conv_a, conv_b, mix_a, mix_b = {}, {}, {}, {}
+    for span in spans_of(height + 2, groups):
+        conv_a[span], mix_a[span] = rest.pop(0), rest.pop(0)
+    for span in spans_of(height, groups):
+        conv_b[span], mix_b[span] = rest.pop(0), rest.pop(0)
+    stitched_ref, keep_ref, send_ref, taps_a, taps_b, grid_ref, final_ref = rest
 
     starts = features.shape[0]
     blocks = []
@@ -188,11 +257,8 @@
     for layer in range(layers):
         dilation = max(1, extent // 2 ** (layers - layer))
         active = jnp.maximum(stream, 0.0).astype(BF16)
-        width = active.shape[0]
-        flat = trunk_in[layer]
-        mid = flat.shape[0]
-        tall = jnp.concatenate([flat[:, q * width : (q + 1) * width] for q in range(3)], axis=0)
-        taps = dot(tall, active)
+        mid = trunk_in.shape[1] // 3
+        taps = dot(trunk_in[layer], active)
         inner = taps[mid : 2 * mid] + jnp.concatenate(
             [
                 shifted(taps[:mid, b * BINS : (b + 1) * BINS], -dilation)
@@ -206,17 +272,6 @@
             trunk_out[layer], squeezed, (((0,), (0,)), ((), ())), preferred_element_type=F32
         )
     projected = dot(pair_weight[...], jax.nn.relu(stream).astype(BF16))
-
-    lane = lax.broadcasted_iota(jnp.int32, (1, lanes), 1)
-    block_of = jnp.zeros((1, lanes), jnp.int32)
-    start_of = jnp.zeros((1, lanes), jnp.int32)
-    for b in range(1, BLOCKS):
-        block_of = jnp.where(lane >= offsets[b], b, block_of)
-        start_of = jnp.where(lane >= offsets[b], offsets[b], start_of)
-    step = lane - start_of
-    first_row = STRIDE * block_of + tower_row - margin
-    column = first_row + step
-    in_column = (column < BINS) & (column >= 0)
 
     right = []
     left = []
@@ -234,11 +289,8 @@
     if lanes > used:
         right.append(jnp.zeros((channels, lanes - used), F32))
     right = jnp.concatenate(right, axis=1)
-    row = lax.broadcasted_iota(jnp.int32, (channels, channels), 0)
-    col = lax.broadcasted_iota(jnp.int32, (channels, channels), 1)
-    rate = jnp.sum(jnp.where(row == col, rate_ref[...], 0.0), axis=1, keepdims=True)
-    rate = jnp.broadcast_to(rate, (channels, LANES))
-    rate = jnp.concatenate([rate] * (lanes // LANES), axis=1)
+    rate = jnp.concatenate([rate_ref[...]] * (lanes // LANES), axis=1)
+    lane = lax.broadcasted_iota(jnp.int32, (1, lanes), 1)
 
     def place_taps(ref, slot, act):
         act = act.astype(BF16)
@@ -246,13 +298,7 @@
         ref[pl.ds(slot * depth + channels, channels), :] = act
         ref[pl.ds(slot * depth + 2 * channels, channels), :] = pltpu.roll(act, lanes - 1, 1)
 
-    def inside(row):
-        at = first_row + row
-        return in_column & (at >= 0) & (at < BINS)
-
     for row in range(height + 2 * margin):
-        apart = jnp.abs(step - row).astype(F32)
-        decay = jnp.log1p(apart)
         tiles = []
         for tile in range(lanes // LANES):
             piece = None
@@ -264,43 +310,29 @@
                 spread = jnp.broadcast_to(left[b][:, row : row + 1], (channels, LANES))
                 piece = spread if piece is None else jnp.where(here >= low, spread, piece)
             tiles.append(piece)
-        mixed = jnp.concatenate(tiles, axis=1) + right - rate * decay
-        place_taps(taps_a, row, jnp.where(inside(row), jnp.maximum(mixed, 0.0), 0.0))
+        mixed = jnp.concatenate(tiles, axis=1) + right - rate * decay_ref[pl.ds(row, 1), :]
+        place_taps(taps_a, row, jnp.maximum(mixed, 0.0) * inside_ref[pl.ds(row, 1), :])
 
     for first in range(0, height + 2, groups):
         span = min(groups, height + 2 - first)
-        conv = dot(conv_a[span], taps_a[pl.ds(first * depth, (span + 2) * depth), :])
-        update = dot(mix_a[span], jnp.maximum(conv, 0.0).astype(BF16))
+        conv = dot(conv_a[span][...], taps_a[pl.ds(first * depth, (span + 2) * depth), :])
+        update = dot(mix_a[span][...], jnp.maximum(conv, 0.0).astype(BF16))
         for r in range(span):
             row = first + r
             kept = taps_a[pl.ds((row + 1) * depth + channels, channels), :].astype(F32)
             grid = kept + update[r * channels : (r + 1) * channels]
             if 1 <= row <= height:
                 grid_ref[pl.ds((row - 1) * channels, channels), :] = grid
-            place_taps(taps_b, row, jnp.where(inside(row + 1), jnp.maximum(grid, 0.0), 0.0))
+            place_taps(taps_b, row, jnp.maximum(grid, 0.0) * inside_ref[pl.ds(row + 1, 1), :])
     for first in range(0, height, groups):
         span = min(groups, height - first)
-        conv = dot(conv_b[span], taps_b[pl.ds(first * depth, (span + 2) * depth), :])
-        update = dot(mix_b[span], jnp.maximum(conv, 0.0).astype(BF16))
+        conv = dot(conv_b[span][...], taps_b[pl.ds(first * depth, (span + 2) * depth), :])
+        update = dot(mix_b[span][...], jnp.maximum(conv, 0.0).astype(BF16))
         rows = pl.ds(first * channels, span * channels)
         final_ref[rows, :] = jnp.maximum(grid_ref[rows, :] + update, 0.0).astype(BF16)
-    targets = head.shape[0] // height
-    contact = dot(head, final_ref[...]).reshape(targets, height, lanes)
-
-    local = lax.broadcasted_iota(jnp.int32, (height, BINS), 0)
-    ahead = lax.broadcasted_iota(jnp.int32, (height, BINS), 1)
-    weight_sum = jnp.zeros((height, BINS), F32)
-    weights = []
-    for b in range(BLOCKS):
-        weight = jnp.where(ahead == STRIDE * b + tower_row + local, stitch_ref[...], 0)
-        weight = jnp.sum(weight.astype(F32), axis=1, keepdims=True)
-        weight = jnp.where(place_ref[1] >= b, weight, 0.0)
-        reach = STRIDE * b + tower_row + local + ahead < BINS
-        weight = jnp.where(reach, weight, 0.0)
-        weights.append(weight)
-        weight_sum = weight_sum + weight
-    scale = 1.0 / jnp.maximum(weight_sum, 1.0)
-    weights = [w * scale for w in weights]
+    targets = head_ref.shape[0] // height
+    contact = dot(head_ref[...], final_ref[...]).reshape(targets, height, lanes)
+
     stitched = []
     map_row = lax.broadcasted_iota(jnp.int32, (height, lanes), 0)
     for t in range(targets):
@@ -314,7 +346,7 @@
             piece = skewed[:, first : first + reach]
             if reach < BINS:
                 piece = jnp.concatenate([piece, jnp.zeros((height, BINS - reach), F32)], axis=1)
-            piece = piece * weights[b]
+            piece = piece * stitch_ref[b]
             band = piece if band is None else band + piece
         stitched_ref[t] = band
         stitched.append(band[:, : 2 * STRIDE])
@@ -345,7 +377,11 @@
         own = jnp.where(here == there, down[t * height : (t + 1) * height], 0.0)
         down_rows.append(jnp.sum(own, axis=0, keepdims=True))
     rows = by_row(square) + by_row(contact)
-    keep_ref[...] = jnp.concatenate(rows + down_rows, axis=0)
+    own = (place_ref[1] * (STRIDE // height) + place_ref[0]) * height
+    missing = STRIDE - own - lax.broadcasted_iota(jnp.int32, (1, LANES), 1)
+    missing = jnp.maximum(missing, 0).astype(F32)
+    up_rows = [row + missing for row in rows[targets:]]
+    keep_ref[...] = jnp.concatenate(rows[:targets] + up_rows + down_rows, axis=0)
     per_row = LANES // height
     first = lax.broadcasted_iota(jnp.int32, (per_row, LANES), 1) < height
     packs = [
@@ -366,7 +402,7 @@
         send_ref[lax.rem(place_ref[0] + k, STRIDE // height)] = jnp.concatenate(packed, axis=0)
 
 
-def finish_kernel(height, place_ref, keep_ref, got_ref, out_ref):
+def finish_kernel(height, keep_ref, got_ref, out_ref):
     targets = out_ref.shape[0]
     per_row = LANES // height
     keep = keep_ref[...][:, :height]
@@ -376,9 +412,7 @@
         at = (q % per_row) * height
         rows.append(got[q // per_row : q // per_row + 1, at : at + height])
     sums = keep[: 2 * targets] + jnp.concatenate(rows, axis=0)
-    own = place_ref[1] * (STRIDE // height) + place_ref[0]
-    row = own * height + lax.broadcasted_iota(jnp.int32, (targets, height), 1)
-    upstream = sums[targets:] + jnp.maximum(STRIDE - row, 0).astype(F32)
+    upstream = sums[targets:]
     downstream = keep[2 * targets :]
     insulation = sums[:targets] / (STRIDE * STRIDE)
     direction = (downstream - upstream) / (downstream + upstream)
@@ -412,6 +446,39 @@
     packs = -(-2 * targets * height // LANES)
     vmem = pl.BlockSpec(memory_space=pltpu.VMEM)
     smem = pl.BlockSpec(memory_space=pltpu.SMEM)
+    layers, mid, width = trunk_in.shape
+    rows = height + 4
+    shapes = [
+        jax.ShapeDtypeStruct((layers, 3 * mid, width // 3), BF16),
+        jax.ShapeDtypeStruct((channels, LANES), F32),
+        jax.ShapeDtypeStruct((rows, lanes), F32),
+        jax.ShapeDtypeStruct((rows, lanes), F32),
+        jax.ShapeDtypeStruct((targets * height, height * channels), BF16),
+        jax.ShapeDtypeStruct((BLOCKS, height, BINS), F32),
+    ]
+    for count in (height + 2, height):
+        for span in spans_of(count, groups):
+            tall = span * channels
+            shapes.append(jax.ShapeDtypeStruct((tall, (span + 2) * 3 * channels), BF16))
+            shapes.append(jax.ShapeDtypeStruct((tall, tall), BF16))
+    prepared = pl.pallas_call(
+        functools.partial(prepare_kernel, height, groups),
+        out_shape=shapes,
+        in_specs=[smem, pl.BlockSpec(memory_space=pltpu.HBM)] + [vmem] * 6,
+        out_specs=[vmem] * len(shapes),
+        compiler_params=pltpu.CompilerParams(vmem_limit_bytes=8 * 1024 * 1024),
+        cost_estimate=pl.CostEstimate(flops=10**9, bytes_accessed=1 << 22, transcendentals=0),
+        name="prepare",
+    )(
+        place,
+        own,
+        trunk_in,
+        distance_rate.reshape(1, channels),
+        tower_conv,
+        tower_mix,
+        head_weight,
+        stitch_weight.reshape(1, BINS),
+    )
     stitched, keep, send = pl.pallas_call(
         functools.partial(main_kernel, height, groups),
         out_shape=[
@@ -419,28 +486,17 @@
             jax.ShapeDtypeStruct((3 * targets, LANES), F32),
             jax.ShapeDtypeStruct((towers, packs, LANES), F32),
         ],
-        in_specs=[smem] + [vmem] * 9,
+        in_specs=[smem] + [vmem] * (3 + len(shapes)),
         out_specs=[vmem] * 3,
         scratch_shapes=[
-            pltpu.VMEM(((height + 4) * 3 * channels, lanes), BF16),
+            pltpu.VMEM((rows * 3 * channels, lanes), BF16),
             pltpu.VMEM(((height + 2) * 3 * channels, lanes), BF16),
             pltpu.VMEM((height * channels, lanes), F32),
             pltpu.VMEM((height * channels, lanes), BF16),
         ],
         compiler_params=pltpu.CompilerParams(vmem_limit_bytes=VMEM_BYTES),
         name="windows",
-    )(
-        place,
-        features,
-        trunk_in,
-        jnp.transpose(trunk_out, (0, 2, 1)),
-        pair_weight,
-        distance_rate.reshape(1, channels),
-        tower_conv,
-        tower_mix,
-        head_weight,
-        stitch_weight.reshape(1, BINS),
-    )
+    )(place, features, jnp.transpose(trunk_out, (0, 2, 1)), pair_weight, *prepared)
     starts = lax.axis_size("genome")
     passed = lax.ppermute(send, "genome", [(i, i + 1) for i in range(starts - 1)])
     ahead = (jnp.arange(towers) > tower_index)[:, None, None]
@@ -448,11 +504,11 @@
     scores = pl.pallas_call(
         functools.partial(finish_kernel, height),
         out_shape=jax.ShapeDtypeStruct((targets, 2, height), F32),
-        in_specs=[smem, vmem, vmem],
+        in_specs=[vmem, vmem],
         out_specs=vmem,
         compiler_params=pltpu.CompilerParams(vmem_limit_bytes=2 * 1024 * 1024),
         name="finish",
-    )(place, keep, got)
+    )(keep, got)
     return (stitched, jnp.transpose(scores, (1, 0, 2)))
 
 

time: 40.1 us -> 39.4 us (0.983)
  waiting for transfers between devices: 8.35 us -> 6.39 us
  local copies, waits for them, and re-layouts: 0.03 us -> 0.92 us
    all_to_all x1, waiting for transfers between devices: 7.05 us -> 5.09 us  [per_device(): features = lax.all_to_all(own, 'genome', 0, 0, tiled=True)]
    pallas_call x0 -> x1, Pallas kernels: none -> 1.02 us  [per_device(): pl.pallas_call(functools.partial(prepare_kernel, height, groups), out_sha...]
    unnamed x16 -> x18, local copies, waits for them, and re-layouts: 0.03 us -> 0.92 us
    pallas_call x1, Pallas kernels: 1.23 us -> 0.69 us  [per_device(): pl.pallas_call(functools.partial(finish_kernel, height), out_shape=jax.Sh...]
  transfers between devices with their start and end apart: 2 -> 2, of which waited for: 2 -> 2; matrix products, arithmetic and copies ran while one was open for 0% -> 0% of each run, Pallas kernels for 0% -> 3%
where the time goes in v7:
time: 39.4 us; the launch traced here: 39.1 us
  Pallas kernels  15 us (38%)
  starting transfers between devices  9.48 us (24%)
  waiting for transfers between devices  6.39 us (16%)
  blocking collectives  6.35 us (16%)
  local copies, waits for them, and re-layouts  0.92 us (2%)
  between operations  0.74 us (2%)
    pallas_call x1, Pallas kernels, per_device(): pl.pallas_call(functools.partial(main_kernel, height, groups), out_shape=...  9.51 us
    all_to_all x1, starting transfers between devices, per_device(): features = lax.all_to_all(own, 'genome', 0, 0, tiled=True)  7.29 us
    all_to_all x1, blocking collectives, per_device(): lax.all_to_all(jnp.where(ahead, send, passed), 'tower', 0, 0, tiled=True)  6.35 us
    all_to_all x1, waiting for transfers between devices, per_device(): features = lax.all_to_all(own, 'genome', 0, 0, tiled=True)  5.09 us
    pallas_call x1, Pallas kernels, stem(): pl.pallas_call(functools.partial(stem_kernel, bins), out_shape=jax.ShapeD...  3.82 us
    ppermute x1, starting transfers between devices, per_device(): lax.ppermute(send, 'genome', [(i, i + 1) for i in range(starts - 1)])  2.19 us
    ppermute x1, waiting for transfers between devices, per_device(): lax.ppermute(send, 'genome', [(i, i + 1) for i in range(starts - 1)])  1.3 us
    pallas_call x1, Pallas kernels, per_device(): pl.pallas_call(functools.partial(prepare_kernel, height, groups), out_sha...  1.02 us
  transfers between devices with their start and end apart: 2, of which 2 were waited for; matrix products, arithmetic and copies ran while one was open for 0% of the time, Pallas kernels for 3%

profile of v7, /device:TPU:0, one launch (start us, length us, event | category | flops | bytes accessed | tf_op | source)
XLA Modules:
  0.0 39.1 jit_solution(4535242592522367248)
XLA Ops:
  0.6 0.0 copy-start.6
  0.6 0.0 copy-start.5
  0.7 0.0 copy-start.4
  0.7 0.0 copy-start.8
  0.7 0.0 copy-start.3
  0.7 0.0 copy-start.7
  0.7 3.8 %stem.1._ = bf16[8,48,128]{2,1,0:T(8,128)(2,1)} custom-call(s32[1024,128]{1,0:T(8,128)} %bitcast.10, bf16[96,8192]{1,0:T(8,128)(2,1)} %weight_hbm.1), custom_call_target="tpu_custom_call" | custom-call | tf_op jit(solution)/shard_map/stem/pallas_call | solution.py:67
  4.5 7.3 %all-to-all-start = ((bf16[8,48,128]{2,1,0:T(8,128)(2,1)}), bf16[8,48,128]{2,1,0:T(8,128)(2,1)S(1)}, u32[]{:S(2)}, u32[]{:S(2)}) async-start(bf16[8,48,128]{2,1,0:T(8,128)(2,1)} %stem.1._), calls=%async_computation | async-start | bytes 196608 | tf_op jit(solution)/shard_map/all_to_all | solution.py:440
  11.8 0.1 pad_add_fusion.place_ref
  11.9 0.0 copy-done.6
  11.9 0.0 copy-done.5
  11.9 0.0 copy-done.4
  11.9 0.0 copy-done.8
  11.9 0.0 copy-done.3
  11.9 0.0 copy-done.7
  11.9 0.0 copy-start
  11.9 0.9 %copy-done = bf16[8,48,128]{2,1,0:T(8,128)(2,1)S(1)} copy-done((bf16[8,48,128]{2,1,0:T(8,128)(2,1)S(1)}, bf16[8,48,128]{2,1,0:T(8,128)(2,1)}, u32[]{:S(2)}) %copy-start) | copy-done | bytes 98328
  12.8 0.0 copy-start.1
  12.8 0.0 copy-start.2
  12.8 1.0 %prepare.1 = (bf16[6,144,96]{2,1,0:T(8,128)(2,1)S(1)}, f32[48,128]{1,0:T(8,128)S(1)}, f32[20,768]{1,0:T(8,128)S(1)}, f32[20,768]{1,0:T(8,128)S(1)}, bf16[80,768]...) custom-call(s32[2]{0:T(128)S(1)} %pad_add_fusion.place_ref, ...), custom_call_target="tpu_custom_call" | custom-call | flops 1000000000 | bytes 4194304 | tf_op jit(solution)/shard_map/prepare/pallas_call | solution.py:464
  13.8 5.1 %all-to-all-done.features = bf16[8,48,128]{2,1,0:T(8,128)(2,1)S(1)} async-done(((bf16[8,48,128]{2,1,0:T(8,128)(2,1)}), bf16[8,48,128]{2,1,0:T(8,128)(2,1)S(1)}, u32[]{:S(2)}, u32[]{:S(2)}) %all-to-all-start) | async-done | bytes 98336 | tf_op jit(solution)/shard_map/all_to_all | solution.py:440
  18.9 0.0 copy-done.1
  18.9 0.0 copy-done.2
  18.9 9.5 %windows.1 = (f32[5,16,256]{2,1,0:T(8,128)}, f32[15,128]{1,0:T(8,128)S(1)}, f32[4,2,128]{2,1,0:T(2,128)S(1)}) custom-call(s32[2]{0:T(128)S(1)} %pad_add_fusion.place_ref, bf16[8,48,128]{2,1,0:T(8,128)(2,1)S(1)} %all-to-all-done.features, bf16[6,48,96]{2,1,0:T(8,128)(2,1)S(1)} %bitcast.7, bf16[96,96]{1,0:T(8,128)(2,1)S(1)} %copy-done.2, ...), custom_call_target="tpu_custom_call" | custom-call | tf_op jit(solution)/shard_map/windows/pallas_call | solution.py:482
  28.5 2.2 %collective-permute-start = (f32[4,2,128]{2,1,0:T(2,128)S(1)}, f32[4,2,128]{2,1,0:T(2,128)S(1)}, u32[]{:S(2)}, u32[]{:S(2)}) collective-permute-start(f32[4,2,128]{2,1,0:T(2,128)S(1)} %get-tuple-element.31), channel_id=1, source_target_pairs={{0,4},{4,8},{8,12},{12,16},{16,20},{20,24},{24,28},{1,5},{5,9},{9,... | collective-permute-start | bytes 12296 | tf_op jit(solution)/shard_map/ppermute | solution.py:501
  30.7 1.3 %collective-permute-done = f32[4,2,128]{2,1,0:T(2,128)S(1)} collective-permute-done((f32[4,2,128]{2,1,0:T(2,128)S(1)}, f32[4,2,128]{2,1,0:T(2,128)S(1)}, u32[]{:S(2)}, u32[]{:S(2)}) %collective-permute-start) | collective-permute-done | bytes 4128 | tf_op jit(solution)/shard_map/ppermute | solution.py:501
  32.0 0.1 broadcast_select_fusion
  32.0 6.4 %all_to_all.10.got_ref = f32[4,2,128]{2,1,0:T(2,128)S(1)} all-to-all(f32[4,2,128]{2,1,0:T(2,128)S(1)} %broadcast_select_fusion), channel_id=1, replica_groups=mesh['genome'=8,'tower'=4] {'tower'}, dimensions={0} | all-to-all | bytes 8192 | tf_op jit(solution)/shard_map/all_to_all | solution.py:503
  38.4 0.7 %finish.1 = f32[5,2,16]{2,1,0:T(2,128)} custom-call(f32[15,128]{1,0:T(8,128)S(1)} %get-tuple-element.30.keep_ref, f32[4,2,128]{2,1,0:T(2,128)S(1)} %all_to_all.10.got_ref), custom_call_target="tpu_custom_call" | custom-call | tf_op jit(solution)/shard_map/finish/pallas_call | solution.py:504
  (1 shorter events, 0.0 us)
Async XLA Ops:
  0.6 11.3 %copy-start.6 = (bf16[5,48]{1,0:T(8,128)(2,1)S(1)}, bf16[5,48]{1,0:T(8,128)(2,1)}, u32[]{:S(2)}) copy-start(bf16[5,48]{1,0:T(8,128)(2,1)} %head_in.1) | copy-start | bytes 1444
  0.6 11.3 %copy-start.5 = (bf16[2,48,48]{2,1,0:T(8,128)(2,1)S(1)}, bf16[2,48,48]{2,1,0:T(8,128)(2,1)}, u32[]{:S(2)}) copy-start(bf16[2,48,48]{2,1,0:T(8,128)(2,1)} %mix_in.1) | copy-start | bytes 27652
  0.7 11.2 %copy-start.4 = (bf16[2,3,48,144]{3,2,1,0:T(8,128)(2,1)S(1)}, bf16[2,3,48,144]{3,2,1,0:T(8,128)(2,1)}, u32[]{:S(2)}) copy-start(bf16[2,3,48,144]{3,2,1,0:T(8,128)(2,1)} %conv_in.1) | copy-start | bytes 248836
  0.7 11.2 %copy-start.8 = (f32[48]{0:T(128)S(1)}, f32[48]{0:T(128)}, u32[]{:S(2)}) copy-start(f32[48]{0:T(128)} %param.16) | copy-start | bytes 580
  0.7 11.2 %copy-start.3 = (bf16[6,48,288]{2,1,0:T(8,128)(2,1)S(1)}, bf16[6,48,288]{2,1,0:T(8,128)(2,1)}, u32[]{:S(2)}) copy-start(bf16[6,48,288]{2,1,0:T(8,128)(2,1)} %trunk_in.1) | copy-start | bytes 497668
  0.7 11.2 %copy-start.7 = (s32[256]{0:T(256)S(1)}, s32[256]{0:T(256)}, u32[]{:S(2)}) copy-start(s32[256]{0:T(256)} %param.11) | copy-start | bytes 3076
  4.5 14.4 %all-to-all-start = ((bf16[8,48,128]{2,1,0:T(8,128)(2,1)}), bf16[8,48,128]{2,1,0:T(8,128)(2,1)S(1)}, u32[]{:S(2)}, u32[]{:S(2)}) async-start(bf16[8,48,128]{2,1,0:T(8,128)(2,1)} %stem.1._), calls=%async_computation | async-start | bytes 196608 | tf_op jit(solution)/shard_map/all_to_all | solution.py:440
  11.9 0.9 %copy-start = (bf16[8,48,128]{2,1,0:T(8,128)(2,1)S(1)}, bf16[8,48,128]{2,1,0:T(8,128)(2,1)}, u32[]{:S(2)}) copy-start(bf16[8,48,128]{2,1,0:T(8,128)(2,1)} %stem.1._) | copy-start | bytes 294916
  12.8 6.1 %copy-start.1 = (bf16[6,96,48]{1,2,0:T(8,128)(2,1)S(1)}, bf16[6,96,48]{1,2,0:T(8,128)(2,1)}, u32[]{:S(2)}) copy-start(bf16[6,96,48]{1,2,0:T(8,128)(2,1)} %param.14) | copy-start | bytes 165892
  12.8 6.1 %copy-start.2 = (bf16[96,96]{1,0:T(8,128)(2,1)S(1)}, bf16[96,96]{1,0:T(8,128)(2,1)}, u32[]{:S(2)}) copy-start(bf16[96,96]{1,0:T(8,128)(2,1)} %pair_weight.1) | copy-start | bytes 55300
  28.5 3.5 %collective-permute-start = (f32[4,2,128]{2,1,0:T(2,128)S(1)}, f32[4,2,128]{2,1,0:T(2,128)S(1)}, u32[]{:S(2)}, u32[]{:S(2)}) collective-permute-start(f32[4,2,128]{2,1,0:T(2,128)S(1)} %get-tuple-element.31), channel_id=1, source_target_pairs={{0,4},{4,8},{8,12},{12,16},{16,20},{20,24},{24,28},{1,5},{5,9},{9,... | collective-permute-start | bytes 12296 | tf_op jit(solution)/shard_map/ppermute | solution.py:501

commit v8 on v7

--- a/solution.py
+++ b/solution.py
@@ -232,7 +232,7 @@
         conv_a[span], mix_a[span] = rest.pop(0), rest.pop(0)
     for span in spans_of(height, groups):
         conv_b[span], mix_b[span] = rest.pop(0), rest.pop(0)
-    stitched_ref, keep_ref, send_ref, taps_a, taps_b, grid_ref, final_ref = rest
+    stitched_ref, keep_ref, send_ref, taps_a, taps_b, grid_ref, final_ref, squeezed_ref = rest
 
     starts = features.shape[0]
     blocks = []
@@ -313,10 +313,20 @@
         mixed = jnp.concatenate(tiles, axis=1) + right - rate * decay_ref[pl.ds(row, 1), :]
         place_taps(taps_a, row, jnp.maximum(mixed, 0.0) * inside_ref[pl.ds(row, 1), :])
 
+    def convolve(kernels, taps, rows):
+        for first in range(0, rows, groups):
+            span = min(groups, rows - first)
+            conv = dot(kernels[span][...], taps[pl.ds(first * depth, (span + 2) * depth), :])
+            squeezed_ref[pl.ds(first * channels, span * channels), :] = jnp.maximum(
+                conv, 0.0
+            ).astype(BF16)
+
+    convolve(conv_a, taps_a, height + 2)
     for first in range(0, height + 2, groups):
         span = min(groups, height + 2 - first)
-        conv = dot(conv_a[span][...], taps_a[pl.ds(first * depth, (span + 2) * depth), :])
-        update = dot(mix_a[span][...], jnp.maximum(conv, 0.0).astype(BF16))
+        update = dot(
+            mix_a[span][...], squeezed_ref[pl.ds(first * channels, span * channels), :]
+        )
         for r in range(span):
             row = first + r
             kept = taps_a[pl.ds((row + 1) * depth + channels, channels), :].astype(F32)
@@ -324,11 +334,11 @@
             if 1 <= row <= height:
                 grid_ref[pl.ds((row - 1) * channels, channels), :] = grid
             place_taps(taps_b, row, jnp.maximum(grid, 0.0) * inside_ref[pl.ds(row + 1, 1), :])
+    convolve(conv_b, taps_b, height)
     for first in range(0, height, groups):
         span = min(groups, height - first)
-        conv = dot(conv_b[span][...], taps_b[pl.ds(first * depth, (span + 2) * depth), :])
-        update = dot(mix_b[span][...], jnp.maximum(conv, 0.0).astype(BF16))
         rows = pl.ds(first * channels, span * channels)
+        update = dot(mix_b[span][...], squeezed_ref[rows, :])
         final_ref[rows, :] = jnp.maximum(grid_ref[rows, :] + update, 0.0).astype(BF16)
     targets = head_ref.shape[0] // height
     contact = dot(head_ref[...], final_ref[...]).reshape(targets, height, lanes)
@@ -493,6 +503,7 @@
             pltpu.VMEM(((height + 2) * 3 * channels, lanes), BF16),
             pltpu.VMEM((height * channels, lanes), F32),
             pltpu.VMEM((height * channels, lanes), BF16),
+            pltpu.VMEM(((height + 2) * channels, lanes), BF16),
         ],
         compiler_params=pltpu.CompilerParams(vmem_limit_bytes=VMEM_BYTES),
         name="windows",

time: 39.4 us -> 39.4 us (level)
  no operation moved by 1% of the time
where the time goes in v8:
time: 39.4 us; the launch traced here: 39.1 us
  Pallas kernels  15 us (38%)
  starting transfers between devices  9.48 us (24%)
  waiting for transfers between devices  6.39 us (16%)
  blocking collectives  6.34 us (16%)
  local copies, waits for them, and re-layouts  0.92 us (2%)
  between operations  0.74 us (2%)
    pallas_call x1, Pallas kernels, per_device(): pl.pallas_call(functools.partial(main_kernel, height, groups), out_shape=...  9.52 us
    all_to_all x1, starting transfers between devices, per_device(): features = lax.all_to_all(own, 'genome', 0, 0, tiled=True)  7.29 us
    all_to_all x1, blocking collectives, per_device(): lax.all_to_all(jnp.where(ahead, send, passed), 'tower', 0, 0, tiled=True)  6.34 us
    all_to_all x1, waiting for transfers between devices, per_device(): features = lax.all_to_all(own, 'genome', 0, 0, tiled=True)  5.09 us
    pallas_call x1, Pallas kernels, stem(): pl.pallas_call(functools.partial(stem_kernel, bins), out_shape=jax.ShapeD...  3.82 us
    ppermute x1, starting transfers between devices, per_device(): lax.ppermute(send, 'genome', [(i, i + 1) for i in range(starts - 1)])  2.19 us
    ppermute x1, waiting for transfers between devices, per_device(): lax.ppermute(send, 'genome', [(i, i + 1) for i in range(starts - 1)])  1.3 us
    pallas_call x1, Pallas kernels, per_device(): pl.pallas_call(functools.partial(prepare_kernel, height, groups), out_sha...  1.02 us
  transfers between devices with their start and end apart: 2, of which 2 were waited for; matrix products, arithmetic and copies ran while one was open for 0% of the time, Pallas kernels for 3%

profile of v8, /device:TPU:0, one launch (start us, length us, event | category | flops | bytes accessed | tf_op | source)
XLA Modules:
  0.0 39.1 jit_solution(8981617227031796746)
XLA Ops:
  0.6 0.0 copy-start.6
  0.6 0.0 copy-start.5
  0.7 0.0 copy-start.4
  0.7 0.0 copy-start.8
  0.7 0.0 copy-start.3
  0.7 0.0 copy-start.7
  0.7 3.8 %stem.1._ = bf16[8,48,128]{2,1,0:T(8,128)(2,1)} custom-call(s32[1024,128]{1,0:T(8,128)} %bitcast.10, bf16[96,8192]{1,0:T(8,128)(2,1)} %weight_hbm.1), custom_call_target="tpu_custom_call" | custom-call | tf_op jit(solution)/shard_map/stem/pallas_call | solution.py:67
  4.5 7.3 %all-to-all-start = ((bf16[8,48,128]{2,1,0:T(8,128)(2,1)}), bf16[8,48,128]{2,1,0:T(8,128)(2,1)S(1)}, u32[]{:S(2)}, u32[]{:S(2)}) async-start(bf16[8,48,128]{2,1,0:T(8,128)(2,1)} %stem.1._), calls=%async_computation | async-start | bytes 196608 | tf_op jit(solution)/shard_map/all_to_all | solution.py:450
  11.8 0.1 pad_add_fusion.place_ref
  11.9 0.0 copy-done.6
  11.9 0.0 copy-done.5
  11.9 0.0 copy-done.4
  11.9 0.0 copy-done.8
  11.9 0.0 copy-done.3
  11.9 0.0 copy-done.7
  11.9 0.0 copy-start
  11.9 0.9 %copy-done = bf16[8,48,128]{2,1,0:T(8,128)(2,1)S(1)} copy-done((bf16[8,48,128]{2,1,0:T(8,128)(2,1)S(1)}, bf16[8,48,128]{2,1,0:T(8,128)(2,1)}, u32[]{:S(2)}) %copy-start) | copy-done | bytes 98328
  12.8 0.0 copy-start.1
  12.8 0.0 copy-start.2
  12.8 1.0 %prepare.1 = (bf16[6,144,96]{2,1,0:T(8,128)(2,1)S(1)}, f32[48,128]{1,0:T(8,128)S(1)}, f32[20,768]{1,0:T(8,128)S(1)}, f32[20,768]{1,0:T(8,128)S(1)}, bf16[80,768]...) custom-call(s32[2]{0:T(128)S(1)} %pad_add_fusion.place_ref, ...), custom_call_target="tpu_custom_call" | custom-call | flops 1000000000 | bytes 4194304 | tf_op jit(solution)/shard_map/prepare/pallas_call | solution.py:474
  13.8 5.1 %all-to-all-done.features = bf16[8,48,128]{2,1,0:T(8,128)(2,1)S(1)} async-done(((bf16[8,48,128]{2,1,0:T(8,128)(2,1)}), bf16[8,48,128]{2,1,0:T(8,128)(2,1)S(1)}, u32[]{:S(2)}, u32[]{:S(2)}) %all-to-all-start) | async-done | bytes 98336 | tf_op jit(solution)/shard_map/all_to_all | solution.py:450
  18.9 0.0 copy-done.1
  18.9 0.0 copy-done.2
  18.9 9.5 %windows.1 = (f32[5,16,256]{2,1,0:T(8,128)}, f32[15,128]{1,0:T(8,128)S(1)}, f32[4,2,128]{2,1,0:T(2,128)S(1)}) custom-call(s32[2]{0:T(128)S(1)} %pad_add_fusion.place_ref, bf16[8,48,128]{2,1,0:T(8,128)(2,1)S(1)} %all-to-all-done.features, bf16[6,48,96]{2,1,0:T(8,128)(2,1)S(1)} %bitcast.7, bf16[96,96]{1,0:T(8,128)(2,1)S(1)} %copy-done.2, ...), custom_call_target="tpu_custom_call" | custom-call | tf_op jit(solution)/shard_map/windows/pallas_call | solution.py:492
  28.5 2.2 %collective-permute-start = (f32[4,2,128]{2,1,0:T(2,128)S(1)}, f32[4,2,128]{2,1,0:T(2,128)S(1)}, u32[]{:S(2)}, u32[]{:S(2)}) collective-permute-start(f32[4,2,128]{2,1,0:T(2,128)S(1)} %get-tuple-element.31), channel_id=1, source_target_pairs={{0,4},{4,8},{8,12},{12,16},{16,20},{20,24},{24,28},{1,5},{5,9},{9,... | collective-permute-start | bytes 12296 | tf_op jit(solution)/shard_map/ppermute | solution.py:512
  30.7 1.3 %collective-permute-done = f32[4,2,128]{2,1,0:T(2,128)S(1)} collective-permute-done((f32[4,2,128]{2,1,0:T(2,128)S(1)}, f32[4,2,128]{2,1,0:T(2,128)S(1)}, u32[]{:S(2)}, u32[]{:S(2)}) %collective-permute-start) | collective-permute-done | bytes 4128 | tf_op jit(solution)/shard_map/ppermute | solution.py:512
  32.0 0.1 broadcast_select_fusion
  32.0 6.3 %all_to_all.10.got_ref = f32[4,2,128]{2,1,0:T(2,128)S(1)} all-to-all(f32[4,2,128]{2,1,0:T(2,128)S(1)} %broadcast_select_fusion), channel_id=1, replica_groups=mesh['genome'=8,'tower'=4] {'tower'}, dimensions={0} | all-to-all | bytes 8192 | tf_op jit(solution)/shard_map/all_to_all | solution.py:514
  38.4 0.7 %finish.1 = f32[5,2,16]{2,1,0:T(2,128)} custom-call(f32[15,128]{1,0:T(8,128)S(1)} %get-tuple-element.30.keep_ref, f32[4,2,128]{2,1,0:T(2,128)S(1)} %all_to_all.10.got_ref), custom_call_target="tpu_custom_call" | custom-call | tf_op jit(solution)/shard_map/finish/pallas_call | solution.py:515
  (1 shorter events, 0.0 us)
Async XLA Ops:
  0.6 11.3 %copy-start.6 = (bf16[5,48]{1,0:T(8,128)(2,1)S(1)}, bf16[5,48]{1,0:T(8,128)(2,1)}, u32[]{:S(2)}) copy-start(bf16[5,48]{1,0:T(8,128)(2,1)} %head_in.1) | copy-start | bytes 1444
  0.6 11.3 %copy-start.5 = (bf16[2,48,48]{2,1,0:T(8,128)(2,1)S(1)}, bf16[2,48,48]{2,1,0:T(8,128)(2,1)}, u32[]{:S(2)}) copy-start(bf16[2,48,48]{2,1,0:T(8,128)(2,1)} %mix_in.1) | copy-start | bytes 27652
  0.7 11.2 %copy-start.4 = (bf16[2,3,48,144]{3,2,1,0:T(8,128)(2,1)S(1)}, bf16[2,3,48,144]{3,2,1,0:T(8,128)(2,1)}, u32[]{:S(2)}) copy-start(bf16[2,3,48,144]{3,2,1,0:T(8,128)(2,1)} %conv_in.1) | copy-start | bytes 248836
  0.7 11.2 %copy-start.8 = (f32[48]{0:T(128)S(1)}, f32[48]{0:T(128)}, u32[]{:S(2)}) copy-start(f32[48]{0:T(128)} %param.16) | copy-start | bytes 580
  0.7 11.2 %copy-start.3 = (bf16[6,48,288]{2,1,0:T(8,128)(2,1)S(1)}, bf16[6,48,288]{2,1,0:T(8,128)(2,1)}, u32[]{:S(2)}) copy-start(bf16[6,48,288]{2,1,0:T(8,128)(2,1)} %trunk_in.1) | copy-start | bytes 497668
  0.7 11.2 %copy-start.7 = (s32[256]{0:T(256)S(1)}, s32[256]{0:T(256)}, u32[]{:S(2)}) copy-start(s32[256]{0:T(256)} %param.11) | copy-start | bytes 3076
  4.5 14.4 %all-to-all-start = ((bf16[8,48,128]{2,1,0:T(8,128)(2,1)}), bf16[8,48,128]{2,1,0:T(8,128)(2,1)S(1)}, u32[]{:S(2)}, u32[]{:S(2)}) async-start(bf16[8,48,128]{2,1,0:T(8,128)(2,1)} %stem.1._), calls=%async_computation | async-start | bytes 196608 | tf_op jit(solution)/shard_map/all_to_all | solution.py:450
  11.9 0.9 %copy-start = (bf16[8,48,128]{2,1,0:T(8,128)(2,1)S(1)}, bf16[8,48,128]{2,1,0:T(8,128)(2,1)}, u32[]{:S(2)}) copy-start(bf16[8,48,128]{2,1,0:T(8,128)(2,1)} %stem.1._) | copy-start | bytes 294916
  12.8 6.1 %copy-start.1 = (bf16[6,96,48]{1,2,0:T(8,128)(2,1)S(1)}, bf16[6,96,48]{1,2,0:T(8,128)(2,1)}, u32[]{:S(2)}) copy-start(bf16[6,96,48]{1,2,0:T(8,128)(2,1)} %param.14) | copy-start | bytes 165892
  12.8 6.1 %copy-start.2 = (bf16[96,96]{1,0:T(8,128)(2,1)S(1)}, bf16[96,96]{1,0:T(8,128)(2,1)}, u32[]{:S(2)}) copy-start(bf16[96,96]{1,0:T(8,128)(2,1)} %pair_weight.1) | copy-start | bytes 55300
  28.5 3.5 %collective-permute-start = (f32[4,2,128]{2,1,0:T(2,128)S(1)}, f32[4,2,128]{2,1,0:T(2,128)S(1)}, u32[]{:S(2)}, u32[]{:S(2)}) collective-permute-start(f32[4,2,128]{2,1,0:T(2,128)S(1)} %get-tuple-element.31), channel_id=1, source_target_pairs={{0,4},{4,8},{8,12},{12,16},{16,20},{20,24},{24,28},{1,5},{5,9},{9,... | collective-permute-start | bytes 12296 | tf_op jit(solution)/shard_map/ppermute | solution.py:512

commit v9 on v8

--- a/solution.py
+++ b/solution.py
@@ -111,11 +111,15 @@
     return jnp.where(row == col, tall, jnp.zeros((), BF16)).reshape(targets * count, count * width)
 
 
-def segments(margin):
-    sizes = [BINS - STRIDE * b + margin + 1 for b in range(BLOCKS)]
-    offsets = [sum(sizes[:b]) for b in range(BLOCKS)]
+def segments(margin, height):
+    whole = [BINS - STRIDE * b + margin + 1 for b in range(BLOCKS)]
+    near = 2 * STRIDE + height - 1 + 2 * margin
+    parts = [(b, b, whole[b]) for b in range(BLOCKS)]
+    parts += [(b + 1, b, min(whole[b], near)) for b in range(BLOCKS)]
+    sizes = [part[2] for part in parts]
+    offsets = [sum(sizes[:k]) for k in range(len(sizes))]
     lanes = -(-sum(sizes) // LANES) * LANES
-    return sizes, offsets, lanes
+    return parts, offsets, lanes
 
 
 def shifted(values, offset):
@@ -152,7 +156,7 @@
     *conv_refs,
 ):
     margin = 2
-    sizes, offsets, lanes = segments(margin)
+    parts, offsets, lanes = segments(margin, height)
     tower_row = place_ref[0] * height
     for layer in range(trunk_in.shape[0]):
         flat = trunk_in[layer]
@@ -176,9 +180,9 @@
     lane = lax.broadcasted_iota(jnp.int32, (height + 2 * margin, lanes), 1)
     block_of = jnp.zeros((height + 2 * margin, lanes), jnp.int32)
     start_of = jnp.zeros((height + 2 * margin, lanes), jnp.int32)
-    for b in range(1, BLOCKS):
-        block_of = jnp.where(lane >= offsets[b], b, block_of)
-        start_of = jnp.where(lane >= offsets[b], offsets[b], start_of)
+    for (_, b, _), offset in zip(parts, offsets):
+        block_of = jnp.where(lane >= offset, b, block_of)
+        start_of = jnp.where(lane >= offset, offset, start_of)
     step = lane - start_of
     first_row = STRIDE * block_of + tower_row - margin
     column = first_row + step
@@ -191,19 +195,20 @@
 
     local = lax.broadcasted_iota(jnp.int32, (height, BINS), 0)
     ahead = lax.broadcasted_iota(jnp.int32, (height, BINS), 1)
-    weight_sum = jnp.zeros((height, BINS), F32)
-    weights = []
-    for b in range(BLOCKS):
-        weight = jnp.where(ahead == STRIDE * b + tower_row + local, stitch_in[...], 0)
-        weight = jnp.sum(weight.astype(F32), axis=1, keepdims=True)
-        weight = jnp.where(place_ref[1] >= b, weight, 0.0)
-        reach = STRIDE * b + tower_row + local + ahead < BINS
-        weight = jnp.where(reach, weight, 0.0)
-        weights.append(weight)
-        weight_sum = weight_sum + weight
-    scale = 1.0 / jnp.maximum(weight_sum, 1.0)
-    for b in range(BLOCKS):
-        stitch_ref[b] = weights[b] * scale
+    for back in range(2):
+        weight_sum = jnp.zeros((height, BINS), F32)
+        weights = []
+        for b in range(BLOCKS):
+            weight = jnp.where(ahead == STRIDE * b + tower_row + local, stitch_in[...], 0)
+            weight = jnp.sum(weight.astype(F32), axis=1, keepdims=True)
+            weight = jnp.where(place_ref[1] - back >= b, weight, 0.0)
+            reach = STRIDE * b + tower_row + local + ahead < BINS
+            weight = jnp.where(reach, weight, 0.0)
+            weights.append(weight)
+            weight_sum = weight_sum + weight
+        scale = 1.0 / jnp.maximum(weight_sum, 1.0)
+        for b in range(BLOCKS):
+            stitch_ref[back * BLOCKS + b] = weights[b] * scale
 
 
 def main_kernel(
@@ -222,7 +227,7 @@
     *rest,
 ):
     margin = 2
-    sizes, offsets, lanes = segments(margin)
+    parts, offsets, lanes = segments(margin, height)
     tower_row = place_ref[0] * height
     channels = rate_ref.shape[0]
     depth = 3 * channels
@@ -236,7 +241,7 @@
 
     starts = features.shape[0]
     blocks = []
-    for d in range(1 - BLOCKS, BLOCKS):
+    for d in range(-BLOCKS, BLOCKS):
         at = place_ref[1] + d
         block = features[jnp.clip(at, 0, starts - 1)]
         blocks.append(jnp.where((at >= 0) & (at < starts), block, jnp.zeros_like(block)))
@@ -249,8 +254,8 @@
     )
     extent = BINS
     windows = []
-    for b in range(BLOCKS):
-        first = (BLOCKS - 1 - b) * STRIDE
+    for b in range(BLOCKS + 1):
+        first = (BLOCKS - b) * STRIDE
         windows.append(blocks[:, first : first + BINS].astype(F32))
     stream = jnp.concatenate(windows, axis=1)
     layers = trunk_in.shape[0]
@@ -263,7 +268,7 @@
             [
                 shifted(taps[:mid, b * BINS : (b + 1) * BINS], -dilation)
                 + shifted(taps[2 * mid :, b * BINS : (b + 1) * BINS], dilation)
-                for b in range(BLOCKS)
+                for b in range(BLOCKS + 1)
             ],
             axis=1,
         )
@@ -275,17 +280,17 @@
 
     right = []
     left = []
-    for b in range(BLOCKS):
+    for window, b, size in parts:
         begin = STRIDE * b + tower_row - margin
         turn = jnp.where(begin > 0, BINS - begin, -begin)
-        terms = projected[:, b * BINS : (b + 1) * BINS]
+        terms = projected[:, window * BINS : (window + 1) * BINS]
         turned = pltpu.roll(terms, turn, 1)
         left.append(turned[:channels, :LANES])
         own = turned[channels:]
-        if sizes[b] > BINS:
-            own = jnp.concatenate([own, own[:, : sizes[b] - BINS]], axis=1)
-        right.append(own[:, : sizes[b]])
-    used = sum(sizes)
+        if size > BINS:
+            own = jnp.concatenate([own, own[:, : size - BINS]], axis=1)
+        right.append(own[:, :size])
+    used = sum(part[2] for part in parts)
     if lanes > used:
         right.append(jnp.zeros((channels, lanes - used), F32))
     right = jnp.concatenate(right, axis=1)
@@ -303,8 +308,8 @@
         for tile in range(lanes // LANES):
             piece = None
             here = lane[:, tile * LANES : (tile + 1) * LANES]
-            for b in range(BLOCKS):
-                low, high = offsets[b], offsets[b] + sizes[b]
+            for b in range(len(parts)):
+                low, high = offsets[b], offsets[b] + parts[b][2]
                 if high <= tile * LANES or low >= (tile + 1) * LANES:
                     continue
                 spread = jnp.broadcast_to(left[b][:, row : row + 1], (channels, LANES))
@@ -343,26 +348,30 @@
     targets = head_ref.shape[0] // height
     contact = dot(head_ref[...], final_ref[...]).reshape(targets, height, lanes)
 
-    stitched = []
+    wide = 2 * STRIDE
+    stitched, before = [], []
     map_row = lax.broadcasted_iota(jnp.int32, (height, lanes), 0)
     for t in range(targets):
-        band = None
         skewed = contact[t]
         for bit in range((height - 1).bit_length()):
             turned = pltpu.roll(skewed, lanes - (1 << bit), 1)
             skewed = jnp.where((map_row >> bit) & 1 == 1, turned, skewed)
-        for b in range(BLOCKS):
-            first, reach = offsets[b] + margin, BINS - STRIDE * b
-            piece = skewed[:, first : first + reach]
-            if reach < BINS:
-                piece = jnp.concatenate([piece, jnp.zeros((height, BINS - reach), F32)], axis=1)
-            piece = piece * stitch_ref[b]
-            band = piece if band is None else band + piece
-        stitched_ref[t] = band
-        stitched.append(band[:, : 2 * STRIDE])
-
-    near = jnp.concatenate(stitched, axis=0)
-    wide = 2 * STRIDE
+        for back, width, bands in ((0, BINS, stitched), (1, wide, before)):
+            band = None
+            for b in range(BLOCKS):
+                k = back * BLOCKS + b
+                first, reach = offsets[k] + margin, min(width, BINS - STRIDE * b)
+                piece = skewed[:, first : first + reach]
+                if reach < width:
+                    piece = jnp.concatenate(
+                        [piece, jnp.zeros((height, width - reach), F32)], axis=1
+                    )
+                piece = piece * stitch_ref[k][:, :width]
+                band = piece if band is None else band + piece
+            bands.append(band)
+        stitched_ref[t] = stitched[t]
+
+    near = jnp.concatenate([band[:, :wide] for band in stitched] + before, axis=0)
     col = lax.broadcasted_iota(jnp.int32, (wide, wide), 0)
     corner = lax.broadcasted_iota(jnp.int32, (wide, wide), 1)
     box = ((col > corner) & (col <= corner + STRIDE) & (corner < STRIDE)).astype(F32)
@@ -373,9 +382,9 @@
     here = lax.broadcasted_iota(jnp.int32, (height, wide), 0)
     there = lax.broadcasted_iota(jnp.int32, (height, wide), 1)
 
-    def by_row(values):
+    def by_row(values, back):
         rows = []
-        for t in range(targets):
+        for t in range(back * targets, (back + 1) * targets):
             own = pltpu.roll(
                 values[t * height : (t + 1) * height], 0, 1, stride=1, stride_axis=0
             )
@@ -386,29 +395,31 @@
     for t in range(targets):
         own = jnp.where(here == there, down[t * height : (t + 1) * height], 0.0)
         down_rows.append(jnp.sum(own, axis=0, keepdims=True))
-    rows = by_row(square) + by_row(contact)
-    own = (place_ref[1] * (STRIDE // height) + place_ref[0]) * height
-    missing = STRIDE - own - lax.broadcasted_iota(jnp.int32, (1, LANES), 1)
-    missing = jnp.maximum(missing, 0).astype(F32)
-    up_rows = [row + missing for row in rows[targets:]]
-    keep_ref[...] = jnp.concatenate(rows[:targets] + up_rows + down_rows, axis=0)
+    rows = by_row(square, 0) + by_row(contact, 0)
+    rows_before = by_row(square, 1) + by_row(contact, 1)
+    keep_ref[...] = jnp.concatenate(rows + down_rows, axis=0)
     per_row = LANES // height
     first = lax.broadcasted_iota(jnp.int32, (per_row, LANES), 1) < height
-    packs = [
-        jnp.concatenate(
-            rows[p : p + per_row]
-            + [jnp.zeros((1, LANES), F32)] * (per_row - len(rows[p : p + per_row])),
-            axis=0,
-        )
-        for p in range(0, len(rows), per_row)
-    ]
+    def packs_of(rows):
+        return [
+            jnp.concatenate(
+                rows[p : p + per_row]
+                + [jnp.zeros((1, LANES), F32)] * (per_row - len(rows[p : p + per_row])),
+                axis=0,
+            )
+            for p in range(0, len(rows), per_row)
+        ]
+
+    packs = list(zip(packs_of(rows), packs_of(rows_before)))
     for k in range(1, STRIDE // height + 1):
+        same = place_ref[0] + k < STRIDE // height
         packed = []
-        for pack in packs:
-            turned = jnp.where(first, pltpu.roll(pack, LANES - k * height, 1), 0.0)
-            turned = pltpu.roll(turned, 0, 1, stride=height, stride_axis=0)
+        for own, previous in packs:
+            turned = pltpu.roll(jnp.where(same, own, previous), LANES - k * height, 1)
+            turned = pltpu.roll(
+                jnp.where(first, turned, 0.0), 0, 1, stride=height, stride_axis=0
+            )
             packed.append(jnp.sum(turned, axis=0, keepdims=True))
-
         send_ref[lax.rem(place_ref[0] + k, STRIDE // height)] = jnp.concatenate(packed, axis=0)
 
 
@@ -452,7 +463,7 @@
     channels = distance_rate.shape[0]
     targets = head_weight.shape[0]
     place = jnp.stack([tower_index, genome_index]).astype(jnp.int32)
-    lanes = segments(2)[2]
+    lanes = segments(2, height)[2]
     packs = -(-2 * targets * height // LANES)
     vmem = pl.BlockSpec(memory_space=pltpu.VMEM)
     smem = pl.BlockSpec(memory_space=pltpu.SMEM)
@@ -464,7 +475,7 @@
         jax.ShapeDtypeStruct((rows, lanes), F32),
         jax.ShapeDtypeStruct((rows, lanes), F32),
         jax.ShapeDtypeStruct((targets * height, height * channels), BF16),
-        jax.ShapeDtypeStruct((BLOCKS, height, BINS), F32),
+        jax.ShapeDtypeStruct((2 * BLOCKS, height, BINS), F32),
     ]
     for count in (height + 2, height):
         for span in spans_of(count, groups):
@@ -508,10 +519,7 @@
         compiler_params=pltpu.CompilerParams(vmem_limit_bytes=VMEM_BYTES),
         name="windows",
     )(place, features, jnp.transpose(trunk_out, (0, 2, 1)), pair_weight, *prepared)
-    starts = lax.axis_size("genome")
-    passed = lax.ppermute(send, "genome", [(i, i + 1) for i in range(starts - 1)])
-    ahead = (jnp.arange(towers) > tower_index)[:, None, None]
-    got = lax.all_to_all(jnp.where(ahead, send, passed), "tower", 0, 0, tiled=True)
+    got = lax.all_to_all(send, "tower", 0, 0, tiled=True)
     scores = pl.pallas_call(
         functools.partial(finish_kernel, height),
         out_shape=jax.ShapeDtypeStruct((targets, 2, height), F32),

time: 39.4 us -> 39.3 us (level)
  Pallas kernels: 15 us -> 18.6 us
  starting transfers between devices: 9.48 us -> 7.29 us
  waiting for transfers between devices: 6.39 us -> 5.06 us
    pallas_call x1, Pallas kernels: 9.52 us -> 13 us  [per_device(): pl.pallas_call(functools.partial(main_kernel, height, groups), out_shape=...]
    ppermute x1 -> x0, starting transfers between devices: 2.19 us -> none  [per_device(): lax.ppermute(send, 'genome', [(i, i + 1) for i in range(starts - 1)])]
    ppermute x1 -> x0, waiting for transfers between devices: 1.3 us -> none  [per_device(): lax.ppermute(send, 'genome', [(i, i + 1) for i in range(starts - 1)])]
  transfers between devices with their start and end apart: 2 -> 1, of which waited for: 2 -> 1; matrix products, arithmetic and copies ran while one was open for 0% -> 0% of each run, Pallas kernels for 3% -> 3%
where the time goes in v9:
time: 39.3 us; the launch traced here: 39 us
  Pallas kernels  18.6 us (47%)
  starting transfers between devices  7.29 us (19%)
  blocking collectives  6.36 us (16%)
  waiting for transfers between devices  5.06 us (13%)
  local copies, waits for them, and re-layouts  0.92 us (2%)
  between operations  0.73 us (2%)
    pallas_call x1, Pallas kernels, per_device(): pl.pallas_call(functools.partial(main_kernel, height, groups), out_shape=...  13 us
    all_to_all x1, starting transfers between devices, per_device(): features = lax.all_to_all(own, 'genome', 0, 0, tiled=True)  7.29 us
    all_to_all x1, blocking collectives, per_device(): got = lax.all_to_all(send, 'tower', 0, 0, tiled=True)  6.36 us
    all_to_all x1, waiting for transfers between devices, per_device(): features = lax.all_to_all(own, 'genome', 0, 0, tiled=True)  5.06 us
    pallas_call x1, Pallas kernels, stem(): pl.pallas_call(functools.partial(stem_kernel, bins), out_shape=jax.ShapeD...  3.83 us
    pallas_call x1, Pallas kernels, per_device(): pl.pallas_call(functools.partial(prepare_kernel, height, groups), out_sha...  1.05 us
    unnamed x18, local copies, waits for them, and re-layouts  0.92 us
  transfers between devices with their start and end apart: 1, of which 1 were waited for; matrix products, arithmetic and copies ran while one was open for 0% of the time, Pallas kernels for 3%

profile of v9, /device:TPU:0, one launch (start us, length us, event | category | flops | bytes accessed | tf_op | source)
XLA Modules:
  0.0 39.0 jit_solution(10567166668051062392)
XLA Ops:
  0.6 0.0 copy-start.6
  0.6 0.0 copy-start.5
  0.7 0.0 copy-start.4
  0.7 0.0 copy-start.8
  0.7 0.0 copy-start.3
  0.7 0.0 copy-start.7
  0.7 3.8 %stem.1._ = bf16[8,48,128]{2,1,0:T(8,128)(2,1)} custom-call(s32[1024,128]{1,0:T(8,128)} %bitcast.10, bf16[96,8192]{1,0:T(8,128)(2,1)} %weight_hbm.1), custom_call_target="tpu_custom_call" | custom-call | tf_op jit(solution)/shard_map/stem/pallas_call | solution.py:67
  4.5 7.3 %all-to-all-start = ((bf16[8,48,128]{2,1,0:T(8,128)(2,1)}), bf16[8,48,128]{2,1,0:T(8,128)(2,1)S(1)}, u32[]{:S(2)}, u32[]{:S(2)}) async-start(bf16[8,48,128]{2,1,0:T(8,128)(2,1)} %stem.1._), calls=%async_computation | async-start | bytes 196608 | tf_op jit(solution)/shard_map/all_to_all | solution.py:461
  11.8 0.1 pad_add_fusion.place_ref
  11.9 0.0 copy-done.6
  11.9 0.0 copy-done.5
  11.9 0.0 copy-done.4
  11.9 0.0 copy-done.8
  11.9 0.0 copy-done.3
  11.9 0.0 copy-done.7
  11.9 0.0 copy-start
  11.9 0.9 %copy-done = bf16[8,48,128]{2,1,0:T(8,128)(2,1)S(1)} copy-done((bf16[8,48,128]{2,1,0:T(8,128)(2,1)S(1)}, bf16[8,48,128]{2,1,0:T(8,128)(2,1)}, u32[]{:S(2)}) %copy-start) | copy-done | bytes 98328
  12.8 0.0 copy-start.1
  12.8 0.0 copy-start.2
  12.8 1.1 %prepare.1 = (bf16[6,144,96]{2,1,0:T(8,128)(2,1)S(1)}, f32[48,128]{1,0:T(8,128)S(1)}, f32[20,1152]{1,0:T(8,128)S(1)}, f32[20,1152]{1,0:T(8,128)S(1)}, bf16[80,76...) custom-call(s32[2]{0:T(128)S(1)} %pad_add_fusion.place_ref, ...), custom_call_target="tpu_custom_call" | custom-call | flops 1000000000 | bytes 4194304 | tf_op jit(solution)/shard_map/prepare/pallas_call | solution.py:485
  13.9 5.1 %all-to-all-done.features = bf16[8,48,128]{2,1,0:T(8,128)(2,1)S(1)} async-done(((bf16[8,48,128]{2,1,0:T(8,128)(2,1)}), bf16[8,48,128]{2,1,0:T(8,128)(2,1)S(1)}, u32[]{:S(2)}, u32[]{:S(2)}) %all-to-all-start) | async-done | bytes 98336 | tf_op jit(solution)/shard_map/all_to_all | solution.py:461
  18.9 0.0 copy-done.1
  18.9 0.0 copy-done.2
  19.0 13.0 %windows.1 = (f32[5,16,256]{2,1,0:T(8,128)}, f32[15,128]{1,0:T(8,128)S(1)}, f32[4,2,128]{2,1,0:T(2,128)S(1)}) custom-call(s32[2]{0:T(128)S(1)} %pad_add_fusion.place_ref, bf16[8,48,128]{2,1,0:T(8,128)(2,1)S(1)} %all-to-all-done.features, bf16[6,48,96]{2,1,0:T(8,128)(2,1)S(1)} %bitcast.7, bf16[96,96]{1,0:T(8,128)(2,1)S(1)} %copy-done.2, ...), custom_call_target="tpu_custom_call" | custom-call | tf_op jit(solution)/shard_map/windows/pallas_call | solution.py:503
  31.9 6.4 %all_to_all.10.got_ref = f32[4,2,128]{2,1,0:T(2,128)S(1)} all-to-all(f32[4,2,128]{2,1,0:T(2,128)S(1)} %get-tuple-element.31), channel_id=1, replica_groups=mesh['genome'=8,'tower'=4] {'tower'}, dimensions={0} | all-to-all | bytes 8192 | tf_op jit(solution)/shard_map/all_to_all | solution.py:522
  38.3 0.7 %finish.1 = f32[5,2,16]{2,1,0:T(2,128)} custom-call(f32[15,128]{1,0:T(8,128)S(1)} %get-tuple-element.30.keep_ref, f32[4,2,128]{2,1,0:T(2,128)S(1)} %all_to_all.10.got_ref), custom_call_target="tpu_custom_call" | custom-call | tf_op jit(solution)/shard_map/finish/pallas_call | solution.py:523
Async XLA Ops:
  0.6 11.3 %copy-start.6 = (bf16[5,48]{1,0:T(8,128)(2,1)S(1)}, bf16[5,48]{1,0:T(8,128)(2,1)}, u32[]{:S(2)}) copy-start(bf16[5,48]{1,0:T(8,128)(2,1)} %head_in.1) | copy-start | bytes 1444
  0.6 11.3 %copy-start.5 = (bf16[2,48,48]{2,1,0:T(8,128)(2,1)S(1)}, bf16[2,48,48]{2,1,0:T(8,128)(2,1)}, u32[]{:S(2)}) copy-start(bf16[2,48,48]{2,1,0:T(8,128)(2,1)} %mix_in.1) | copy-start | bytes 27652
  0.7 11.3 %copy-start.4 = (bf16[2,3,48,144]{3,2,1,0:T(8,128)(2,1)S(1)}, bf16[2,3,48,144]{3,2,1,0:T(8,128)(2,1)}, u32[]{:S(2)}) copy-start(bf16[2,3,48,144]{3,2,1,0:T(8,128)(2,1)} %conv_in.1) | copy-start | bytes 248836
  0.7 11.2 %copy-start.8 = (f32[48]{0:T(128)S(1)}, f32[48]{0:T(128)}, u32[]{:S(2)}) copy-start(f32[48]{0:T(128)} %param.16) | copy-start | bytes 580
  0.7 11.2 %copy-start.3 = (bf16[6,48,288]{2,1,0:T(8,128)(2,1)S(1)}, bf16[6,48,288]{2,1,0:T(8,128)(2,1)}, u32[]{:S(2)}) copy-start(bf16[6,48,288]{2,1,0:T(8,128)(2,1)} %trunk_in.1) | copy-start | bytes 497668
  0.7 11.2 %copy-start.7 = (s32[256]{0:T(256)S(1)}, s32[256]{0:T(256)}, u32[]{:S(2)}) copy-start(s32[256]{0:T(256)} %param.11) | copy-start | bytes 3076
  4.5 14.4 %all-to-all-start = ((bf16[8,48,128]{2,1,0:T(8,128)(2,1)}), bf16[8,48,128]{2,1,0:T(8,128)(2,1)S(1)}, u32[]{:S(2)}, u32[]{:S(2)}) async-start(bf16[8,48,128]{2,1,0:T(8,128)(2,1)} %stem.1._), calls=%async_computation | async-start | bytes 196608 | tf_op jit(solution)/shard_map/all_to_all | solution.py:461
  11.9 0.9 %copy-start = (bf16[8,48,128]{2,1,0:T(8,128)(2,1)S(1)}, bf16[8,48,128]{2,1,0:T(8,128)(2,1)}, u32[]{:S(2)}) copy-start(bf16[8,48,128]{2,1,0:T(8,128)(2,1)} %stem.1._) | copy-start | bytes 294916
  12.8 6.1 %copy-start.1 = (bf16[6,96,48]{1,2,0:T(8,128)(2,1)S(1)}, bf16[6,96,48]{1,2,0:T(8,128)(2,1)}, u32[]{:S(2)}) copy-start(bf16[6,96,48]{1,2,0:T(8,128)(2,1)} %param.14) | copy-start | bytes 165892
  12.8 6.1 %copy-start.2 = (bf16[96,96]{1,0:T(8,128)(2,1)S(1)}, bf16[96,96]{1,0:T(8,128)(2,1)}, u32[]{:S(2)}) copy-start(bf16[96,96]{1,0:T(8,128)(2,1)} %pair_weight.1) | copy-start | bytes 55300

commit v10 on v9

--- a/solution.py
+++ b/solution.py
@@ -237,7 +237,7 @@
         conv_a[span], mix_a[span] = rest.pop(0), rest.pop(0)
     for span in spans_of(height, groups):
         conv_b[span], mix_b[span] = rest.pop(0), rest.pop(0)
-    stitched_ref, keep_ref, send_ref, taps_a, taps_b, grid_ref, final_ref, squeezed_ref = rest
+    stitched_ref, keep_ref, send_ref, taps_a, taps_b, grid_ref, final_ref = rest
 
     starts = features.shape[0]
     blocks = []
@@ -297,10 +297,8 @@
     rate = jnp.concatenate([rate_ref[...]] * (lanes // LANES), axis=1)
     lane = lax.broadcasted_iota(jnp.int32, (1, lanes), 1)
 
-    def place_taps(ref, slot, act):
-        act = act.astype(BF16)
+    def place_sides(ref, slot, act):
         ref[pl.ds(slot * depth, channels), :] = pltpu.roll(act, 1, 1)
-        ref[pl.ds(slot * depth + channels, channels), :] = act
         ref[pl.ds(slot * depth + 2 * channels, channels), :] = pltpu.roll(act, lanes - 1, 1)
 
     for row in range(height + 2 * margin):
@@ -316,35 +314,36 @@
                 piece = spread if piece is None else jnp.where(here >= low, spread, piece)
             tiles.append(piece)
         mixed = jnp.concatenate(tiles, axis=1) + right - rate * decay_ref[pl.ds(row, 1), :]
-        place_taps(taps_a, row, jnp.maximum(mixed, 0.0) * inside_ref[pl.ds(row, 1), :])
-
-    def convolve(kernels, taps, rows):
-        for first in range(0, rows, groups):
-            span = min(groups, rows - first)
-            conv = dot(kernels[span][...], taps[pl.ds(first * depth, (span + 2) * depth), :])
-            squeezed_ref[pl.ds(first * channels, span * channels), :] = jnp.maximum(
-                conv, 0.0
-            ).astype(BF16)
-
-    convolve(conv_a, taps_a, height + 2)
+        act = (jnp.maximum(mixed, 0.0) * inside_ref[pl.ds(row, 1), :]).astype(BF16)
+        taps_a[pl.ds(row * depth + channels, channels), :] = act
+        place_sides(taps_a, row, act)
+
+    chunks = [pl.ds(at, min(2 * LANES, lanes - at)) for at in range(0, lanes, 2 * LANES)]
+
+    def update(kernels, mixes, taps, first, span, chunk):
+        conv = dot(kernels[span][...], taps[pl.ds(first * depth, (span + 2) * depth), chunk])
+        return dot(mixes[span][...], jnp.maximum(conv, 0.0).astype(BF16))
+
     for first in range(0, height + 2, groups):
         span = min(groups, height + 2 - first)
-        update = dot(
-            mix_a[span][...], squeezed_ref[pl.ds(first * channels, span * channels), :]
-        )
-        for r in range(span):
-            row = first + r
-            kept = taps_a[pl.ds((row + 1) * depth + channels, channels), :].astype(F32)
-            grid = kept + update[r * channels : (r + 1) * channels]
-            if 1 <= row <= height:
-                grid_ref[pl.ds((row - 1) * channels, channels), :] = grid
-            place_taps(taps_b, row, jnp.maximum(grid, 0.0) * inside_ref[pl.ds(row + 1, 1), :])
-    convolve(conv_b, taps_b, height)
+        for chunk in chunks:
+            added = update(conv_a, mix_a, taps_a, first, span, chunk)
+            for r in range(span):
+                row = first + r
+                kept = taps_a[pl.ds((row + 1) * depth + channels, channels), chunk]
+                grid = kept.astype(F32) + added[r * channels : (r + 1) * channels]
+                if 1 <= row <= height:
+                    grid_ref[pl.ds((row - 1) * channels, channels), chunk] = grid
+                act = jnp.maximum(grid, 0.0) * inside_ref[pl.ds(row + 1, 1), chunk]
+                taps_b[pl.ds(row * depth + channels, channels), chunk] = act.astype(BF16)
+        for row in range(first, first + span):
+            place_sides(taps_b, row, taps_b[pl.ds(row * depth + channels, channels), :])
     for first in range(0, height, groups):
         span = min(groups, height - first)
         rows = pl.ds(first * channels, span * channels)
-        update = dot(mix_b[span][...], squeezed_ref[rows, :])
-        final_ref[rows, :] = jnp.maximum(grid_ref[rows, :] + update, 0.0).astype(BF16)
+        for chunk in chunks:
+            added = update(conv_b, mix_b, taps_b, first, span, chunk)
+            final_ref[rows, chunk] = jnp.maximum(grid_ref[rows, chunk] + added, 0.0).astype(BF16)
     targets = head_ref.shape[0] // height
     contact = dot(head_ref[...], final_ref[...]).reshape(targets, height, lanes)
 
@@ -514,7 +513,6 @@
             pltpu.VMEM(((height + 2) * 3 * channels, lanes), BF16),
             pltpu.VMEM((height * channels, lanes), F32),
             pltpu.VMEM((height * channels, lanes), BF16),
-            pltpu.VMEM(((height + 2) * channels, lanes), BF16),
         ],
         compiler_params=pltpu.CompilerParams(vmem_limit_bytes=VMEM_BYTES),
         name="windows",

time: 39.3 us -> 46.3 us (1.18)
  Pallas kernels: 18.6 us -> 25.6 us
    pallas_call x1, Pallas kernels: 13 us -> 20 us  [per_device(): pl.pallas_call(functools.partial(main_kernel, height, groups), out_shape=...]
  transfers between devices with their start and end apart: 1 -> 1, of which waited for: 1 -> 1; matrix products, arithmetic and copies ran while one was open for 0% -> 0% of each run, Pallas kernels for 3% -> 2%
where the time goes in v10:
time: 46.3 us; the launch traced here: 46 us
  Pallas kernels  25.6 us (55%)
  starting transfers between devices  7.29 us (16%)
  blocking collectives  6.34 us (14%)
  waiting for transfers between devices  5.06 us (11%)
  local copies, waits for them, and re-layouts  0.92 us (2%)
  between operations  0.73 us (2%)
    pallas_call x1, Pallas kernels, per_device(): pl.pallas_call(functools.partial(main_kernel, height, groups), out_shape=...  20 us
    all_to_all x1, starting transfers between devices, per_device(): features = lax.all_to_all(own, 'genome', 0, 0, tiled=True)  7.29 us
    all_to_all x1, blocking collectives, per_device(): got = lax.all_to_all(send, 'tower', 0, 0, tiled=True)  6.34 us
    all_to_all x1, waiting for transfers between devices, per_device(): features = lax.all_to_all(own, 'genome', 0, 0, tiled=True)  5.06 us
    pallas_call x1, Pallas kernels, stem(): pl.pallas_call(functools.partial(stem_kernel, bins), out_shape=jax.ShapeD...  3.83 us
    pallas_call x1, Pallas kernels, per_device(): pl.pallas_call(functools.partial(prepare_kernel, height, groups), out_sha...  1.05 us
  transfers between devices with their start and end apart: 1, of which 1 were waited for; matrix products, arithmetic and copies ran while one was open for 0% of the time, Pallas kernels for 2%

profile of v10, /device:TPU:0, one launch (start us, length us, event | category | flops | bytes accessed | tf_op | source)
XLA Modules:
  0.0 46.0 jit_solution(13040048701479607025)
XLA Ops:
  0.6 0.0 copy-start.6
  0.6 0.0 copy-start.5
  0.7 0.0 copy-start.4
  0.7 0.0 copy-start.8
  0.7 0.0 copy-start.3
  0.7 0.0 copy-start.7
  0.7 3.8 %stem.1._ = bf16[8,48,128]{2,1,0:T(8,128)(2,1)} custom-call(s32[1024,128]{1,0:T(8,128)} %bitcast.10, bf16[96,8192]{1,0:T(8,128)(2,1)} %weight_hbm.1), custom_call_target="tpu_custom_call" | custom-call | tf_op jit(solution)/shard_map/stem/pallas_call | solution.py:67
  4.5 7.3 %all-to-all-start = ((bf16[8,48,128]{2,1,0:T(8,128)(2,1)}), bf16[8,48,128]{2,1,0:T(8,128)(2,1)S(1)}, u32[]{:S(2)}, u32[]{:S(2)}) async-start(bf16[8,48,128]{2,1,0:T(8,128)(2,1)} %stem.1._), calls=%async_computation | async-start | bytes 196608 | tf_op jit(solution)/shard_map/all_to_all | solution.py:460
  11.8 0.1 pad_add_fusion.place_ref
  11.9 0.0 copy-done.6
  11.9 0.0 copy-done.5
  11.9 0.0 copy-done.4
  11.9 0.0 copy-done.8
  11.9 0.0 copy-done.3
  11.9 0.0 copy-done.7
  11.9 0.0 copy-start
  11.9 0.9 %copy-done = bf16[8,48,128]{2,1,0:T(8,128)(2,1)S(1)} copy-done((bf16[8,48,128]{2,1,0:T(8,128)(2,1)S(1)}, bf16[8,48,128]{2,1,0:T(8,128)(2,1)}, u32[]{:S(2)}) %copy-start) | copy-done | bytes 98328
  12.8 0.0 copy-start.1
  12.8 0.0 copy-start.2
  12.8 1.1 %prepare.1 = (bf16[6,144,96]{2,1,0:T(8,128)(2,1)S(1)}, f32[48,128]{1,0:T(8,128)S(1)}, f32[20,1152]{1,0:T(8,128)S(1)}, f32[20,1152]{1,0:T(8,128)S(1)}, bf16[80,76...) custom-call(s32[2]{0:T(128)S(1)} %pad_add_fusion.place_ref, ...), custom_call_target="tpu_custom_call" | custom-call | flops 1000000000 | bytes 4194304 | tf_op jit(solution)/shard_map/prepare/pallas_call | solution.py:484
  13.9 5.1 %all-to-all-done.features = bf16[8,48,128]{2,1,0:T(8,128)(2,1)S(1)} async-done(((bf16[8,48,128]{2,1,0:T(8,128)(2,1)}), bf16[8,48,128]{2,1,0:T(8,128)(2,1)S(1)}, u32[]{:S(2)}, u32[]{:S(2)}) %all-to-all-start) | async-done | bytes 98336 | tf_op jit(solution)/shard_map/all_to_all | solution.py:460
  18.9 0.0 copy-done.1
  18.9 0.0 copy-done.2
  19.0 20.0 %windows.1 = (f32[5,16,256]{2,1,0:T(8,128)}, f32[15,128]{1,0:T(8,128)S(1)}, f32[4,2,128]{2,1,0:T(2,128)S(1)}) custom-call(s32[2]{0:T(128)S(1)} %pad_add_fusion.place_ref, bf16[8,48,128]{2,1,0:T(8,128)(2,1)S(1)} %all-to-all-done.features, bf16[6,48,96]{2,1,0:T(8,128)(2,1)S(1)} %bitcast.7, bf16[96,96]{1,0:T(8,128)(2,1)S(1)} %copy-done.2, ...), custom_call_target="tpu_custom_call" | custom-call | tf_op jit(solution)/shard_map/windows/pallas_call | solution.py:502
  39.0 6.3 %all_to_all.10.got_ref = f32[4,2,128]{2,1,0:T(2,128)S(1)} all-to-all(f32[4,2,128]{2,1,0:T(2,128)S(1)} %get-tuple-element.31), channel_id=1, replica_groups=mesh['genome'=8,'tower'=4] {'tower'}, dimensions={0} | all-to-all | bytes 8192 | tf_op jit(solution)/shard_map/all_to_all | solution.py:520
  45.3 0.7 %finish.1 = f32[5,2,16]{2,1,0:T(2,128)} custom-call(f32[15,128]{1,0:T(8,128)S(1)} %get-tuple-element.30.keep_ref, f32[4,2,128]{2,1,0:T(2,128)S(1)} %all_to_all.10.got_ref), custom_call_target="tpu_custom_call" | custom-call | tf_op jit(solution)/shard_map/finish/pallas_call | solution.py:521
Async XLA Ops:
  0.6 11.3 %copy-start.6 = (bf16[5,48]{1,0:T(8,128)(2,1)S(1)}, bf16[5,48]{1,0:T(8,128)(2,1)}, u32[]{:S(2)}) copy-start(bf16[5,48]{1,0:T(8,128)(2,1)} %head_in.1) | copy-start | bytes 1444
  0.6 11.3 %copy-start.5 = (bf16[2,48,48]{2,1,0:T(8,128)(2,1)S(1)}, bf16[2,48,48]{2,1,0:T(8,128)(2,1)}, u32[]{:S(2)}) copy-start(bf16[2,48,48]{2,1,0:T(8,128)(2,1)} %mix_in.1) | copy-start | bytes 27652
  0.7 11.3 %copy-start.4 = (bf16[2,3,48,144]{3,2,1,0:T(8,128)(2,1)S(1)}, bf16[2,3,48,144]{3,2,1,0:T(8,128)(2,1)}, u32[]{:S(2)}) copy-start(bf16[2,3,48,144]{3,2,1,0:T(8,128)(2,1)} %conv_in.1) | copy-start | bytes 248836
  0.7 11.2 %copy-start.8 = (f32[48]{0:T(128)S(1)}, f32[48]{0:T(128)}, u32[]{:S(2)}) copy-start(f32[48]{0:T(128)} %param.16) | copy-start | bytes 580
  0.7 11.2 %copy-start.3 = (bf16[6,48,288]{2,1,0:T(8,128)(2,1)S(1)}, bf16[6,48,288]{2,1,0:T(8,128)(2,1)}, u32[]{:S(2)}) copy-start(bf16[6,48,288]{2,1,0:T(8,128)(2,1)} %trunk_in.1) | copy-start | bytes 497668
  0.7 11.2 %copy-start.7 = (s32[256]{0:T(256)S(1)}, s32[256]{0:T(256)}, u32[]{:S(2)}) copy-start(s32[256]{0:T(256)} %param.11) | copy-start | bytes 3076
  4.5 14.4 %all-to-all-start = ((bf16[8,48,128]{2,1,0:T(8,128)(2,1)}), bf16[8,48,128]{2,1,0:T(8,128)(2,1)S(1)}, u32[]{:S(2)}, u32[]{:S(2)}) async-start(bf16[8,48,128]{2,1,0:T(8,128)(2,1)} %stem.1._), calls=%async_computation | async-start | bytes 196608 | tf_op jit(solution)/shard_map/all_to_all | solution.py:460
  11.9 0.9 %copy-start = (bf16[8,48,128]{2,1,0:T(8,128)(2,1)S(1)}, bf16[8,48,128]{2,1,0:T(8,128)(2,1)}, u32[]{:S(2)}) copy-start(bf16[8,48,128]{2,1,0:T(8,128)(2,1)} %stem.1._) | copy-start | bytes 294916
  12.8 6.1 %copy-start.1 = (bf16[6,96,48]{1,2,0:T(8,128)(2,1)S(1)}, bf16[6,96,48]{1,2,0:T(8,128)(2,1)}, u32[]{:S(2)}) copy-start(bf16[6,96,48]{1,2,0:T(8,128)(2,1)} %param.14) | copy-start | bytes 165892
  12.8 6.1 %copy-start.2 = (bf16[96,96]{1,0:T(8,128)(2,1)S(1)}, bf16[96,96]{1,0:T(8,128)(2,1)}, u32[]{:S(2)}) copy-start(bf16[96,96]{1,0:T(8,128)(2,1)} %pair_weight.1) | copy-start | bytes 55300

commit v11 on v9

--- a/solution.py
+++ b/solution.py
@@ -318,33 +318,34 @@
         mixed = jnp.concatenate(tiles, axis=1) + right - rate * decay_ref[pl.ds(row, 1), :]
         place_taps(taps_a, row, jnp.maximum(mixed, 0.0) * inside_ref[pl.ds(row, 1), :])
 
-    def convolve(kernels, taps, rows):
-        for first in range(0, rows, groups):
+    def tower_block(kernels, mixes, taps, rows):
+        for group, first in enumerate(range(0, rows, groups)):
             span = min(groups, rows - first)
             conv = dot(kernels[span][...], taps[pl.ds(first * depth, (span + 2) * depth), :])
-            squeezed_ref[pl.ds(first * channels, span * channels), :] = jnp.maximum(
+            squeezed_ref[pl.ds(0, span * channels), pl.ds(group * lanes, lanes)] = jnp.maximum(
                 conv, 0.0
             ).astype(BF16)
-
-    convolve(conv_a, taps_a, height + 2)
-    for first in range(0, height + 2, groups):
-        span = min(groups, height + 2 - first)
-        update = dot(
-            mix_a[span][...], squeezed_ref[pl.ds(first * channels, span * channels), :]
-        )
-        for r in range(span):
-            row = first + r
-            kept = taps_a[pl.ds((row + 1) * depth + channels, channels), :].astype(F32)
-            grid = kept + update[r * channels : (r + 1) * channels]
-            if 1 <= row <= height:
-                grid_ref[pl.ds((row - 1) * channels, channels), :] = grid
-            place_taps(taps_b, row, jnp.maximum(grid, 0.0) * inside_ref[pl.ds(row + 1, 1), :])
-    convolve(conv_b, taps_b, height)
-    for first in range(0, height, groups):
-        span = min(groups, height - first)
-        rows = pl.ds(first * channels, span * channels)
-        update = dot(mix_b[span][...], squeezed_ref[rows, :])
-        final_ref[rows, :] = jnp.maximum(grid_ref[rows, :] + update, 0.0).astype(BF16)
+        full, left_over = rows // groups, rows % groups
+        wide = dot(mixes[groups][...], squeezed_ref[:, pl.ds(0, full * lanes)])
+        added = [
+            wide[(row % groups) * channels :][:channels, (row // groups) * lanes :][:, :lanes]
+            for row in range(full * groups)
+        ]
+        if left_over:
+            rest = squeezed_ref[pl.ds(0, left_over * channels), pl.ds(full * lanes, lanes)]
+            last = dot(mixes[left_over][...], rest)
+            added += [last[r * channels : (r + 1) * channels] for r in range(left_over)]
+        return added
+
+    for row, added in enumerate(tower_block(conv_a, mix_a, taps_a, height + 2)):
+        kept = taps_a[pl.ds((row + 1) * depth + channels, channels), :].astype(F32)
+        grid = kept + added
+        if 1 <= row <= height:
+            grid_ref[pl.ds((row - 1) * channels, channels), :] = grid
+        place_taps(taps_b, row, jnp.maximum(grid, 0.0) * inside_ref[pl.ds(row + 1, 1), :])
+    for row, added in enumerate(tower_block(conv_b, mix_b, taps_b, height)):
+        rows = pl.ds(row * channels, channels)
+        final_ref[rows, :] = jnp.maximum(grid_ref[rows, :] + added, 0.0).astype(BF16)
     targets = head_ref.shape[0] // height
     contact = dot(head_ref[...], final_ref[...]).reshape(targets, height, lanes)
 
@@ -514,7 +515,7 @@
             pltpu.VMEM(((height + 2) * 3 * channels, lanes), BF16),
             pltpu.VMEM((height * channels, lanes), F32),
             pltpu.VMEM((height * channels, lanes), BF16),
-            pltpu.VMEM(((height + 2) * channels, lanes), BF16),
+            pltpu.VMEM((groups * channels, -(-(height + 2) // groups) * lanes), BF16),
         ],
         compiler_params=pltpu.CompilerParams(vmem_limit_bytes=VMEM_BYTES),
         name="windows",

time: 39.3 us -> 39 us (level)
  no operation moved by 1% of the time
where the time goes in v11:
time: 39 us; the launch traced here: 38.7 us
  Pallas kernels  18.3 us (47%)
  starting transfers between devices  7.29 us (19%)
  blocking collectives  6.34 us (16%)
  waiting for transfers between devices  5.06 us (13%)
  local copies, waits for them, and re-layouts  0.92 us (2%)
  between operations  0.73 us (2%)
    pallas_call x1, Pallas kernels, per_device(): pl.pallas_call(functools.partial(main_kernel, height, groups), out_shape=...  12.7 us
    all_to_all x1, starting transfers between devices, per_device(): features = lax.all_to_all(own, 'genome', 0, 0, tiled=True)  7.29 us
    all_to_all x1, blocking collectives, per_device(): got = lax.all_to_all(send, 'tower', 0, 0, tiled=True)  6.34 us
    all_to_all x1, waiting for transfers between devices, per_device(): features = lax.all_to_all(own, 'genome', 0, 0, tiled=True)  5.06 us
    pallas_call x1, Pallas kernels, stem(): pl.pallas_call(functools.partial(stem_kernel, bins), out_shape=jax.ShapeD...  3.83 us
    pallas_call x1, Pallas kernels, per_device(): pl.pallas_call(functools.partial(prepare_kernel, height, groups), out_sha...  1.05 us
    unnamed x18, local copies, waits for them, and re-layouts  0.92 us
  transfers between devices with their start and end apart: 1, of which 1 were waited for; matrix products, arithmetic and copies ran while one was open for 0% of the time, Pallas kernels for 3%

profile of v11, /device:TPU:0, one launch (start us, length us, event | category | flops | bytes accessed | tf_op | source)
XLA Modules:
  0.0 38.7 jit_solution(979436745095711738)
XLA Ops:
  0.6 0.0 copy-start.6
  0.6 0.0 copy-start.5
  0.7 0.0 copy-start.4
  0.7 0.0 copy-start.8
  0.7 0.0 copy-start.3
  0.7 0.0 copy-start.7
  0.7 3.8 %stem.1._ = bf16[8,48,128]{2,1,0:T(8,128)(2,1)} custom-call(s32[1024,128]{1,0:T(8,128)} %bitcast.10, bf16[96,8192]{1,0:T(8,128)(2,1)} %weight_hbm.1), custom_call_target="tpu_custom_call" | custom-call | tf_op jit(solution)/shard_map/stem/pallas_call | solution.py:67
  4.5 7.3 %all-to-all-start = ((bf16[8,48,128]{2,1,0:T(8,128)(2,1)}), bf16[8,48,128]{2,1,0:T(8,128)(2,1)S(1)}, u32[]{:S(2)}, u32[]{:S(2)}) async-start(bf16[8,48,128]{2,1,0:T(8,128)(2,1)} %stem.1._), calls=%async_computation | async-start | bytes 196608 | tf_op jit(solution)/shard_map/all_to_all | solution.py:462
  11.8 0.1 pad_add_fusion.place_ref
  11.9 0.0 copy-done.6
  11.9 0.0 copy-done.5
  11.9 0.0 copy-done.4
  11.9 0.0 copy-done.8
  11.9 0.0 copy-done.3
  11.9 0.0 copy-done.7
  11.9 0.0 copy-start
  11.9 0.9 %copy-done = bf16[8,48,128]{2,1,0:T(8,128)(2,1)S(1)} copy-done((bf16[8,48,128]{2,1,0:T(8,128)(2,1)S(1)}, bf16[8,48,128]{2,1,0:T(8,128)(2,1)}, u32[]{:S(2)}) %copy-start) | copy-done | bytes 98328
  12.8 0.0 copy-start.1
  12.8 0.0 copy-start.2
  12.8 1.1 %prepare.1 = (bf16[6,144,96]{2,1,0:T(8,128)(2,1)S(1)}, f32[48,128]{1,0:T(8,128)S(1)}, f32[20,1152]{1,0:T(8,128)S(1)}, f32[20,1152]{1,0:T(8,128)S(1)}, bf16[80,76...) custom-call(s32[2]{0:T(128)S(1)} %pad_add_fusion.place_ref, ...), custom_call_target="tpu_custom_call" | custom-call | flops 1000000000 | bytes 4194304 | tf_op jit(solution)/shard_map/prepare/pallas_call | solution.py:486
  13.9 5.1 %all-to-all-done.features = bf16[8,48,128]{2,1,0:T(8,128)(2,1)S(1)} async-done(((bf16[8,48,128]{2,1,0:T(8,128)(2,1)}), bf16[8,48,128]{2,1,0:T(8,128)(2,1)S(1)}, u32[]{:S(2)}, u32[]{:S(2)}) %all-to-all-start) | async-done | bytes 98336 | tf_op jit(solution)/shard_map/all_to_all | solution.py:462
  18.9 0.0 copy-done.1
  18.9 0.0 copy-done.2
  19.0 12.7 %windows.1 = (f32[5,16,256]{2,1,0:T(8,128)}, f32[15,128]{1,0:T(8,128)S(1)}, f32[4,2,128]{2,1,0:T(2,128)S(1)}) custom-call(s32[2]{0:T(128)S(1)} %pad_add_fusion.place_ref, bf16[8,48,128]{2,1,0:T(8,128)(2,1)S(1)} %all-to-all-done.features, bf16[6,48,96]{2,1,0:T(8,128)(2,1)S(1)} %bitcast.7, bf16[96,96]{1,0:T(8,128)(2,1)S(1)} %copy-done.2, ...), custom_call_target="tpu_custom_call" | custom-call | tf_op jit(solution)/shard_map/windows/pallas_call | solution.py:504
  31.7 6.3 %all_to_all.10.got_ref = f32[4,2,128]{2,1,0:T(2,128)S(1)} all-to-all(f32[4,2,128]{2,1,0:T(2,128)S(1)} %get-tuple-element.31), channel_id=1, replica_groups=mesh['genome'=8,'tower'=4] {'tower'}, dimensions={0} | all-to-all | bytes 8192 | tf_op jit(solution)/shard_map/all_to_all | solution.py:523
  38.0 0.7 %finish.1 = f32[5,2,16]{2,1,0:T(2,128)} custom-call(f32[15,128]{1,0:T(8,128)S(1)} %get-tuple-element.30.keep_ref, f32[4,2,128]{2,1,0:T(2,128)S(1)} %all_to_all.10.got_ref), custom_call_target="tpu_custom_call" | custom-call | tf_op jit(solution)/shard_map/finish/pallas_call | solution.py:524
Async XLA Ops:
  0.6 11.3 %copy-start.6 = (bf16[5,48]{1,0:T(8,128)(2,1)S(1)}, bf16[5,48]{1,0:T(8,128)(2,1)}, u32[]{:S(2)}) copy-start(bf16[5,48]{1,0:T(8,128)(2,1)} %head_in.1) | copy-start | bytes 1444
  0.6 11.3 %copy-start.5 = (bf16[2,48,48]{2,1,0:T(8,128)(2,1)S(1)}, bf16[2,48,48]{2,1,0:T(8,128)(2,1)}, u32[]{:S(2)}) copy-start(bf16[2,48,48]{2,1,0:T(8,128)(2,1)} %mix_in.1) | copy-start | bytes 27652
  0.7 11.3 %copy-start.4 = (bf16[2,3,48,144]{3,2,1,0:T(8,128)(2,1)S(1)}, bf16[2,3,48,144]{3,2,1,0:T(8,128)(2,1)}, u32[]{:S(2)}) copy-start(bf16[2,3,48,144]{3,2,1,0:T(8,128)(2,1)} %conv_in.1) | copy-start | bytes 248836
  0.7 11.2 %copy-start.8 = (f32[48]{0:T(128)S(1)}, f32[48]{0:T(128)}, u32[]{:S(2)}) copy-start(f32[48]{0:T(128)} %param.16) | copy-start | bytes 580
  0.7 11.2 %copy-start.3 = (bf16[6,48,288]{2,1,0:T(8,128)(2,1)S(1)}, bf16[6,48,288]{2,1,0:T(8,128)(2,1)}, u32[]{:S(2)}) copy-start(bf16[6,48,288]{2,1,0:T(8,128)(2,1)} %trunk_in.1) | copy-start | bytes 497668
  0.7 11.2 %copy-start.7 = (s32[256]{0:T(256)S(1)}, s32[256]{0:T(256)}, u32[]{:S(2)}) copy-start(s32[256]{0:T(256)} %param.11) | copy-start | bytes 3076
  4.5 14.4 %all-to-all-start = ((bf16[8,48,128]{2,1,0:T(8,128)(2,1)}), bf16[8,48,128]{2,1,0:T(8,128)(2,1)S(1)}, u32[]{:S(2)}, u32[]{:S(2)}) async-start(bf16[8,48,128]{2,1,0:T(8,128)(2,1)} %stem.1._), calls=%async_computation | async-start | bytes 196608 | tf_op jit(solution)/shard_map/all_to_all | solution.py:462
  11.9 0.9 %copy-start = (bf16[8,48,128]{2,1,0:T(8,128)(2,1)S(1)}, bf16[8,48,128]{2,1,0:T(8,128)(2,1)}, u32[]{:S(2)}) copy-start(bf16[8,48,128]{2,1,0:T(8,128)(2,1)} %stem.1._) | copy-start | bytes 294916
  12.8 6.1 %copy-start.1 = (bf16[6,96,48]{1,2,0:T(8,128)(2,1)S(1)}, bf16[6,96,48]{1,2,0:T(8,128)(2,1)}, u32[]{:S(2)}) copy-start(bf16[6,96,48]{1,2,0:T(8,128)(2,1)} %param.14) | copy-start | bytes 165892
  12.8 6.1 %copy-start.2 = (bf16[96,96]{1,0:T(8,128)(2,1)S(1)}, bf16[96,96]{1,0:T(8,128)(2,1)}, u32[]{:S(2)}) copy-start(bf16[96,96]{1,0:T(8,128)(2,1)} %pair_weight.1) | copy-start | bytes 55300

commit v12 on v11

--- a/solution.py
+++ b/solution.py
@@ -37,17 +37,23 @@
     row = lax.broadcasted_iota(jnp.int32, (LANES, 4 * LANES), 0)
     col = lax.broadcasted_iota(jnp.int32, (LANES, 4 * LANES), 1)
     repeat = (row == col // 4).astype(F32).astype(BF16)
-    letter = (lax.broadcasted_iota(jnp.int32, (bins, 4 * LANES), 1) % 4).astype(F32)
+    letter = (lax.broadcasted_iota(jnp.int32, (1, 4 * LANES), 1) % 4).astype(F32)
     base_copy.wait()
     total = None
     per_chunk = groups // chunks
     for k in range(chunks):
-        hot = []
-        for q in range(per_chunk):
-            rows = bases[pl.ds(k * per_chunk + q, bins, stride=groups), :]
-            spread = dot(rows.astype(F32).astype(BF16), repeat)
-            hot.append(jnp.where(spread == letter, 1.0, 0.0).astype(BF16))
-        hot = jnp.concatenate(hot, axis=1)
+        rows = jnp.concatenate(
+            [
+                bases[pl.ds(k * per_chunk + q, bins, stride=groups), :]
+                for q in range(per_chunk)
+            ],
+            axis=0,
+        )
+        spread = dot(rows.astype(F32).astype(BF16), repeat)
+        hot = jnp.where(spread == letter, 1.0, 0.0).astype(BF16)
+        hot = jnp.concatenate(
+            [hot[q * bins : (q + 1) * bins] for q in range(per_chunk)], axis=1
+        )
         copies[k].wait()
         part = lax.dot_general(
             weight[k], hot, (((1,), (1,)), ((), ())), preferred_element_type=F32
@@ -63,7 +69,7 @@
 def stem(genome_bases, stem_weight, slots):
     bins = genome_bases.shape[0] // BP
     channels, depth = stem_weight.shape
-    chunks = 4
+    chunks = 2
     return pl.pallas_call(
         functools.partial(stem_kernel, bins),
         out_shape=jax.ShapeDtypeStruct((slots, channels // 2, 2 * bins), BF16),

time: 39 us -> 38.9 us (level)
  no operation moved by 1% of the time
where the time goes in v12:
time: 38.9 us; the launch traced here: 38.6 us
  Pallas kernels  18.2 us (47%)
  starting transfers between devices  7.29 us (19%)
  blocking collectives  6.33 us (16%)
  waiting for transfers between devices  5.06 us (13%)
  local copies, waits for them, and re-layouts  0.92 us (2%)
  between operations  0.73 us (2%)
    pallas_call x1, Pallas kernels, per_device(): pl.pallas_call(functools.partial(main_kernel, height, groups), out_shape=...  12.7 us
    all_to_all x1, starting transfers between devices, per_device(): features = lax.all_to_all(own, 'genome', 0, 0, tiled=True)  7.29 us
    all_to_all x1, blocking collectives, per_device(): got = lax.all_to_all(send, 'tower', 0, 0, tiled=True)  6.33 us
    all_to_all x1, waiting for transfers between devices, per_device(): features = lax.all_to_all(own, 'genome', 0, 0, tiled=True)  5.06 us
    pallas_call x1, Pallas kernels, stem(): pl.pallas_call(functools.partial(stem_kernel, bins), out_shape=jax.ShapeD...  3.75 us
    pallas_call x1, Pallas kernels, per_device(): pl.pallas_call(functools.partial(prepare_kernel, height, groups), out_sha...  1.05 us
    unnamed x18, local copies, waits for them, and re-layouts  0.92 us
  transfers between devices with their start and end apart: 1, of which 1 were waited for; matrix products, arithmetic and copies ran while one was open for 0% of the time, Pallas kernels for 3%

profile of v12, /device:TPU:0, one launch (start us, length us, event | category | flops | bytes accessed | tf_op | source)
XLA Modules:
  0.0 38.6 jit_solution(5053796020019693749)
XLA Ops:
  0.6 0.0 copy-start.6
  0.6 0.0 copy-start.5
  0.7 0.0 copy-start.4
  0.7 0.0 copy-start.8
  0.7 0.0 copy-start.3
  0.7 0.0 copy-start.7
  0.7 3.7 %stem.1._ = bf16[8,48,128]{2,1,0:T(8,128)(2,1)} custom-call(s32[1024,128]{1,0:T(8,128)} %bitcast.10, bf16[96,8192]{1,0:T(8,128)(2,1)} %weight_hbm.1), custom_call_target="tpu_custom_call" | custom-call | tf_op jit(solution)/shard_map/stem/pallas_call | solution.py:73
  4.4 7.3 %all-to-all-start = ((bf16[8,48,128]{2,1,0:T(8,128)(2,1)}), bf16[8,48,128]{2,1,0:T(8,128)(2,1)S(1)}, u32[]{:S(2)}, u32[]{:S(2)}) async-start(bf16[8,48,128]{2,1,0:T(8,128)(2,1)} %stem.1._), calls=%async_computation | async-start | bytes 196608 | tf_op jit(solution)/shard_map/all_to_all | solution.py:468
  11.7 0.1 pad_add_fusion.place_ref
  11.8 0.0 copy-done.6
  11.8 0.0 copy-done.5
  11.8 0.0 copy-done.4
  11.8 0.0 copy-done.8
  11.8 0.0 copy-done.3
  11.8 0.0 copy-done.7
  11.9 0.0 copy-start
  11.9 0.9 %copy-done = bf16[8,48,128]{2,1,0:T(8,128)(2,1)S(1)} copy-done((bf16[8,48,128]{2,1,0:T(8,128)(2,1)S(1)}, bf16[8,48,128]{2,1,0:T(8,128)(2,1)}, u32[]{:S(2)}) %copy-start) | copy-done | bytes 98328
  12.7 0.0 copy-start.1
  12.7 0.0 copy-start.2
  12.7 1.1 %prepare.1 = (bf16[6,144,96]{2,1,0:T(8,128)(2,1)S(1)}, f32[48,128]{1,0:T(8,128)S(1)}, f32[20,1152]{1,0:T(8,128)S(1)}, f32[20,1152]{1,0:T(8,128)S(1)}, bf16[80,76...) custom-call(s32[2]{0:T(128)S(1)} %pad_add_fusion.place_ref, ...), custom_call_target="tpu_custom_call" | custom-call | flops 1000000000 | bytes 4194304 | tf_op jit(solution)/shard_map/prepare/pallas_call | solution.py:492
  13.8 5.1 %all-to-all-done.features = bf16[8,48,128]{2,1,0:T(8,128)(2,1)S(1)} async-done(((bf16[8,48,128]{2,1,0:T(8,128)(2,1)}), bf16[8,48,128]{2,1,0:T(8,128)(2,1)S(1)}, u32[]{:S(2)}, u32[]{:S(2)}) %all-to-all-start) | async-done | bytes 98336 | tf_op jit(solution)/shard_map/all_to_all | solution.py:468
  18.9 0.0 copy-done.1
  18.9 0.0 copy-done.2
  18.9 12.7 %windows.1 = (f32[5,16,256]{2,1,0:T(8,128)}, f32[15,128]{1,0:T(8,128)S(1)}, f32[4,2,128]{2,1,0:T(2,128)S(1)}) custom-call(s32[2]{0:T(128)S(1)} %pad_add_fusion.place_ref, bf16[8,48,128]{2,1,0:T(8,128)(2,1)S(1)} %all-to-all-done.features, bf16[6,48,96]{2,1,0:T(8,128)(2,1)S(1)} %bitcast.7, bf16[96,96]{1,0:T(8,128)(2,1)S(1)} %copy-done.2, ...), custom_call_target="tpu_custom_call" | custom-call | tf_op jit(solution)/shard_map/windows/pallas_call | solution.py:510
  31.6 6.3 %all_to_all.10.got_ref = f32[4,2,128]{2,1,0:T(2,128)S(1)} all-to-all(f32[4,2,128]{2,1,0:T(2,128)S(1)} %get-tuple-element.31), channel_id=1, replica_groups=mesh['genome'=8,'tower'=4] {'tower'}, dimensions={0} | all-to-all | bytes 8192 | tf_op jit(solution)/shard_map/all_to_all | solution.py:529
  37.9 0.7 %finish.1 = f32[5,2,16]{2,1,0:T(2,128)} custom-call(f32[15,128]{1,0:T(8,128)S(1)} %get-tuple-element.30.keep_ref, f32[4,2,128]{2,1,0:T(2,128)S(1)} %all_to_all.10.got_ref), custom_call_target="tpu_custom_call" | custom-call | tf_op jit(solution)/shard_map/finish/pallas_call | solution.py:530
Async XLA Ops:
  0.6 11.2 %copy-start.6 = (bf16[5,48]{1,0:T(8,128)(2,1)S(1)}, bf16[5,48]{1,0:T(8,128)(2,1)}, u32[]{:S(2)}) copy-start(bf16[5,48]{1,0:T(8,128)(2,1)} %head_in.1) | copy-start | bytes 1444
  0.6 11.2 %copy-start.5 = (bf16[2,48,48]{2,1,0:T(8,128)(2,1)S(1)}, bf16[2,48,48]{2,1,0:T(8,128)(2,1)}, u32[]{:S(2)}) copy-start(bf16[2,48,48]{2,1,0:T(8,128)(2,1)} %mix_in.1) | copy-start | bytes 27652
  0.7 11.2 %copy-start.4 = (bf16[2,3,48,144]{3,2,1,0:T(8,128)(2,1)S(1)}, bf16[2,3,48,144]{3,2,1,0:T(8,128)(2,1)}, u32[]{:S(2)}) copy-start(bf16[2,3,48,144]{3,2,1,0:T(8,128)(2,1)} %conv_in.1) | copy-start | bytes 248836
  0.7 11.2 %copy-start.8 = (f32[48]{0:T(128)S(1)}, f32[48]{0:T(128)}, u32[]{:S(2)}) copy-start(f32[48]{0:T(128)} %param.16) | copy-start | bytes 580
  0.7 11.2 %copy-start.3 = (bf16[6,48,288]{2,1,0:T(8,128)(2,1)S(1)}, bf16[6,48,288]{2,1,0:T(8,128)(2,1)}, u32[]{:S(2)}) copy-start(bf16[6,48,288]{2,1,0:T(8,128)(2,1)} %trunk_in.1) | copy-start | bytes 497668
  0.7 11.2 %copy-start.7 = (s32[256]{0:T(256)S(1)}, s32[256]{0:T(256)}, u32[]{:S(2)}) copy-start(s32[256]{0:T(256)} %param.11) | copy-start | bytes 3076
  4.4 14.4 %all-to-all-start = ((bf16[8,48,128]{2,1,0:T(8,128)(2,1)}), bf16[8,48,128]{2,1,0:T(8,128)(2,1)S(1)}, u32[]{:S(2)}, u32[]{:S(2)}) async-start(bf16[8,48,128]{2,1,0:T(8,128)(2,1)} %stem.1._), calls=%async_computation | async-start | bytes 196608 | tf_op jit(solution)/shard_map/all_to_all | solution.py:468
  11.9 0.9 %copy-start = (bf16[8,48,128]{2,1,0:T(8,128)(2,1)S(1)}, bf16[8,48,128]{2,1,0:T(8,128)(2,1)}, u32[]{:S(2)}) copy-start(bf16[8,48,128]{2,1,0:T(8,128)(2,1)} %stem.1._) | copy-start | bytes 294916
  12.7 6.1 %copy-start.1 = (bf16[6,96,48]{1,2,0:T(8,128)(2,1)S(1)}, bf16[6,96,48]{1,2,0:T(8,128)(2,1)}, u32[]{:S(2)}) copy-start(bf16[6,96,48]{1,2,0:T(8,128)(2,1)} %param.14) | copy-start | bytes 165892
  12.7 6.1 %copy-start.2 = (bf16[96,96]{1,0:T(8,128)(2,1)S(1)}, bf16[96,96]{1,0:T(8,128)(2,1)}, u32[]{:S(2)}) copy-start(bf16[96,96]{1,0:T(8,128)(2,1)} %pair_weight.1) | copy-start | bytes 55300

commit v13 on v12

--- a/solution.py
+++ b/solution.py
@@ -434,7 +434,7 @@
     targets = out_ref.shape[0]
     per_row = LANES // height
     keep = keep_ref[...][:, :height]
-    got = jnp.sum(got_ref[...], axis=0)
+    got = got_ref[...]
     rows = []
     for q in range(2 * targets):
         at = (q % per_row) * height
@@ -526,7 +526,7 @@
         compiler_params=pltpu.CompilerParams(vmem_limit_bytes=VMEM_BYTES),
         name="windows",
     )(place, features, jnp.transpose(trunk_out, (0, 2, 1)), pair_weight, *prepared)
-    got = lax.all_to_all(send, "tower", 0, 0, tiled=True)
+    got = lax.psum_scatter(send, "tower", scatter_dimension=0)
     scores = pl.pallas_call(
         functools.partial(finish_kernel, height),
         out_shape=jax.ShapeDtypeStruct((targets, 2, height), F32),

time: 38.9 us -> 38.8 us (level)
  local copies, waits for them, and re-layouts: 0.92 us -> 2.03 us
  blocking collectives: 6.33 us -> 5.63 us
  waiting for transfers between devices: 5.06 us -> 4.5 us
    all_to_all x1 -> x0, blocking collectives: 6.33 us -> none  [per_device(): got = lax.all_to_all(send, 'tower', 0, 0, tiled=True)]
    unnamed x0 -> x1, blocking collectives: none -> 5.63 us
    unnamed x18 -> x21, local copies, waits for them, and re-layouts: 0.92 us -> 1.48 us
    all_to_all x1, waiting for transfers between devices: 5.06 us -> 4.5 us  [per_device(): features = lax.all_to_all(own, 'genome', 0, 0, tiled=True)]
    reduce_scatter x0 -> x1, local copies, waits for them, and re-layouts: none -> 0.55 us  [per_device(): got = lax.psum_scatter(send, 'tower', scatter_dimension=0)]
  transfers between devices with their start and end apart: 1 -> 1, of which waited for: 1 -> 1; matrix products, arithmetic and copies ran while one was open for 0% -> 2% of each run, Pallas kernels for 3% -> 3%
where the time goes in v13:
time: 38.8 us; the launch traced here: 38.5 us
  Pallas kernels  18.2 us (47%)
  starting transfers between devices  7.29 us (19%)
  blocking collectives  5.63 us (15%)
  waiting for transfers between devices  4.5 us (12%)
  local copies, waits for them, and re-layouts  2.03 us (5%)
  between operations  0.75 us (2%)
    pallas_call x1, Pallas kernels, per_device(): pl.pallas_call(functools.partial(main_kernel, height, groups), out_shape=...  12.7 us
    all_to_all x1, starting transfers between devices, per_device(): features = lax.all_to_all(own, 'genome', 0, 0, tiled=True)  7.29 us
    unnamed x1, blocking collectives  5.63 us
    all_to_all x1, waiting for transfers between devices, per_device(): features = lax.all_to_all(own, 'genome', 0, 0, tiled=True)  4.5 us
    pallas_call x1, Pallas kernels, stem(): pl.pallas_call(functools.partial(stem_kernel, bins), out_shape=jax.ShapeD...  3.77 us
    unnamed x21, local copies, waits for them, and re-layouts  1.48 us
    pallas_call x1, Pallas kernels, per_device(): pl.pallas_call(functools.partial(prepare_kernel, height, groups), out_sha...  1.05 us
  transfers between devices with their start and end apart: 1, of which 1 were waited for; matrix products, arithmetic and copies ran while one was open for 2% of the time, Pallas kernels for 3%

profile of v13, /device:TPU:0, one launch (start us, length us, event | category | flops | bytes accessed | tf_op | source)
XLA Modules:
  0.0 38.5 jit_solution(2953835325842971634)
XLA Ops:
  0.6 0.0 copy-start.9
  0.6 0.0 copy-start.3
  0.7 0.0 copy-start.8
  0.7 0.0 copy-start.4
  0.7 0.0 copy-start.5
  0.7 0.0 copy-start.6
  0.7 0.0 copy-start.7
  0.7 3.8 %stem.1._ = bf16[8,48,128]{2,1,0:T(8,128)(2,1)} custom-call(s32[1024,128]{1,0:T(8,128)} %bitcast.13, bf16[96,8192]{1,0:T(8,128)(2,1)} %weight_hbm.1), custom_call_target="tpu_custom_call" | custom-call | tf_op jit(solution)/shard_map/stem/pallas_call | solution.py:73
  4.5 7.3 %all-to-all-start = ((bf16[8,48,128]{2,1,0:T(8,128)(2,1)}), bf16[8,48,128]{2,1,0:T(8,128)(2,1)S(1)}, u32[]{:S(2)}, u32[]{:S(2)}) async-start(bf16[8,48,128]{2,1,0:T(8,128)(2,1)} %stem.1._), calls=%async_computation | async-start | bytes 196608 | tf_op jit(solution)/shard_map/all_to_all | solution.py:468
  11.8 0.0 copy-done.9
  11.8 0.6 %dynamic-slice = u32[1]{0:T(128)} dynamic-slice(u32[32]{0:T(128)S(1)} %copy-done.9, u32[]{:T(128)S(6)} %add.3), dynamic_slice_sizes={1} | dynamic-slice | bytes 12
  12.3 0.1 pad_add_fusion.place_ref
  12.4 0.0 copy-done.3
  12.4 0.0 copy-done.8
  12.4 0.0 copy-done.4
  12.4 0.0 copy-done.5
  12.4 0.0 copy-done.6
  12.4 0.0 copy-done.7
  12.4 0.0 copy-start
  12.5 0.9 %copy-done = bf16[8,48,128]{2,1,0:T(8,128)(2,1)S(1)} copy-done((bf16[8,48,128]{2,1,0:T(8,128)(2,1)S(1)}, bf16[8,48,128]{2,1,0:T(8,128)(2,1)}, u32[]{:S(2)}) %copy-start) | copy-done | bytes 98328
  13.3 0.0 copy-start.1
  13.3 0.0 copy-start.2
  13.3 1.1 %prepare.1 = (bf16[6,144,96]{2,1,0:T(8,128)(2,1)S(1)}, f32[48,128]{1,0:T(8,128)S(1)}, f32[20,1152]{1,0:T(8,128)S(1)}, f32[20,1152]{1,0:T(8,128)S(1)}, bf16[80,76...) custom-call(s32[2]{0:T(128)S(1)} %pad_add_fusion.place_ref, ...), custom_call_target="tpu_custom_call" | custom-call | flops 1000000000 | bytes 4194304 | tf_op jit(solution)/shard_map/prepare/pallas_call | solution.py:492
  14.4 4.5 %all-to-all-done.features = bf16[8,48,128]{2,1,0:T(8,128)(2,1)S(1)} async-done(((bf16[8,48,128]{2,1,0:T(8,128)(2,1)}), bf16[8,48,128]{2,1,0:T(8,128)(2,1)S(1)}, u32[]{:S(2)}, u32[]{:S(2)}) %all-to-all-start) | async-done | bytes 98336 | tf_op jit(solution)/shard_map/all_to_all | solution.py:468
  18.9 0.0 copy-done.1
  18.9 0.0 copy-done.2
  18.9 12.7 %windows.1 = (f32[5,16,256]{2,1,0:T(8,128)}, f32[15,128]{1,0:T(8,128)S(1)}, f32[4,2,128]{2,1,0:T(2,128)S(1)}) custom-call(s32[2]{0:T(128)S(1)} %pad_add_fusion.place_ref, bf16[8,48,128]{2,1,0:T(8,128)(2,1)S(1)} %all-to-all-done.features, bf16[6,48,96]{2,1,0:T(8,128)(2,1)S(1)} %bitcast.10, bf16[96,96]{1,0:T(8,128)(2,1)S(1)} %copy-done.2, ...), custom_call_target="tpu_custom_call" | custom-call | tf_op jit(solution)/shard_map/windows/pallas_call | solution.py:510
  31.6 5.6 %all-reduce = f32[4,2,128]{2,1,0:T(2,128)S(1)} all-reduce(f32[4,2,128]{2,1,0:T(2,128)S(1)} %get-tuple-element.31), channel_id=2, replica_groups=mesh['genome'=8,'tower'=4] {'tower'}, use_global_device_ids=true, to_apply=%region_0.0.clone | all-reduce | flops 1024 | bytes 8192
  37.3 0.5 %dynamic-slice_bitcast_fusion.got_ref = f32[2,128]{1,0:T(2,128)S(1)} fusion(f32[4,2,128]{2,1,0:T(2,128)S(1)} %all-reduce, u32[]{:T(128)} %bitcast.6), kind=kLoop, calls=%fused_computation | loop fusion | bytes 2052 | tf_op jit(solution)/shard_map/reduce_scatter | solution.py:529
  37.8 0.7 %finish.1 = f32[5,2,16]{2,1,0:T(2,128)} custom-call(f32[15,128]{1,0:T(8,128)S(1)} %get-tuple-element.30.keep_ref, f32[2,128]{1,0:T(2,128)S(1)} %dynamic-slice_bitcast_fusion.got_ref), custom_call_target="tpu_custom_call" | custom-call | tf_op jit(solution)/shard_map/finish/pallas_call | solution.py:530
Async XLA Ops:
  0.6 11.1 %copy-start.9 = (u32[32]{0:T(128)S(1)}, u32[32]{0:T(128)}, u32[]{:S(2)}) copy-start(u32[32]{0:T(128)} %constant.11) | copy-start | bytes 388
  0.6 11.8 %copy-start.3 = (bf16[6,48,288]{2,1,0:T(8,128)(2,1)S(1)}, bf16[6,48,288]{2,1,0:T(8,128)(2,1)}, u32[]{:S(2)}) copy-start(bf16[6,48,288]{2,1,0:T(8,128)(2,1)} %trunk_in.1) | copy-start | bytes 497668
  0.7 11.8 %copy-start.8 = (f32[48]{0:T(128)S(1)}, f32[48]{0:T(128)}, u32[]{:S(2)}) copy-start(f32[48]{0:T(128)} %param.16) | copy-start | bytes 580
  0.7 11.8 %copy-start.4 = (bf16[2,3,48,144]{3,2,1,0:T(8,128)(2,1)S(1)}, bf16[2,3,48,144]{3,2,1,0:T(8,128)(2,1)}, u32[]{:S(2)}) copy-start(bf16[2,3,48,144]{3,2,1,0:T(8,128)(2,1)} %conv_in.1) | copy-start | bytes 248836
  0.7 11.7 %copy-start.5 = (bf16[2,48,48]{2,1,0:T(8,128)(2,1)S(1)}, bf16[2,48,48]{2,1,0:T(8,128)(2,1)}, u32[]{:S(2)}) copy-start(bf16[2,48,48]{2,1,0:T(8,128)(2,1)} %mix_in.1) | copy-start | bytes 27652
  0.7 11.7 %copy-start.6 = (bf16[5,48]{1,0:T(8,128)(2,1)S(1)}, bf16[5,48]{1,0:T(8,128)(2,1)}, u32[]{:S(2)}) copy-start(bf16[5,48]{1,0:T(8,128)(2,1)} %head_in.1) | copy-start | bytes 1444
  0.7 11.7 %copy-start.7 = (s32[256]{0:T(256)S(1)}, s32[256]{0:T(256)}, u32[]{:S(2)}) copy-start(s32[256]{0:T(256)} %param.11) | copy-start | bytes 3076
  4.5 14.4 %all-to-all-start = ((bf16[8,48,128]{2,1,0:T(8,128)(2,1)}), bf16[8,48,128]{2,1,0:T(8,128)(2,1)S(1)}, u32[]{:S(2)}, u32[]{:S(2)}) async-start(bf16[8,48,128]{2,1,0:T(8,128)(2,1)} %stem.1._), calls=%async_computation | async-start | bytes 196608 | tf_op jit(solution)/shard_map/all_to_all | solution.py:468
  12.4 0.9 %copy-start = (bf16[8,48,128]{2,1,0:T(8,128)(2,1)S(1)}, bf16[8,48,128]{2,1,0:T(8,128)(2,1)}, u32[]{:S(2)}) copy-start(bf16[8,48,128]{2,1,0:T(8,128)(2,1)} %stem.1._) | copy-start | bytes 294916
  13.3 5.6 %copy-start.1 = (bf16[6,96,48]{1,2,0:T(8,128)(2,1)S(1)}, bf16[6,96,48]{1,2,0:T(8,128)(2,1)}, u32[]{:S(2)}) copy-start(bf16[6,96,48]{1,2,0:T(8,128)(2,1)} %param.14) | copy-start | bytes 165892
  13.3 5.6 %copy-start.2 = (bf16[96,96]{1,0:T(8,128)(2,1)S(1)}, bf16[96,96]{1,0:T(8,128)(2,1)}, u32[]{:S(2)}) copy-start(bf16[96,96]{1,0:T(8,128)(2,1)} %pair_weight.1) | copy-start | bytes 55300

commit v14 on v13

--- a/solution.py
+++ b/solution.py
@@ -430,11 +430,11 @@
         send_ref[lax.rem(place_ref[0] + k, STRIDE // height)] = jnp.concatenate(packed, axis=0)
 
 
-def finish_kernel(height, keep_ref, got_ref, out_ref):
+def finish_kernel(height, place_ref, keep_ref, got_ref, out_ref):
     targets = out_ref.shape[0]
     per_row = LANES // height
     keep = keep_ref[...][:, :height]
-    got = got_ref[...]
+    got = got_ref[place_ref[0]]
     rows = []
     for q in range(2 * targets):
         at = (q % per_row) * height
@@ -526,15 +526,15 @@
         compiler_params=pltpu.CompilerParams(vmem_limit_bytes=VMEM_BYTES),
         name="windows",
     )(place, features, jnp.transpose(trunk_out, (0, 2, 1)), pair_weight, *prepared)
-    got = lax.psum_scatter(send, "tower", scatter_dimension=0)
+    got = lax.psum(send, "tower")
     scores = pl.pallas_call(
         functools.partial(finish_kernel, height),
         out_shape=jax.ShapeDtypeStruct((targets, 2, height), F32),
-        in_specs=[vmem, vmem],
+        in_specs=[smem, vmem, vmem],
         out_specs=vmem,
         compiler_params=pltpu.CompilerParams(vmem_limit_bytes=2 * 1024 * 1024),
         name="finish",
-    )(keep, got)
+    )(place, keep, got)
     return (stitched, jnp.transpose(scores, (1, 0, 2)))
 
 

time: 38.8 us -> 38.7 us (level)
  local copies, waits for them, and re-layouts: 2.03 us -> 0.92 us
  Pallas kernels: 18.2 us -> 18.8 us
  waiting for transfers between devices: 4.5 us -> 5.06 us
    unnamed x1 -> x0, blocking collectives: 5.63 us -> none
    psum x0 -> x1, blocking collectives: none -> 5.63 us  [per_device(): got = lax.psum(send, 'tower')]
    unnamed x21 -> x18, local copies, waits for them, and re-layouts: 1.48 us -> 0.92 us
    all_to_all x1, waiting for transfers between devices: 4.5 us -> 5.06 us  [per_device(): features = lax.all_to_all(own, 'genome', 0, 0, tiled=True)]
    reduce_scatter x1 -> x0, local copies, waits for them, and re-layouts: 0.55 us -> none  [per_device(): got = lax.psum_scatter(send, 'tower', scatter_dimension=0)]
    pallas_call x1, Pallas kernels: 0.68 us -> 1.23 us  [per_device(): pl.pallas_call(functools.partial(finish_kernel, height), out_shape=jax.Sh...]
  transfers between devices with their start and end apart: 1 -> 1, of which waited for: 1 -> 1; matrix products, arithmetic and copies ran while one was open for 2% -> 0% of each run, Pallas kernels for 3% -> 3%
where the time goes in v14:
time: 38.7 us; the launch traced here: 38.5 us
  Pallas kernels  18.8 us (49%)
  starting transfers between devices  7.29 us (19%)
  blocking collectives  5.63 us (15%)
  waiting for transfers between devices  5.06 us (13%)
  local copies, waits for them, and re-layouts  0.92 us (2%)
  between operations  0.73 us (2%)
    pallas_call x1, Pallas kernels, per_device(): pl.pallas_call(functools.partial(main_kernel, height, groups), out_shape=...  12.7 us
    all_to_all x1, starting transfers between devices, per_device(): features = lax.all_to_all(own, 'genome', 0, 0, tiled=True)  7.29 us
    psum x1, blocking collectives, per_device(): got = lax.psum(send, 'tower')  5.63 us
    all_to_all x1, waiting for transfers between devices, per_device(): features = lax.all_to_all(own, 'genome', 0, 0, tiled=True)  5.06 us
    pallas_call x1, Pallas kernels, stem(): pl.pallas_call(functools.partial(stem_kernel, bins), out_shape=jax.ShapeD...  3.76 us
    pallas_call x1, Pallas kernels, per_device(): pl.pallas_call(functools.partial(finish_kernel, height), out_shape=jax.Sh...  1.23 us
    pallas_call x1, Pallas kernels, per_device(): pl.pallas_call(functools.partial(prepare_kernel, height, groups), out_sha...  1.05 us
    unnamed x18, local copies, waits for them, and re-layouts  0.92 us
  transfers between devices with their start and end apart: 1, of which 1 were waited for; matrix products, arithmetic and copies ran while one was open for 0% of the time, Pallas kernels for 3%

profile of v14, /device:TPU:0, one launch (start us, length us, event | category | flops | bytes accessed | tf_op | source)
XLA Modules:
  0.0 38.5 jit_solution(16966636777306349128)
XLA Ops:
  0.6 0.0 copy-start.6
  0.6 0.0 copy-start.5
  0.7 0.0 copy-start.4
  0.7 0.0 copy-start.8
  0.7 0.0 copy-start.3
  0.7 0.0 copy-start.7
  0.7 3.8 %stem.1._ = bf16[8,48,128]{2,1,0:T(8,128)(2,1)} custom-call(s32[1024,128]{1,0:T(8,128)} %bitcast.10, bf16[96,8192]{1,0:T(8,128)(2,1)} %weight_hbm.1), custom_call_target="tpu_custom_call" | custom-call | tf_op jit(solution)/shard_map/stem/pallas_call | solution.py:73
  4.5 7.3 %all-to-all-start = ((bf16[8,48,128]{2,1,0:T(8,128)(2,1)}), bf16[8,48,128]{2,1,0:T(8,128)(2,1)S(1)}, u32[]{:S(2)}, u32[]{:S(2)}) async-start(bf16[8,48,128]{2,1,0:T(8,128)(2,1)} %stem.1._), calls=%async_computation | async-start | bytes 196608 | tf_op jit(solution)/shard_map/all_to_all | solution.py:468
  11.7 0.1 pad_add_fusion.place_ref
  11.8 0.0 copy-done.6
  11.8 0.0 copy-done.5
  11.8 0.0 copy-done.4
  11.8 0.0 copy-done.8
  11.8 0.0 copy-done.3
  11.8 0.0 copy-done.7
  11.9 0.0 copy-start
  11.9 0.9 %copy-done = bf16[8,48,128]{2,1,0:T(8,128)(2,1)S(1)} copy-done((bf16[8,48,128]{2,1,0:T(8,128)(2,1)S(1)}, bf16[8,48,128]{2,1,0:T(8,128)(2,1)}, u32[]{:S(2)}) %copy-start) | copy-done | bytes 98328
  12.8 0.0 copy-start.1
  12.8 0.0 copy-start.2
  12.8 1.1 %prepare.1 = (bf16[6,144,96]{2,1,0:T(8,128)(2,1)S(1)}, f32[48,128]{1,0:T(8,128)S(1)}, f32[20,1152]{1,0:T(8,128)S(1)}, f32[20,1152]{1,0:T(8,128)S(1)}, bf16[80,76...) custom-call(s32[2]{0:T(128)S(1)} %pad_add_fusion.place_ref, ...), custom_call_target="tpu_custom_call" | custom-call | flops 1000000000 | bytes 4194304 | tf_op jit(solution)/shard_map/prepare/pallas_call | solution.py:492
  13.8 5.1 %all-to-all-done.features = bf16[8,48,128]{2,1,0:T(8,128)(2,1)S(1)} async-done(((bf16[8,48,128]{2,1,0:T(8,128)(2,1)}), bf16[8,48,128]{2,1,0:T(8,128)(2,1)S(1)}, u32[]{:S(2)}, u32[]{:S(2)}) %all-to-all-start) | async-done | bytes 98336 | tf_op jit(solution)/shard_map/all_to_all | solution.py:468
  18.9 0.0 copy-done.1
  18.9 0.0 copy-done.2
  18.9 12.7 %windows.1 = (f32[5,16,256]{2,1,0:T(8,128)}, f32[15,128]{1,0:T(8,128)S(1)}, f32[4,2,128]{2,1,0:T(2,128)S(1)}) custom-call(s32[2]{0:T(128)S(1)} %pad_add_fusion.place_ref, bf16[8,48,128]{2,1,0:T(8,128)(2,1)S(1)} %all-to-all-done.features, bf16[6,48,96]{2,1,0:T(8,128)(2,1)S(1)} %bitcast.7, bf16[96,96]{1,0:T(8,128)(2,1)S(1)} %copy-done.2, ...), custom_call_target="tpu_custom_call" | custom-call | tf_op jit(solution)/shard_map/windows/pallas_call | solution.py:510
  31.6 5.6 %psum.7.got_ref = f32[4,2,128]{2,1,0:T(2,128)S(1)} all-reduce(f32[4,2,128]{2,1,0:T(2,128)S(1)} %get-tuple-element.31), channel_id=1, replica_groups=mesh['genome'=8,'tower'=4] {'tower'}, use_global_device_ids=true, to_apply=%region_0.0 | all-reduce | flops 1024 | bytes 8192 | tf_op jit(solution)/shard_map/psum | solution.py:529
  37.2 1.2 %finish.1 = f32[5,2,16]{2,1,0:T(2,128)} custom-call(s32[2]{0:T(128)S(1)} %pad_add_fusion.place_ref, f32[15,128]{1,0:T(8,128)S(1)} %get-tuple-element.30.keep_ref, f32[4,2,128]{2,1,0:T(2,128)S(1)} %psum.7.got_ref), custom_call_target="tpu_custom_call" | custom-call | tf_op jit(solution)/shard_map/finish/pallas_call | solution.py:530
Async XLA Ops:
  0.6 11.2 %copy-start.6 = (bf16[5,48]{1,0:T(8,128)(2,1)S(1)}, bf16[5,48]{1,0:T(8,128)(2,1)}, u32[]{:S(2)}) copy-start(bf16[5,48]{1,0:T(8,128)(2,1)} %head_in.1) | copy-start | bytes 1444
  0.6 11.2 %copy-start.5 = (bf16[2,48,48]{2,1,0:T(8,128)(2,1)S(1)}, bf16[2,48,48]{2,1,0:T(8,128)(2,1)}, u32[]{:S(2)}) copy-start(bf16[2,48,48]{2,1,0:T(8,128)(2,1)} %mix_in.1) | copy-start | bytes 27652
  0.7 11.2 %copy-start.4 = (bf16[2,3,48,144]{3,2,1,0:T(8,128)(2,1)S(1)}, bf16[2,3,48,144]{3,2,1,0:T(8,128)(2,1)}, u32[]{:S(2)}) copy-start(bf16[2,3,48,144]{3,2,1,0:T(8,128)(2,1)} %conv_in.1) | copy-start | bytes 248836
  0.7 11.2 %copy-start.8 = (f32[48]{0:T(128)S(1)}, f32[48]{0:T(128)}, u32[]{:S(2)}) copy-start(f32[48]{0:T(128)} %param.16) | copy-start | bytes 580
  0.7 11.2 %copy-start.3 = (bf16[6,48,288]{2,1,0:T(8,128)(2,1)S(1)}, bf16[6,48,288]{2,1,0:T(8,128)(2,1)}, u32[]{:S(2)}) copy-start(bf16[6,48,288]{2,1,0:T(8,128)(2,1)} %trunk_in.1) | copy-start | bytes 497668
  0.7 11.2 %copy-start.7 = (s32[256]{0:T(256)S(1)}, s32[256]{0:T(256)}, u32[]{:S(2)}) copy-start(s32[256]{0:T(256)} %param.11) | copy-start | bytes 3076
  4.5 14.4 %all-to-all-start = ((bf16[8,48,128]{2,1,0:T(8,128)(2,1)}), bf16[8,48,128]{2,1,0:T(8,128)(2,1)S(1)}, u32[]{:S(2)}, u32[]{:S(2)}) async-start(bf16[8,48,128]{2,1,0:T(8,128)(2,1)} %stem.1._), calls=%async_computation | async-start | bytes 196608 | tf_op jit(solution)/shard_map/all_to_all | solution.py:468
  11.9 0.9 %copy-start = (bf16[8,48,128]{2,1,0:T(8,128)(2,1)S(1)}, bf16[8,48,128]{2,1,0:T(8,128)(2,1)}, u32[]{:S(2)}) copy-start(bf16[8,48,128]{2,1,0:T(8,128)(2,1)} %stem.1._) | copy-start | bytes 294916
  12.8 6.1 %copy-start.1 = (bf16[6,96,48]{1,2,0:T(8,128)(2,1)S(1)}, bf16[6,96,48]{1,2,0:T(8,128)(2,1)}, u32[]{:S(2)}) copy-start(bf16[6,96,48]{1,2,0:T(8,128)(2,1)} %param.14) | copy-start | bytes 165892
  12.8 6.1 %copy-start.2 = (bf16[96,96]{1,0:T(8,128)(2,1)S(1)}, bf16[96,96]{1,0:T(8,128)(2,1)}, u32[]{:S(2)}) copy-start(bf16[96,96]{1,0:T(8,128)(2,1)} %pair_weight.1) | copy-start | bytes 55300
